TPU v7x, 256 devices: a whole 4x4x8 slice. The times are simulated.
256 devices in a mesh: mp: 16 (over y, z_hi), tp: 16 (over z_lo, x, core).
Axes of the slice: x: 4, y: 4, z: 8 (z_hi: 4, z_lo: 2; z = z_hi * 2 + z_lo), core: 2. Of those that a mesh axis runs over, the one named last changes fastest.
Arguments:
- activations: bfloat16 [16, 4, 256, 8192], P('mp', None, None, 'tp'), may hold values from -100 to 100
- cotangents: bfloat16 [16, 4, 256, 4096], P('mp', None, None, 'tp'), may hold values from -0.3984375 to 0.3984375
- checkpoints: bfloat16 [16, 8192, 4096], P('mp', 'tp'), may hold values from -6 to 6
Outputs:
- merged: bfloat16 [8192, 4096], P('tp')
All inputs are finite; a program needn't handle non-finite values.
Results may differ from a plain program's by a relative error of at most 0.022.
Values may be sent and summed in bfloat16 or wider, within the bound.
No kernel may reach another device: no remote copies, remote signals or barrier semaphores. Data moves between devices by JAX's collectives and lax.ppermute only.
A program may use at most 128 MiB of HBM per device.

v0:
```python
import jax
import jax.numpy as jnp
from jax import lax
from jax.sharding import PartitionSpec as P


def batch_grad(inputs, grads_out):
    return lax.dot_general(
        inputs, grads_out, (((0,), (0,)), ((), ())), preferred_element_type=jnp.float32
    )


def on_device(activations, cotangents, checkpoints):
    batches = activations.shape[1]
    columns = cotangents.shape[3] * lax.axis_size("tp")
    fisher = jnp.zeros((activations.shape[3], columns), jnp.float32)
    for number in range(batches):
        gathered = lax.all_gather(cotangents[0, number], "tp", axis=1, tiled=True)
        grad = batch_grad(activations[0, number], gathered)
        fisher = fisher + grad * grad
    weighted = fisher * checkpoints[0].astype(jnp.float32)
    numer, denom = (
        lax.psum_scatter(
            weighted.astype(jnp.bfloat16), "mp", scatter_dimension=0, tiled=True
        ).astype(jnp.float32),
        lax.psum_scatter(fisher.astype(jnp.bfloat16), "mp", scatter_dimension=0, tiled=True).astype(
            jnp.float32
        ),
    )
    owned = (numer / denom).astype(jnp.bfloat16)
    merged = lax.all_gather(owned, "mp", axis=0, tiled=True)
    return merged


def solution(mesh):
    in_specs = (P("mp", None, None, "tp"), P("mp", None, None, "tp"), P("mp", "tp", None))
    out_specs = P("tp", None)
    return jax.shard_map(
        on_device, mesh=mesh, in_specs=in_specs, out_specs=out_specs, check_vma=False
    )
```

profile of v0, /device:TPU:22, one launch (start us, length us, event | category | flops | bytes accessed | tf_op | source)
XLA Modules:
  0.0 471.2 jit_solution(3031983599143198572)
XLA Ops:
  6.5 0.0 all-gather.16.cloned.1.call-start
  6.5 1.9 fusion.16
  8.4 0.0 all-gather.16.cloned.1.call-update
  8.5 0.0 all-gather.12.cloned.1.call-start
  8.5 0.7 all-gather.12.cloned.1.call-update
  9.2 0.0 all-gather.14.cloned.1.call-start
  9.3 0.7 all-gather.14.cloned.1.call-update
  9.9 0.0 all-gather.18.cloned.1.call-start
  10.0 0.5 all-gather.18.cloned.1.call-update
  10.5 0.0 copy-start
  10.5 0.0 reduce-scatter.3.cloned.1.call-start
  10.6 40.6 %all-gather.16.cloned.1.call-done = bf16[1,1,256,4096]{3,2,1,0:T(8,128)(2,1)} async-done(((bf16[1,1,256,256]{3,2,1,0:T(8,128)(2,1)}), bf16[1,1,256,4096]{3,2,1,0:T(8,128)(2,1)}) %all-gather.16.cloned.1.call-update) | async-done | bytes 2097168 | tf_op jit(solution)/shard_map/all_gather | solution.py:18
  51.2 6.2 %fusion.2 = f32[512,4096]{1,0:T(8,128)} fusion(bf16[1,1,256,4096]{3,2,1,0:T(8,128)(2,1)} %all-gather.16.cloned.1.call-done, bf16[1,4,256,512]{3,2,1,0:T(8,128)(2,1)} %param.3), kind=kOutput, calls=%fused_computation.4 | convolution fusion | flops 1073741824 | bytes 10747904 | tf_op jit(solution)/shard_map/dot_general | solution.py:8
  57.4 35.4 %all-gather.12.cloned.1.call-done = bf16[1,1,256,4096]{3,2,1,0:T(8,128)(2,1)} async-done(((bf16[1,1,256,256]{3,2,1,0:T(8,128)(2,1)}), bf16[1,1,256,4096]{3,2,1,0:T(8,128)(2,1)}) %all-gather.12.cloned.1.call-update) | async-done | bytes 2097168 | tf_op jit(solution)/shard_map/all_gather | solution.py:18
  92.8 0.0 copy-done
  92.8 6.1 %fusion.6 = f32[512,4096]{1,0:T(8,128)} fusion(bf16[1,1,256,4096]{3,2,1,0:T(8,128)(2,1)} %all-gather.12.cloned.1.call-done, bf16[1,4,256,512]{3,2,1,0:T(8,128)(2,1)S(1)} %copy-done), kind=kOutput, calls=%fused_computation.8 | convolution fusion | flops 1073741824 | bytes 10747904 | tf_op jit(solution)/shard_map/dot_general | solution.py:8
  98.9 35.5 %all-gather.14.cloned.1.call-done = bf16[1,1,256,4096]{3,2,1,0:T(8,128)(2,1)} async-done(((bf16[1,1,256,256]{3,2,1,0:T(8,128)(2,1)}), bf16[1,1,256,4096]{3,2,1,0:T(8,128)(2,1)}) %all-gather.14.cloned.1.call-update) | async-done | bytes 2097168 | tf_op jit(solution)/shard_map/all_gather | solution.py:18
  134.4 6.1 %fusion.4 = f32[512,4096]{1,0:T(8,128)} fusion(bf16[1,1,256,4096]{3,2,1,0:T(8,128)(2,1)} %all-gather.14.cloned.1.call-done, bf16[1,4,256,512]{3,2,1,0:T(8,128)(2,1)S(1)} %copy-done), kind=kOutput, calls=%fused_computation.6 | convolution fusion | flops 1073741824 | bytes 10747904 | tf_op jit(solution)/shard_map/dot_general | solution.py:8
  140.5 35.3 %all-gather.18.cloned.1.call-done = bf16[1,1,256,4096]{3,2,1,0:T(8,128)(2,1)} async-done(((bf16[1,1,256,256]{3,2,1,0:T(8,128)(2,1)}), bf16[1,1,256,4096]{3,2,1,0:T(8,128)(2,1)}) %all-gather.18.cloned.1.call-update) | async-done | bytes 2097168 | tf_op jit(solution)/shard_map/all_gather | solution.py:18
  175.8 14.4 %fusion = (bf16[512,4096]{1,0:T(8,128)(2,1)}, bf16[512,4096]{1,0:T(8,128)(2,1)}) fusion(bf16[1,512,4096]{2,1,0:T(8,128)(2,1)} %param.5, bf16[1,1,256,4096]{3,2,1,0:T(8,128)(2,1)} %all-gather.18.cloned.1.call-done, bf16[1,4,256,512]{3,2,1,0:T(8,128)(2,1)S(1)} %copy-done, f32[512,4096]{1,0:T(8,128)} %fusion.2, f32[512,4096]{1,0:T(8,128)} %fusion.4, ...), kind=kOutput, calls=%fused_computation.1 | convolution fusion | flops 1096810496 | bytes 40108032 | tf_op jit(solution)/shard_map/dot_general | solution.py:8
  190.2 0.0 reduce-scatter.3.cloned.1.call-update
  190.2 0.0 reduce-scatter.5.cloned.1.call-start
  190.2 0.5 reduce-scatter.5.cloned.1.call-update
  190.8 0.0 all-gather.10.cloned.1.call-start
  190.8 94.7 %reduce-scatter.3.cloned.1.call-done = bf16[32,4096]{1,0:T(8,128)(2,1)} async-done(((bf16[512,4096]{1,0:T(8,128)(2,1)}), bf16[32,4096]{1,0:T(8,128)(2,1)}) %reduce-scatter.3.cloned.1.call-update) | async-done | bytes 262160 | tf_op jit(solution)/shard_map/reduce_scatter | solution.py:23
  285.5 97.4 %reduce-scatter.5.cloned.1.call-done = bf16[32,4096]{1,0:T(8,128)(2,1)} async-done(((bf16[512,4096]{1,0:T(8,128)(2,1)}), bf16[32,4096]{1,0:T(8,128)(2,1)}) %reduce-scatter.5.cloned.1.call-update) | async-done | bytes 262160 | tf_op jit(solution)/shard_map/reduce_scatter | solution.py:26
  382.9 1.8 divide_convert_fusion
  384.7 0.0 all-gather.10.cloned.1.call-update
  384.7 74.9 %all-gather.10.cloned.1.call-done = bf16[512,4096]{1,0:T(8,128)(2,1)} async-done(((bf16[32,4096]{1,0:T(8,128)(2,1)}), bf16[512,4096]{1,0:T(8,128)(2,1)}) %all-gather.10.cloned.1.call-update) | async-done | bytes 4194320 | tf_op jit(solution)/shard_map/all_gather | solution.py:31
  459.7 4.7 copy.5
Async XLA Ops:
  6.5 44.7 %all-gather.16.cloned.1.call-start = ((), (), s32[]{:S(2)}) async-start(), calls=%async_computation.7 | async-start | bytes 2228224 | tf_op jit(solution)/shard_map/all_gather | solution.py:18
  8.5 84.3 %all-gather.12.cloned.1.call-start = ((), (), s32[]{:S(2)}) async-start(), calls=%async_computation.5 | async-start | bytes 2228224 | tf_op jit(solution)/shard_map/all_gather | solution.py:18
  9.2 125.2 %all-gather.14.cloned.1.call-start = ((), (), s32[]{:S(2)}) async-start(), calls=%async_computation.6 | async-start | bytes 2228224 | tf_op jit(solution)/shard_map/all_gather | solution.py:18
  9.9 165.8 %all-gather.18.cloned.1.call-start = ((), (), s32[]{:S(2)}) async-start(), calls=%async_computation.8 | async-start | bytes 2228224 | tf_op jit(solution)/shard_map/all_gather | solution.py:18
  10.5 82.3 %copy-start = (bf16[1,4,256,512]{3,2,1,0:T(8,128)(2,1)S(1)}, bf16[1,4,256,512]{3,2,1,0:T(8,128)(2,1)}, u32[]{:S(2)}) copy-start(bf16[1,4,256,512]{3,2,1,0:T(8,128)(2,1)} %param.3) | copy-start | bytes 3145732
  10.5 274.9 %reduce-scatter.3.cloned.1.call-start = ((), (), s32[]{:S(2)}) async-start(), calls=%async_computation.2 | async-start | bytes 4456448 | tf_op jit(solution)/shard_map/reduce_scatter | solution.py:23
  190.2 192.7 %reduce-scatter.5.cloned.1.call-start = ((), (), s32[]{:S(2)}) async-start(), calls=%async_computation.3 | async-start | bytes 4456448 | tf_op jit(solution)/shard_map/reduce_scatter | solution.py:26
  190.8 268.9 %all-gather.10.cloned.1.call-start = ((), (), s32[]{:S(2)}) async-start(), calls=%async_computation.4 | async-start | bytes 4456448 | tf_op jit(solution)/shard_map/all_gather | solution.py:31
Sparse Core Ops, SparseCore 0:
  9.1 42.0 all-gather.15
  53.0 39.7 all-gather.11
  94.6 39.7 all-gather.13
  136.0 39.7 all-gather.17
  190.3 95.1 reduce-scatter.2
  289.4 93.4 reduce-scatter.4
  385.3 74.3 all-gather.9
where the time goes:
time: 473 us; the launch traced here: 471 us
  waiting for transfers between devices  416 us (88%)
  matrix products  32.8 us (7%)
  between operations  13.5 us (3%)
  local copies, waits for them, and re-layouts  6.59 us (1%)
    all_gather x4, waiting for transfers between devices, on_device(): gathered = lax.all_gather(cotangents[0, number], 'tp', axis=1, tiled=True)  147 us
    reduce_scatter x1, waiting for transfers between devices, on_device(): lax.psum_scatter(fisher.astype(jnp.bfloat16), 'mp', scatter_dimension=0,...  97.4 us
    reduce_scatter x1, waiting for transfers between devices, on_device(): lax.psum_scatter(weighted.astype(jnp.bfloat16), 'mp', scatter_dimension=0...  94.7 us
    all_gather x1, waiting for transfers between devices, on_device(): merged = lax.all_gather(owned, 'mp', axis=0, tiled=True)  74.9 us
    dot_general x4, matrix products, batch_grad(): lax.dot_general(inputs, grads_out, (((0,), (0,)), ((), ())), preferred_el...  32.8 us
  transfers between devices with their start and end apart: 7, of which 7 were waited for; matrix products, arithmetic and copies ran while one was open for 4% of the time, Pallas kernels for 0%

commit v1 on v0

v1 whole, which is shorter than its diff:
```python
import functools

import jax
import jax.numpy as jnp
from jax import lax
from jax.experimental import pallas as pl
from jax.experimental.pallas import tpu as pltpu
from jax.sharding import Mesh
from jax.sharding import PartitionSpec as P

BF = jnp.bfloat16
F32 = jnp.float32
TILE = 256
ROWS = 512
S = 32
MIB = 1024 * 1024
ORDER = (
    "hV SA SC A0",
    "hB C0 hD A1",
    "B0 D0 A2 C1",
    "A3 B1 A4 C2",
    "D1 C3 A5 A6",
    "B2 D2 B3 D3",
    "C4 B4 D4 C5",
    "B5 D5 D6 C6",
    "A7 D7 B6 A8",
    "C7 B7 D8 C8",
    "B8",
)
ORDER = [step for line in ORDER for step in line.split()]
GROUPS = ()
MERGE = 9
ANY = pl.BlockSpec(memory_space=pl.ANY)


def partner(i, core, which):
    swap = core if which == 0 else 1 - core
    return (i ^ 1) * (1 - swap) + (3 - i) * swap


def exchange(value, axis, which):
    pairs = [
        (i * 2 + core, partner(i, core, which) * 2 + core) for i in range(4) for core in range(2)
    ]
    return lax.ppermute(value, (axis, "c"), pairs)


def swap(value, axis):
    return lax.ppermute(value, axis, [(0, 1), (1, 0)])


def bits(i, core):
    flips = (i // 2 + i) % 2, i // 2
    return (
        flips[0] * (1 - core) + flips[1] * core,
        flips[1] * (1 - core) + flips[0] * core,
    )


def params(limit=8):
    return dict(
        compiler_params=pltpu.CompilerParams(vmem_limit_bytes=limit * MIB),
        cost_estimate=pl.CostEstimate(flops=1, bytes_accessed=1, transcendentals=0),
    )


def hold_kernel(value, after, out):
    pass


def hold(value, after):
    return pl.pallas_call(
        hold_kernel,
        out_shape=jax.ShapeDtypeStruct(value.shape, value.dtype),
        in_specs=[ANY, ANY],
        out_specs=ANY,
        input_output_aliases={0: 0},
        name="hold",
        **params(),
    )(value, after)


def stack_kernel(a, b, after, out):
    out[0] = a[...]
    out[1] = b[...]


def stack(a, b, after):
    whole = pl.BlockSpec(memory_space=pltpu.VMEM)
    return pl.pallas_call(
        stack_kernel,
        out_shape=jax.ShapeDtypeStruct((2, *a.shape), BF),
        in_specs=[whole, whole, ANY],
        out_specs=whole,
        name="stack",
        **params(),
    )(a, b, after)


def fisher_kernel(where, acts, mine, peer, weights, after, send, keep, total, tiles, sems):
    mark = where[0]
    chips = mine.shape[0]

    def fetch(tile):
        column = pl.multiple_of(where[1 + tile] * TILE, TILE)
        return pltpu.make_async_copy(
            weights.at[:, pl.ds(column, TILE)], tiles.at[tile], sems.at[tile]
        )

    for tile in range(2 * chips):
        fetch(tile).start()
    for tile in range(2 * chips):
        cots = (mine, peer)[tile % 2]
        for number in range(4):
            grad = jnp.dot(acts[number], cots[tile // 2, number], preferred_element_type=F32)
            if number == 0:
                total[...] = grad * grad
            else:
                total[...] += grad * grad
        fetch(tile).wait()
        cols = slice(tile * TILE, (tile + 1) * TILE)
        for k in range(16):
            part = pl.ds(pl.multiple_of((mark ^ (15 - k)) * S, S), S)
            value = total[part, :]
            ref, at = (send, k) if k < 8 else (keep, k - 8)
            out = slice(at * S, (at + 1) * S)
            ref[0, out, cols] = (value * tiles[tile, part, :].astype(F32)).astype(BF)
            ref[1, out, cols] = value.astype(BF)


def fisher_parts(acts, mine, peer, weights, where, after):
    chips = mine.shape[0]
    columns = 2 * TILE * chips
    whole = pl.BlockSpec(memory_space=pltpu.VMEM)
    return pl.pallas_call(
        fisher_kernel,
        out_shape=[jax.ShapeDtypeStruct((2, ROWS // 2, columns), BF)] * 2,
        in_specs=[
            pl.BlockSpec(memory_space=pltpu.SMEM),
            whole,
            whole,
            whole,
            pl.BlockSpec(memory_space=pltpu.HBM),
            ANY,
        ],
        out_specs=[whole, whole],
        scratch_shapes=[
            pltpu.VMEM((ROWS, TILE), F32),
            pltpu.VMEM((2 * chips, ROWS, TILE), BF),
            pltpu.SemaphoreType.DMA((2 * chips,)),
        ],
        name="fisher_parts",
        **params(14),
    )(where, acts, mine, peer, weights, after)


def add_kernel(split, divide, *refs):
    out, refs = refs[-1], refs[:-2]
    counts, columns = split
    at = 0
    parts = []
    for count, width in zip(counts, columns):
        parts.append(refs[at : at + count])
        at += count
    joint = refs[at:]
    first = 0
    for own, width in zip(parts, columns):
        cols = slice(first, first + width)
        first += width
        total = own[0][...].astype(F32)
        for ref in own[1:]:
            total = total + ref[...].astype(F32)
        for ref in joint:
            total = total + ref[:, :, cols].astype(F32)
        if divide:
            out[:, cols] = (total[0] / total[1]).astype(BF)
        else:
            out[:, :, cols] = total.astype(BF)


def add_up(parts, joint, rows, after, divide):
    widths = tuple(part[0][0].shape[2] for part in parts)
    columns = sum(widths)
    shape = (rows, columns) if divide else (2, rows, columns)
    arrays = [pair for part in parts for pair in part] + joint

    def block(array, at):
        return pl.BlockSpec((2, rows, array.shape[2]), lambda i: (0, at // rows, 0))

    split = tuple(len(part) for part in parts), widths
    return pl.pallas_call(
        functools.partial(add_kernel, split, divide),
        out_shape=jax.ShapeDtypeStruct(shape, BF),
        grid=(1,),
        in_specs=[block(*pair) for pair in arrays] + [ANY],
        out_specs=pl.BlockSpec(shape, lambda i: (0,) * len(shape)),
        name="merge" if divide else "add_up",
        **params(),
    )(*[array for array, _ in arrays], after)


def join_kernel(a, b, after, out):
    rows = a.shape[0]
    out[:rows] = a[...]
    out[rows:] = b[...]


def join(a, b, after):
    whole = pl.BlockSpec(memory_space=pltpu.VMEM)
    return pl.pallas_call(
        join_kernel,
        out_shape=jax.ShapeDtypeStruct((2 * a.shape[0], a.shape[1]), BF),
        in_specs=[whole, whole, ANY],
        out_specs=whole,
        name="join",
        **params(),
    )(a, b, after)


def place_kernel(where, far, near, *refs):
    out = refs[-1]
    mark = where[0]
    for k in range(16):
        ref, at = (far, k) if k < 8 else (near, k - 8)
        part = pl.ds(pl.multiple_of((mark ^ (15 - k)) * S, S), S)
        out[part, :] = ref[at * S : (at + 1) * S, :]


def place(out, far, near, at, chips, where, weights, after):
    tiles = 2 * chips
    block = pl.BlockSpec((ROWS // 2, TILE), lambda i, s: (0, i + 2 * at))
    extra = [after] if out is None else [after, out]
    return pl.pallas_call(
        place_kernel,
        out_shape=jax.ShapeDtypeStruct(weights.shape, BF),
        grid_spec=pltpu.PrefetchScalarGridSpec(
            num_scalar_prefetch=1,
            grid=(tiles,),
            in_specs=[block, block] + [ANY] * len(extra),
            out_specs=pl.BlockSpec((ROWS, TILE), lambda i, s: (0, s[1 + i])),
        ),
        input_output_aliases={} if out is None else {4: 0},
        name="place",
        **params(),
    )(where, far, near, *extra)


def on_device(activations, cotangents, checkpoints):
    y, w, v, x, c = (lax.axis_index(axis) for axis in ("y", "w", "v", "x", "c"))
    weights = checkpoints[0]
    own = cotangents[0]
    y1, y2 = bits(y, c)
    w1, w2 = bits(w, c)
    mark = y1 * 8 + w1 * 4 + y2 * 2 + w2

    near = exchange(own, "x", 0)
    other = swap(own, "v")
    acts = jnp.swapaxes(activations[0], 1, 2)

    def chip(which, core):
        first = partner(x, core, 0)
        second = partner(x, core, 1)
        return (x, first, second, partner(second, core, 0))[which]

    def places(layer, pair):
        tiles = [mark]
        for which in pair:
            for core in (c, 1 - c):
                tiles.append((layer * 4 + chip(which, core)) * 2 + core)
        return jnp.stack(tiles).astype(jnp.int32)

    where = {
        "A": places(v, (0, 1)),
        "B": places(v, (2, 3)),
        "C": places(1 - v, (0, 1)),
        "D": places(1 - v, (2, 3)),
    }
    mine, peer = {}, {}
    parts = {name: [] for name in where}
    joint = {group: [] for group in GROUPS}
    made = {}
    last, out = acts, None

    for step in ORDER:
        if step == "SA":
            last = mine["A"] = stack(own, near, last)
            peer["A"] = swap(mine["A"], "c")
            mine["B"] = exchange(mine["A"], "x", 1)
            continue
        if step == "hV":
            last = other = hold(other, last)
            beyond = exchange(other, "x", 0)
            continue
        if step == "SC":
            last = mine["C"] = stack(other, beyond, last)
            peer["C"] = swap(mine["C"], "c")
            mine["D"] = exchange(mine["C"], "x", 1)
            continue
        if step in ("hB", "hD"):
            name = step[1]
            last = mine[name] = hold(mine[name], last)
            peer[name] = swap(mine[name], "c")
            continue
        name, stage = step[:-1], int(step[-1])
        have = made.get(name)
        axis = "yw"[(stage if stage < 4 else 7 - stage) % 2]
        which = (stage if stage < 4 else 7 - stage) // 2
        if stage == 0:
            send, keep = fisher_parts(acts, mine[name], peer[name], weights, where[name], last)
            parts[name] = [(keep, 0), (exchange(send, axis, which), 0)]
            last = send
        elif stage < 5:
            rows = (128, 64, 32, 32)[stage - 1]
            start = (0, 128, 192, 224)[stage - 1]
            chunks = [[(a, start - f) for a, f in parts[c]] for c in name]
            both = [(a, start - f) for a, f in joint.get(name, [])]
            last = add_up(chunks, both, rows, last, stage == 4)
            if stage < 4:
                came = exchange(last, axis, which), start + rows
                (joint[name] if name in joint and stage >= MERGE else parts[name]).append(came)
            else:
                made[name] = [last, exchange(last, axis, which)]
        elif stage < 8:
            last = join(have[1], have[0], last)
            made[name] = [last, exchange(last, axis, which)]
        else:
            at = 0
            for c in name:
                out = place(out, have[1], have[0], at, mine[c].shape[0], where[c], weights, last)
                at += mine[c].shape[0]
    return out


def solution(mesh):
    fine = Mesh(mesh.devices.reshape(4, 4, 2, 4, 2), ("y", "w", "v", "x", "c"))
    mp, tp = ("y", "w"), ("v", "x", "c")
    in_specs = (P(mp, None, None, tp), P(mp, None, None, tp), P(mp, tp, None))
    return jax.shard_map(
        on_device, mesh=fine, in_specs=in_specs, out_specs=P(tp, None), check_vma=False
    )
```

time: 473 us -> 212 us (0.45)
  the two profiles are of different devices: /device:TPU:22 before, /device:TPU:24 now
where the time goes in v1:
time: 212 us; the launch traced here: 211 us
  waiting for transfers between devices  83.8 us (40%)
  starting transfers between devices  77.3 us (36%)
  Pallas kernels  38.2 us (18%)
  local copies, waits for them, and re-layouts  11.5 us (5%)
    ppermute x36, starting transfers between devices, exchange(): return lax.ppermute(value, (axis, 'c'), pairs)  74.6 us
    ppermute x36, waiting for transfers between devices, exchange(): return lax.ppermute(value, (axis, 'c'), pairs)  74.6 us
    pallas_call x4, Pallas kernels, fisher_parts(): pl.pallas_call(fisher_kernel, out_shape=[jax.ShapeDtypeStruct((2, ROWS //...  17.8 us
    unnamed x23, local copies, waits for them, and re-layouts  11.2 us
    ppermute x5, waiting for transfers between devices, swap(): return lax.ppermute(value, axis, [(0, 1), (1, 0)])  9.24 us
    pallas_call x16, Pallas kernels, add_up(): pl.pallas_call(functools.partial(add_kernel, split, divide), out_shape=ja...  9.16 us
    pallas_call x4, Pallas kernels, place(): pl.pallas_call(place_kernel, out_shape=jax.ShapeDtypeStruct(weights.shape...  8.96 us
  transfers between devices with their start and end apart: 41, of which 20 were waited for; matrix products, arithmetic and copies ran while one was open for 1% of the time, Pallas kernels for 17%

profile of v1, /device:TPU:24, one launch (start us, length us, event | category | flops | bytes accessed | tf_op | source)
XLA Modules:
  0.0 211.2 jit_solution(3590765632710516015)
XLA Ops:
  0.0 1.9 collective-permute-start.1
  1.9 1.5 collective-permute-start
  4.9 9.2 %collective-permute-done.1.value = bf16[4,256,256]{2,1,0:T(8,128)(2,1)S(1)} collective-permute-done((bf16[4,256,256]{2,1,0:T(8,128)(2,1)}, bf16[4,256,256]{2,1,0:T(8,128)(2,1)S(1)}, u32[]{:S(2)}, u32[]{:S(2)}) %collective-permute-start.1) | collective-permute-done | bytes 524320 | tf_op jit(solution)/shard_map/ppermute | solution.py:49
  16.9 1.9 collective-permute-start.2
  18.8 7.8 %collective-permute-done.4.b = bf16[4,256,256]{2,1,0:T(8,128)(2,1)S(1)} collective-permute-done((bf16[4,256,256]{2,1,0:T(8,128)(2,1)S(1)}, bf16[4,256,256]{2,1,0:T(8,128)(2,1)S(1)}, u32[]{:S(2)}, u32[]{:S(2)}) %collective-permute-start.4) | collective-permute-done | bytes 524320 | tf_op jit(solution)/shard_map/ppermute | solution.py:45
  27.6 3.4 %collective-permute-start.7 = (bf16[2,4,256,256]{3,2,1,0:T(8,128)(2,1)}, bf16[2,4,256,256]{3,2,1,0:T(8,128)(2,1)}, u32[]{:S(2)}, u32[]{:S(2)}) collective-permute-start(bf16[2,4,256,256]{3,2,1,0:T(8,128)(2,1)} %stack.90.after.mine), channel_id=1, source_target_pairs={{0,6},{1,3},{2,4},{3,1},{4,2},{5,7},{6,0},{7,5},{8,14},{9,11},{10,... | collective-permute-start | bytes 3145736 | tf_op jit(solution)/shard_map/ppermute | solution.py:45
  31.1 2.2 %copy-done = bf16[1,512,4096]{2,1,0:T(8,128)(2,1)S(1)} copy-done((bf16[1,512,4096]{2,1,0:T(8,128)(2,1)S(1)}, bf16[1,512,4096]{2,1,0:T(8,128)(2,1)}, u32[]{:S(2)}) %copy-start) | copy-done | bytes 4194328
  33.3 4.4 %fisher_parts.4 = (bf16[2,256,1024]{2,1,0:T(8,128)(2,1)}, bf16[2,256,1024]{2,1,0:T(8,128)(2,1)S(1)}) custom-call(s32[5]{0:T(128)S(1)} %stack.78.where, bf16[4,512,256]{2,1,0:T(8,128)(2,1)S(1)} %bitcast.27, bf16[2,4,256,256]{3,2,1,0:T(8,128)(2,1)} %stack.89.after.mine, bf16[2,4,256,256]{3,2,1,0:T(8,128)(2,1)S(1)} %collective-permute-done.3.peer, ...), custom_call_target="tpu_custom_call" | custom-call | flops 1 | bytes 1 | tf_op jit(solution)/shard_map/fisher_parts/pallas_call | solution.py:135
  38.7 2.2 %copy-done.1 = bf16[1,512,4096]{2,1,0:T(8,128)(2,1)S(1)} copy-done((bf16[1,512,4096]{2,1,0:T(8,128)(2,1)S(1)}, bf16[1,512,4096]{2,1,0:T(8,128)(2,1)}, u32[]{:S(2)}) %copy-start.1) | copy-done | bytes 4194328
  40.9 4.7 %fisher_parts.5 = (bf16[2,256,1024]{2,1,0:T(8,128)(2,1)}, bf16[2,256,1024]{2,1,0:T(8,128)(2,1)S(1)}) custom-call(s32[5]{0:T(128)S(1)} %stack.83.where, bf16[4,512,256]{2,1,0:T(8,128)(2,1)S(1)} %bitcast.28, bf16[2,4,256,256]{3,2,1,0:T(8,128)(2,1)} %stack.90.after.mine, bf16[2,4,256,256]{3,2,1,0:T(8,128)(2,1)} %collective-permute-done.8.peer, ...), custom_call_target="tpu_custom_call" | custom-call | flops 1 | bytes 1 | tf_op jit(solution)/shard_map/fisher_parts/pallas_call | solution.py:135
  48.5 4.4 %collective-permute-done.6.refs_1_ = bf16[2,256,1024]{2,1,0:T(8,128)(2,1)S(1)} collective-permute-done((bf16[2,256,1024]{2,1,0:T(8,128)(2,1)}, bf16[2,256,1024]{2,1,0:T(8,128)(2,1)S(1)}, u32[]{:S(2)}, u32[]{:S(2)}) %collective-permute-start.6) | collective-permute-done | bytes 1048608 | tf_op jit(solution)/shard_map/ppermute | solution.py:45
  53.9 3.3 %collective-permute-start.10 = (bf16[2,128,1024]{2,1,0:T(8,128)(2,1)}, bf16[2,128,1024]{2,1,0:T(8,128)(2,1)}, u32[]{:S(2)}, u32[]{:S(2)}) collective-permute-start(bf16[2,128,1024]{2,1,0:T(8,128)(2,1)} %add_up.12.after), channel_id=1, source_target_pairs={{0,16},{1,49},{16,0},{17,33},{32,48},{33,17},{48,32},{49,1},{2,18}... | collective-permute-start | bytes 1572872 | tf_op jit(solution)/shard_map/ppermute | solution.py:45
  57.2 2.2 %copy-done.2 = bf16[1,512,4096]{2,1,0:T(8,128)(2,1)S(1)} copy-done((bf16[1,512,4096]{2,1,0:T(8,128)(2,1)S(1)}, bf16[1,512,4096]{2,1,0:T(8,128)(2,1)}, u32[]{:S(2)}) %copy-start.2) | copy-done | bytes 4194328
  59.4 4.7 %fisher_parts.6 = (bf16[2,256,1024]{2,1,0:T(8,128)(2,1)}, bf16[2,256,1024]{2,1,0:T(8,128)(2,1)S(1)}) custom-call(s32[5]{0:T(128)S(1)} %stack.73.where, bf16[4,512,256]{2,1,0:T(8,128)(2,1)S(1)} %bitcast.29, bf16[2,4,256,256]{3,2,1,0:T(8,128)(2,1)} %hold.4.after.mine, bf16[2,4,256,256]{3,2,1,0:T(8,128)(2,1)} %collective-permute-done.5.peer, ...), custom_call_target="tpu_custom_call" | custom-call | flops 1 | bytes 1 | tf_op jit(solution)/shard_map/fisher_parts/pallas_call | solution.py:135
  65.0 2.2 %copy-done.3 = bf16[1,512,4096]{2,1,0:T(8,128)(2,1)S(1)} copy-done((bf16[1,512,4096]{2,1,0:T(8,128)(2,1)S(1)}, bf16[1,512,4096]{2,1,0:T(8,128)(2,1)}, u32[]{:S(2)}) %copy-start.3) | copy-done | bytes 4194328
  67.2 3.9 %fisher_parts.7 = (bf16[2,256,1024]{2,1,0:T(8,128)(2,1)S(1)}, bf16[2,256,1024]{2,1,0:T(8,128)(2,1)S(1)}) custom-call(s32[5]{0:T(128)S(1)} %stack.88.where, bf16[4,512,256]{2,1,0:T(8,128)(2,1)S(1)} %bitcast.30, bf16[2,4,256,256]{3,2,1,0:T(8,128)(2,1)} %hold.5.refs_2_.mine, bf16[2,4,256,256]{3,2,1,0:T(8,128)(2,1)} %collective-permute-done.11.peer, ...), custom_call_target="tpu_custom_call" | custom-call | flops 1 | bytes 1 | tf_op jit(solution)/shard_map/fisher_parts/pallas_call | solution.py:135
  75.3 10.2 %collective-permute-done.12.refs_3_ = bf16[2,64,1024]{2,1,0:T(8,128)(2,1)S(1)} collective-permute-done((bf16[2,64,1024]{2,1,0:T(8,128)(2,1)S(1)}, bf16[2,64,1024]{2,1,0:T(8,128)(2,1)S(1)}, u32[]{:S(2)}, u32[]{:S(2)}) %collective-permute-start.12) | collective-permute-done | bytes 262176 | tf_op jit(solution)/shard_map/ppermute | solution.py:45
  86.5 5.7 %collective-permute-start.15 = (bf16[2,32,1024]{2,1,0:T(8,128)(2,1)S(1)}, bf16[2,32,1024]{2,1,0:T(8,128)(2,1)S(1)}, u32[]{:S(2)}, u32[]{:S(2)}) collective-permute-start(bf16[2,32,1024]{2,1,0:T(8,128)(2,1)S(1)} %add_up.15.refs_2_), channel_id=1, source_target_pairs={{0,48},{1,17},{16,32},{17,1},{32,16},{33,49},{48,0},{49,33},{2,50}... | collective-permute-start | bytes 393224 | tf_op jit(solution)/shard_map/ppermute | solution.py:45
  92.3 1.5 collective-permute-start.14
  93.9 8.1 %collective-permute-done.15.refs_4_ = bf16[2,32,1024]{2,1,0:T(8,128)(2,1)S(1)} collective-permute-done((bf16[2,32,1024]{2,1,0:T(8,128)(2,1)S(1)}, bf16[2,32,1024]{2,1,0:T(8,128)(2,1)S(1)}, u32[]{:S(2)}, u32[]{:S(2)}) %collective-permute-start.15) | collective-permute-done | bytes 131104 | tf_op jit(solution)/shard_map/ppermute | solution.py:45
  105.3 3.9 %collective-permute-start.16 = (bf16[32,1024]{1,0:T(8,128)(2,1)S(1)}, bf16[32,1024]{1,0:T(8,128)(2,1)S(1)}, u32[]{:S(2)}, u32[]{:S(2)}) collective-permute-start(bf16[32,1024]{1,0:T(8,128)(2,1)S(1)} %merge.4.refs_3_.b), channel_id=1, source_target_pairs={{0,48},{1,17},{16,32},{17,1},{32,16},{33,49},{48,0},{49,33},{2,50}... | collective-permute-start | bytes 196616 | tf_op jit(solution)/shard_map/ppermute | solution.py:45
  109.2 3.7 %collective-permute-done.18.refs_3_ = bf16[2,64,1024]{2,1,0:T(8,128)(2,1)S(1)} collective-permute-done((bf16[2,64,1024]{2,1,0:T(8,128)(2,1)S(1)}, bf16[2,64,1024]{2,1,0:T(8,128)(2,1)S(1)}, u32[]{:S(2)}, u32[]{:S(2)}) %collective-permute-start.18) | collective-permute-done | bytes 262176 | tf_op jit(solution)/shard_map/ppermute | solution.py:45
  115.1 5.3 %collective-permute-done.20.a = bf16[64,1024]{1,0:T(8,128)(2,1)S(1)} collective-permute-done((bf16[64,1024]{1,0:T(8,128)(2,1)S(1)}, bf16[64,1024]{1,0:T(8,128)(2,1)S(1)}, u32[]{:S(2)}, u32[]{:S(2)}) %collective-permute-start.20) | collective-permute-done | bytes 131104 | tf_op jit(solution)/shard_map/ppermute | solution.py:45
  121.6 2.4 %collective-permute-start.25 = (bf16[2,64,1024]{2,1,0:T(8,128)(2,1)S(1)}, bf16[2,64,1024]{2,1,0:T(8,128)(2,1)S(1)}, u32[]{:S(2)}, u32[]{:S(2)}) collective-permute-start(bf16[2,64,1024]{2,1,0:T(8,128)(2,1)S(1)} %add_up.21.refs_4_), channel_id=1, source_target_pairs={{0,192},{1,65},{64,128},{65,1},{128,64},{129,193},{192,0},{193,129... | collective-permute-start | bytes 786440 | tf_op jit(solution)/shard_map/ppermute | solution.py:45
  124.0 3.6 %collective-permute-start.24 = (bf16[2,32,1024]{2,1,0:T(8,128)(2,1)S(1)}, bf16[2,32,1024]{2,1,0:T(8,128)(2,1)S(1)}, u32[]{:S(2)}, u32[]{:S(2)}) collective-permute-start(bf16[2,32,1024]{2,1,0:T(8,128)(2,1)S(1)} %add_up.19.after), channel_id=1, source_target_pairs={{0,48},{1,17},{16,32},{17,1},{32,16},{33,49},{48,0},{49,33},{2,50}... | collective-permute-start | bytes 393224 | tf_op jit(solution)/shard_map/ppermute | solution.py:45
  128.2 3.7 %collective-permute-start.23 = (bf16[2,32,1024]{2,1,0:T(8,128)(2,1)S(1)}, bf16[2,32,1024]{2,1,0:T(8,128)(2,1)S(1)}, u32[]{:S(2)}, u32[]{:S(2)}) collective-permute-start(bf16[2,32,1024]{2,1,0:T(8,128)(2,1)S(1)} %add_up.22.refs_4_), channel_id=1, source_target_pairs={{0,48},{1,17},{16,32},{17,1},{32,16},{33,49},{48,0},{49,33},{2,50}... | collective-permute-start | bytes 393224 | tf_op jit(solution)/shard_map/ppermute | solution.py:45
  132.1 2.7 %collective-permute-start.28 = (bf16[2,32,1024]{2,1,0:T(8,128)(2,1)S(1)}, bf16[2,32,1024]{2,1,0:T(8,128)(2,1)S(1)}, u32[]{:S(2)}, u32[]{:S(2)}) collective-permute-start(bf16[2,32,1024]{2,1,0:T(8,128)(2,1)S(1)} %add_up.23.refs_5_), channel_id=1, source_target_pairs={{0,48},{1,17},{16,32},{17,1},{32,16},{33,49},{48,0},{49,33},{2,50}... | collective-permute-start | bytes 393224 | tf_op jit(solution)/shard_map/ppermute | solution.py:45
  135.8 1.6 collective-permute-start.27
  137.5 2.7 %collective-permute-start.26 = (bf16[32,1024]{1,0:T(8,128)(2,1)S(1)}, bf16[32,1024]{1,0:T(8,128)(2,1)S(1)}, u32[]{:S(2)}, u32[]{:S(2)}) collective-permute-start(bf16[32,1024]{1,0:T(8,128)(2,1)S(1)} %merge.6.refs_5_.b), channel_id=1, source_target_pairs={{0,48},{1,17},{16,32},{17,1},{32,16},{33,49},{48,0},{49,33},{2,50}... | collective-permute-start | bytes 196616 | tf_op jit(solution)/shard_map/ppermute | solution.py:45
  140.8 3.8 %collective-permute-start.30 = (bf16[32,1024]{1,0:T(8,128)(2,1)S(1)}, bf16[32,1024]{1,0:T(8,128)(2,1)S(1)}, u32[]{:S(2)}, u32[]{:S(2)}) collective-permute-start(bf16[32,1024]{1,0:T(8,128)(2,1)S(1)} %merge.7.after.b), channel_id=1, source_target_pairs={{0,48},{1,17},{16,32},{17,1},{32,16},{33,49},{48,0},{49,33},{2,50}... | collective-permute-start | bytes 196616 | tf_op jit(solution)/shard_map/ppermute | solution.py:45
  144.6 5.1 %collective-permute-done.26.a = bf16[32,1024]{1,0:T(8,128)(2,1)S(1)} collective-permute-done((bf16[32,1024]{1,0:T(8,128)(2,1)S(1)}, bf16[32,1024]{1,0:T(8,128)(2,1)S(1)}, u32[]{:S(2)}, u32[]{:S(2)}) %collective-permute-start.26) | collective-permute-done | bytes 65568 | tf_op jit(solution)/shard_map/ppermute | solution.py:45
  149.7 1.5 collective-permute-done.30.a
  151.2 1.8 collective-permute-start.31
  153.0 12.0 %collective-permute-start.33 = (bf16[128,1024]{1,0:T(8,128)(2,1)S(1)}, bf16[128,1024]{1,0:T(8,128)(2,1)S(1)}, u32[]{:S(2)}, u32[]{:S(2)}) collective-permute-start(bf16[128,1024]{1,0:T(8,128)(2,1)S(1)} %join.13.refs_3_.b), channel_id=1, source_target_pairs={{0,16},{1,49},{16,0},{17,33},{32,48},{33,17},{48,32},{49,1},{2,18}... | collective-permute-start | bytes 786440 | tf_op jit(solution)/shard_map/ppermute | solution.py:45
  165.1 3.5 %collective-permute-start.32 = (bf16[128,1024]{1,0:T(8,128)(2,1)S(1)}, bf16[128,1024]{1,0:T(8,128)(2,1)S(1)}, u32[]{:S(2)}, u32[]{:S(2)}) collective-permute-start(bf16[128,1024]{1,0:T(8,128)(2,1)S(1)} %join.17.after.b), channel_id=1, source_target_pairs={{0,16},{1,49},{16,0},{17,33},{32,48},{33,17},{48,32},{49,1},{2,18}... | collective-permute-start | bytes 786440 | tf_op jit(solution)/shard_map/ppermute | solution.py:45
  168.6 3.5 %collective-permute-start.34 = (bf16[64,1024]{1,0:T(8,128)(2,1)S(1)}, bf16[64,1024]{1,0:T(8,128)(2,1)S(1)}, u32[]{:S(2)}, u32[]{:S(2)}) collective-permute-start(bf16[64,1024]{1,0:T(8,128)(2,1)S(1)} %join.14.after.b), channel_id=1, source_target_pairs={{0,192},{1,65},{64,128},{65,1},{128,64},{129,193},{192,0},{193,129... | collective-permute-start | bytes 393224 | tf_op jit(solution)/shard_map/ppermute | solution.py:45
  172.2 4.4 %collective-permute-done.34.a = bf16[64,1024]{1,0:T(8,128)(2,1)S(1)} collective-permute-done((bf16[64,1024]{1,0:T(8,128)(2,1)S(1)}, bf16[64,1024]{1,0:T(8,128)(2,1)S(1)}, u32[]{:S(2)}, u32[]{:S(2)}) %collective-permute-start.34) | collective-permute-done | bytes 131104 | tf_op jit(solution)/shard_map/ppermute | solution.py:45
  176.8 5.8 %collective-permute-done.32.a = bf16[128,1024]{1,0:T(8,128)(2,1)S(1)} collective-permute-done((bf16[128,1024]{1,0:T(8,128)(2,1)S(1)}, bf16[128,1024]{1,0:T(8,128)(2,1)S(1)}, u32[]{:S(2)}, u32[]{:S(2)}) %collective-permute-start.32) | collective-permute-done | bytes 262176 | tf_op jit(solution)/shard_map/ppermute | solution.py:45
  182.9 2.0 collective-permute-start.39
  185.6 4.5 %collective-permute-done.35.a = bf16[128,1024]{1,0:T(8,128)(2,1)S(1)} collective-permute-done((bf16[128,1024]{1,0:T(8,128)(2,1)S(1)}, bf16[128,1024]{1,0:T(8,128)(2,1)S(1)}, u32[]{:S(2)}, u32[]{:S(2)}) %collective-permute-start.35) | collective-permute-done | bytes 262176 | tf_op jit(solution)/shard_map/ppermute | solution.py:45
  190.2 1.9 collective-permute-done.40.far
  192.1 2.2 %place.4.refs_1_ = bf16[512,4096]{1,0:T(8,128)(2,1)} custom-call(s32[5]{0:T(128)S(1)} %stack.78.where, bf16[256,1024]{1,0:T(8,128)(2,1)S(1)} %collective-permute-done.40.far, bf16[256,1024]{1,0:T(8,128)(2,1)S(1)} %join.19.after.near, bf16[128,1024]{1,0:T(8,128)(2,1)S(1)} %join.21.after.b.refs_0_), custom_call_target="tpu_custom_call" | custom-call | flops 1 | bytes 1 | tf_op jit(solution)/shard_map/place/pallas_call | solution.py:233
  194.3 3.4 %collective-permute-done.39.far = bf16[256,1024]{1,0:T(8,128)(2,1)S(1)} collective-permute-done((bf16[256,1024]{1,0:T(8,128)(2,1)S(1)}, bf16[256,1024]{1,0:T(8,128)(2,1)S(1)}, u32[]{:S(2)}, u32[]{:S(2)}) %collective-permute-start.39) | collective-permute-done | bytes 524320 | tf_op jit(solution)/shard_map/ppermute | solution.py:45
  197.7 2.2 %place.5.refs_1_ = bf16[512,4096]{1,0:T(8,128)(2,1)} custom-call(s32[5]{0:T(128)S(1)} %stack.88.where, bf16[256,1024]{1,0:T(8,128)(2,1)S(1)} %collective-permute-done.39.far, bf16[256,1024]{1,0:T(8,128)(2,1)S(1)} %join.20.after.near, bf16[256,1024]{1,0:T(8,128)(2,1)S(1)} %join.23.refs_0_.near, ...), custom_call_target="tpu_custom_call", output_to_operand_aliasing={{}: (4, {})} | custom-call | flops 1 | bytes 1 | tf_op jit(solution)/shard_map/place/pallas_call | solution.py:233
  200.0 3.4 %collective-permute-done.38.far = bf16[256,1024]{1,0:T(8,128)(2,1)S(1)} collective-permute-done((bf16[256,1024]{1,0:T(8,128)(2,1)S(1)}, bf16[256,1024]{1,0:T(8,128)(2,1)S(1)}, u32[]{:S(2)}, u32[]{:S(2)}) %collective-permute-start.38) | collective-permute-done | bytes 524320 | tf_op jit(solution)/shard_map/ppermute | solution.py:45
  203.3 2.2 %place.6.refs_1_ = bf16[512,4096]{1,0:T(8,128)(2,1)} custom-call(s32[5]{0:T(128)S(1)} %stack.83.where, bf16[256,1024]{1,0:T(8,128)(2,1)S(1)} %collective-permute-done.38.far, bf16[256,1024]{1,0:T(8,128)(2,1)S(1)} %join.22.after.near, bf16[256,1024]{1,0:T(8,128)(2,1)S(1)} %join.23.refs_0_.near, ...), custom_call_target="tpu_custom_call", output_to_operand_aliasing={{}: (4, {})} | custom-call | flops 1 | bytes 1 | tf_op jit(solution)/shard_map/place/pallas_call | solution.py:233
  205.6 3.4 %collective-permute-done.37.far = bf16[256,1024]{1,0:T(8,128)(2,1)S(1)} collective-permute-done((bf16[256,1024]{1,0:T(8,128)(2,1)S(1)}, bf16[256,1024]{1,0:T(8,128)(2,1)S(1)}, u32[]{:S(2)}, u32[]{:S(2)}) %collective-permute-start.37) | collective-permute-done | bytes 524320 | tf_op jit(solution)/shard_map/ppermute | solution.py:45
  209.0 2.2 %place.7 = bf16[512,4096]{1,0:T(8,128)(2,1)} custom-call(s32[5]{0:T(128)S(1)} %stack.73.where, bf16[256,1024]{1,0:T(8,128)(2,1)S(1)} %collective-permute-done.37.far, bf16[256,1024]{1,0:T(8,128)(2,1)S(1)} %join.23.refs_0_.near, bf16[256,1024]{1,0:T(8,128)(2,1)S(1)} %join.23.refs_0_.near, bf16[512,4096]{1,0:T(8,128)(2,1)} %place.6.refs_1_), custom_call_target="tpu_custom_call", output_to_operand_aliasing={{}: (4, {})} | custom-call | flops 1 | bytes 1 | tf_op jit(solution)/shard_map/place/pallas_call | solution.py:233
  (102 shorter events, 26.6 us)
Async XLA Ops:
  0.0 15.6 %copy-start.10 = (bf16[1,4,256,256]{3,2,1,0:T(8,128)(2,1)S(1)}, bf16[1,4,256,256]{3,2,1,0:T(8,128)(2,1)}, u32[]{:S(2)}) copy-start(bf16[1,4,256,256]{3,2,1,0:T(8,128)(2,1)} %param.4) | copy-start | bytes 1572868
  0.0 14.1 %collective-permute-start.1 = (bf16[4,256,256]{2,1,0:T(8,128)(2,1)}, bf16[4,256,256]{2,1,0:T(8,128)(2,1)S(1)}, u32[]{:S(2)}, u32[]{:S(2)}) collective-permute-start(bf16[4,256,256]{2,1,0:T(8,128)(2,1)} %bitcast.31), channel_id=1, source_target_pairs={{0,8},{8,0},{1,9},{9,1},{2,10},{10,2},{3,11},{11,3},{4,12},{12,4},... | collective-permute-start | bytes 1572872 | tf_op jit(solution)/shard_map/ppermute | solution.py:49
  1.9 13.7 %collective-permute-start = (bf16[4,256,256]{2,1,0:T(8,128)(2,1)}, bf16[4,256,256]{2,1,0:T(8,128)(2,1)S(1)}, u32[]{:S(2)}, u32[]{:S(2)}) collective-permute-start(bf16[4,256,256]{2,1,0:T(8,128)(2,1)} %bitcast.32), channel_id=1, source_target_pairs={{0,2},{1,7},{2,0},{3,5},{4,6},{5,3},{6,4},{7,1},{8,10},{9,15},{10,... | collective-permute-start | bytes 1572872 | tf_op jit(solution)/shard_map/ppermute | solution.py:45
  14.1 12.4 %collective-permute-start.4 = (bf16[4,256,256]{2,1,0:T(8,128)(2,1)S(1)}, bf16[4,256,256]{2,1,0:T(8,128)(2,1)S(1)}, u32[]{:S(2)}, u32[]{:S(2)}) collective-permute-start(bf16[4,256,256]{2,1,0:T(8,128)(2,1)S(1)} %hold.3.after.a), channel_id=1, source_target_pairs={{0,2},{1,7},{2,0},{3,5},{4,6},{5,3},{6,4},{7,1},{8,10},{9,15},{10,... | collective-permute-start | bytes 1572872 | tf_op jit(solution)/shard_map/ppermute | solution.py:45
  16.7 14.5 %collective-permute-start.3 = (bf16[2,4,256,256]{3,2,1,0:T(8,128)(2,1)}, bf16[2,4,256,256]{3,2,1,0:T(8,128)(2,1)S(1)}, u32[]{:S(2)}, u32[]{:S(2)}) collective-permute-start(bf16[2,4,256,256]{3,2,1,0:T(8,128)(2,1)} %stack.89.after.mine), channel_id=1, source_target_pairs={{0,1},{1,0},{2,3},{3,2},{4,5},{5,4},{6,7},{7,6},{8,9},{9,8},{10,11... | collective-permute-start | bytes 3145736 | tf_op jit(solution)/shard_map/ppermute | solution.py:49
  16.9 21.7 %collective-permute-start.2 = (bf16[2,4,256,256]{3,2,1,0:T(8,128)(2,1)}, bf16[2,4,256,256]{3,2,1,0:T(8,128)(2,1)}, u32[]{:S(2)}, u32[]{:S(2)}) collective-permute-start(bf16[2,4,256,256]{3,2,1,0:T(8,128)(2,1)} %stack.89.after.mine), channel_id=1, source_target_pairs={{0,6},{1,3},{2,4},{3,1},{4,2},{5,7},{6,0},{7,5},{8,14},{9,11},{10,... | collective-permute-start | bytes 3145736 | tf_op jit(solution)/shard_map/ppermute | solution.py:45
  27.6 11.1 %collective-permute-start.8 = (bf16[2,4,256,256]{3,2,1,0:T(8,128)(2,1)}, bf16[2,4,256,256]{3,2,1,0:T(8,128)(2,1)}, u32[]{:S(2)}, u32[]{:S(2)}) collective-permute-start(bf16[2,4,256,256]{3,2,1,0:T(8,128)(2,1)} %stack.90.after.mine), channel_id=1, source_target_pairs={{0,1},{1,0},{2,3},{3,2},{4,5},{5,4},{6,7},{7,6},{8,9},{9,8},{10,11... | collective-permute-start | bytes 3145736 | tf_op jit(solution)/shard_map/ppermute | solution.py:49
  27.6 19.0 %collective-permute-start.7 = (bf16[2,4,256,256]{3,2,1,0:T(8,128)(2,1)}, bf16[2,4,256,256]{3,2,1,0:T(8,128)(2,1)}, u32[]{:S(2)}, u32[]{:S(2)}) collective-permute-start(bf16[2,4,256,256]{3,2,1,0:T(8,128)(2,1)} %stack.90.after.mine), channel_id=1, source_target_pairs={{0,6},{1,3},{2,4},{3,1},{4,2},{5,7},{6,0},{7,5},{8,14},{9,11},{10,... | collective-permute-start | bytes 3145736 | tf_op jit(solution)/shard_map/ppermute | solution.py:45
  37.7 15.1 %copy-start.6 = (bf16[2,256,1024]{2,1,0:T(8,128)(2,1)}, bf16[2,256,1024]{2,1,0:T(8,128)(2,1)S(1)}, u32[]{:S(2)}) copy-start(bf16[2,256,1024]{2,1,0:T(8,128)(2,1)S(1)} %get-tuple-element.14.refs_0_) | copy-start | bytes 3145732
  37.8 15.1 %collective-permute-start.6 = (bf16[2,256,1024]{2,1,0:T(8,128)(2,1)}, bf16[2,256,1024]{2,1,0:T(8,128)(2,1)S(1)}, u32[]{:S(2)}, u32[]{:S(2)}) collective-permute-start(bf16[2,256,1024]{2,1,0:T(8,128)(2,1)} %get-tuple-element.13.after), channel_id=1, source_target_pairs={{0,64},{1,193},{64,0},{65,129},{128,192},{129,65},{192,128},{193,1... | collective-permute-start | bytes 3145736 | tf_op jit(solution)/shard_map/ppermute | solution.py:45
  38.6 18.6 %collective-permute-start.5 = (bf16[2,4,256,256]{3,2,1,0:T(8,128)(2,1)}, bf16[2,4,256,256]{3,2,1,0:T(8,128)(2,1)}, u32[]{:S(2)}, u32[]{:S(2)}) collective-permute-start(bf16[2,4,256,256]{3,2,1,0:T(8,128)(2,1)} %hold.4.after.mine), channel_id=1, source_target_pairs={{0,1},{1,0},{2,3},{3,2},{4,5},{5,4},{6,7},{7,6},{8,9},{9,8},{10,11... | collective-permute-start | bytes 3145736 | tf_op jit(solution)/shard_map/ppermute | solution.py:49
  38.7 2.2 %copy-start.1 = (bf16[1,512,4096]{2,1,0:T(8,128)(2,1)S(1)}, bf16[1,512,4096]{2,1,0:T(8,128)(2,1)}, u32[]{:S(2)}) copy-start(bf16[1,512,4096]{2,1,0:T(8,128)(2,1)} %param.5) | copy-start | bytes 12582916
  46.6 18.5 %collective-permute-start.11 = (bf16[2,4,256,256]{3,2,1,0:T(8,128)(2,1)}, bf16[2,4,256,256]{3,2,1,0:T(8,128)(2,1)}, u32[]{:S(2)}, u32[]{:S(2)}) collective-permute-start(bf16[2,4,256,256]{3,2,1,0:T(8,128)(2,1)} %hold.5.refs_2_.mine), channel_id=1, source_target_pairs={{0,1},{1,0},{2,3},{3,2},{4,5},{5,4},{6,7},{7,6},{8,9},{9,8},{10,11... | collective-permute-start | bytes 3145736 | tf_op jit(solution)/shard_map/ppermute | solution.py:49
  47.1 26.5 %collective-permute-start.13 = (bf16[2,256,1024]{2,1,0:T(8,128)(2,1)}, bf16[2,256,1024]{2,1,0:T(8,128)(2,1)}, u32[]{:S(2)}, u32[]{:S(2)}) collective-permute-start(bf16[2,256,1024]{2,1,0:T(8,128)(2,1)} %get-tuple-element.15.after), channel_id=1, source_target_pairs={{0,64},{1,193},{64,0},{65,129},{128,192},{129,65},{192,128},{193,1... | collective-permute-start | bytes 3145736 | tf_op jit(solution)/shard_map/ppermute | solution.py:45
  52.9 11.2 %copy-start.8 = (bf16[2,256,1024]{2,1,0:T(8,128)(2,1)}, bf16[2,256,1024]{2,1,0:T(8,128)(2,1)S(1)}, u32[]{:S(2)}) copy-start(bf16[2,256,1024]{2,1,0:T(8,128)(2,1)S(1)} %collective-permute-done.6.refs_1_) | copy-start | bytes 3145732
  53.9 18.6 %collective-permute-start.10 = (bf16[2,128,1024]{2,1,0:T(8,128)(2,1)}, bf16[2,128,1024]{2,1,0:T(8,128)(2,1)}, u32[]{:S(2)}, u32[]{:S(2)}) collective-permute-start(bf16[2,128,1024]{2,1,0:T(8,128)(2,1)} %add_up.12.after), channel_id=1, source_target_pairs={{0,16},{1,49},{16,0},{17,33},{32,48},{33,17},{48,32},{49,1},{2,18}... | collective-permute-start | bytes 1572872 | tf_op jit(solution)/shard_map/ppermute | solution.py:45
  64.1 28.1 %collective-permute-start.9 = (bf16[2,256,1024]{2,1,0:T(8,128)(2,1)}, bf16[2,256,1024]{2,1,0:T(8,128)(2,1)S(1)}, u32[]{:S(2)}, u32[]{:S(2)}) collective-permute-start(bf16[2,256,1024]{2,1,0:T(8,128)(2,1)} %get-tuple-element.17.after), channel_id=1, source_target_pairs={{0,64},{1,193},{64,0},{65,129},{128,192},{129,65},{192,128},{193,1... | collective-permute-start | bytes 3145736 | tf_op jit(solution)/shard_map/ppermute | solution.py:45
  67.2 5.3 %copy-start.7 = (bf16[2,256,1024]{2,1,0:T(8,128)(2,1)S(1)}, bf16[2,256,1024]{2,1,0:T(8,128)(2,1)}, u32[]{:S(2)}) copy-start(bf16[2,256,1024]{2,1,0:T(8,128)(2,1)} %copy-done.6) | copy-start | bytes 3145732
  67.2 5.3 %copy-start.9 = (bf16[2,256,1024]{2,1,0:T(8,128)(2,1)S(1)}, bf16[2,256,1024]{2,1,0:T(8,128)(2,1)}, u32[]{:S(2)}) copy-start(bf16[2,256,1024]{2,1,0:T(8,128)(2,1)} %copy-done.8) | copy-start | bytes 3145732
  67.2 6.4 %copy-start.5 = (bf16[2,256,1024]{2,1,0:T(8,128)(2,1)S(1)}, bf16[2,256,1024]{2,1,0:T(8,128)(2,1)}, u32[]{:S(2)}) copy-start(bf16[2,256,1024]{2,1,0:T(8,128)(2,1)} %copy-done.4) | copy-start | bytes 3145732
  71.2 32.9 %collective-permute-start.19 = (bf16[2,256,1024]{2,1,0:T(8,128)(2,1)S(1)}, bf16[2,256,1024]{2,1,0:T(8,128)(2,1)S(1)}, u32[]{:S(2)}, u32[]{:S(2)}) collective-permute-start(bf16[2,256,1024]{2,1,0:T(8,128)(2,1)S(1)} %get-tuple-element.18.refs_3_), channel_id=1, source_target_pairs={{0,64},{1,193},{64,0},{65,129},{128,192},{129,65},{192,128},{193,1... | collective-permute-start | bytes 3145736 | tf_op jit(solution)/shard_map/ppermute | solution.py:45
  74.9 28.2 %collective-permute-start.17 = (bf16[2,128,1024]{2,1,0:T(8,128)(2,1)S(1)}, bf16[2,128,1024]{2,1,0:T(8,128)(2,1)S(1)}, u32[]{:S(2)}, u32[]{:S(2)}) collective-permute-start(bf16[2,128,1024]{2,1,0:T(8,128)(2,1)S(1)} %add_up.14.refs_4_), channel_id=1, source_target_pairs={{0,16},{1,49},{16,0},{17,33},{32,48},{33,17},{48,32},{49,1},{2,18}... | collective-permute-start | bytes 1572872 | tf_op jit(solution)/shard_map/ppermute | solution.py:45
  75.0 10.5 %collective-permute-start.12 = (bf16[2,64,1024]{2,1,0:T(8,128)(2,1)S(1)}, bf16[2,64,1024]{2,1,0:T(8,128)(2,1)S(1)}, u32[]{:S(2)}, u32[]{:S(2)}) collective-permute-start(bf16[2,64,1024]{2,1,0:T(8,128)(2,1)S(1)} %add_up.13.refs_2_), channel_id=1, source_target_pairs={{0,192},{1,65},{64,128},{65,1},{128,64},{129,193},{192,0},{193,129... | collective-permute-start | bytes 786440 | tf_op jit(solution)/shard_map/ppermute | solution.py:45
  86.5 15.5 %collective-permute-start.15 = (bf16[2,32,1024]{2,1,0:T(8,128)(2,1)S(1)}, bf16[2,32,1024]{2,1,0:T(8,128)(2,1)S(1)}, u32[]{:S(2)}, u32[]{:S(2)}) collective-permute-start(bf16[2,32,1024]{2,1,0:T(8,128)(2,1)S(1)} %add_up.15.refs_2_), channel_id=1, source_target_pairs={{0,48},{1,17},{16,32},{17,1},{32,16},{33,49},{48,0},{49,33},{2,50}... | collective-permute-start | bytes 393224 | tf_op jit(solution)/shard_map/ppermute | solution.py:45
  92.3 28.1 %collective-permute-start.14 = (bf16[2,128,1024]{2,1,0:T(8,128)(2,1)S(1)}, bf16[2,128,1024]{2,1,0:T(8,128)(2,1)S(1)}, u32[]{:S(2)}, u32[]{:S(2)}) collective-permute-start(bf16[2,128,1024]{2,1,0:T(8,128)(2,1)S(1)} %add_up.16.refs_5_), channel_id=1, source_target_pairs={{0,16},{1,49},{16,0},{17,33},{32,48},{33,17},{48,32},{49,1},{2,18}... | collective-permute-start | bytes 1572872 | tf_op jit(solution)/shard_map/ppermute | solution.py:45
  104.2 17.2 %collective-permute-start.22 = (bf16[2,128,1024]{2,1,0:T(8,128)(2,1)S(1)}, bf16[2,128,1024]{2,1,0:T(8,128)(2,1)S(1)}, u32[]{:S(2)}, u32[]{:S(2)}) collective-permute-start(bf16[2,128,1024]{2,1,0:T(8,128)(2,1)S(1)} %add_up.18.refs_4_), channel_id=1, source_target_pairs={{0,16},{1,49},{16,0},{17,33},{32,48},{33,17},{48,32},{49,1},{2,18}... | collective-permute-start | bytes 1572872 | tf_op jit(solution)/shard_map/ppermute | solution.py:45
  105.3 7.6 %collective-permute-start.18 = (bf16[2,64,1024]{2,1,0:T(8,128)(2,1)S(1)}, bf16[2,64,1024]{2,1,0:T(8,128)(2,1)S(1)}, u32[]{:S(2)}, u32[]{:S(2)}) collective-permute-start(bf16[2,64,1024]{2,1,0:T(8,128)(2,1)S(1)} %add_up.17.refs_2_), channel_id=1, source_target_pairs={{0,192},{1,65},{64,128},{65,1},{128,64},{129,193},{192,0},{193,129... | collective-permute-start | bytes 786440 | tf_op jit(solution)/shard_map/ppermute | solution.py:45
  105.3 8.8 %collective-permute-start.16 = (bf16[32,1024]{1,0:T(8,128)(2,1)S(1)}, bf16[32,1024]{1,0:T(8,128)(2,1)S(1)}, u32[]{:S(2)}, u32[]{:S(2)}) collective-permute-start(bf16[32,1024]{1,0:T(8,128)(2,1)S(1)} %merge.4.refs_3_.b), channel_id=1, source_target_pairs={{0,48},{1,17},{16,32},{17,1},{32,16},{33,49},{48,0},{49,33},{2,50}... | collective-permute-start | bytes 196616 | tf_op jit(solution)/shard_map/ppermute | solution.py:45
  114.1 6.3 %collective-permute-start.20 = (bf16[64,1024]{1,0:T(8,128)(2,1)S(1)}, bf16[64,1024]{1,0:T(8,128)(2,1)S(1)}, u32[]{:S(2)}, u32[]{:S(2)}) collective-permute-start(bf16[64,1024]{1,0:T(8,128)(2,1)S(1)} %join.12.b.after), channel_id=1, source_target_pairs={{0,192},{1,65},{64,128},{65,1},{128,64},{129,193},{192,0},{193,129... | collective-permute-start | bytes 393224 | tf_op jit(solution)/shard_map/ppermute | solution.py:45
  120.5 7.7 %collective-permute-start.21 = (bf16[2,64,1024]{2,1,0:T(8,128)(2,1)S(1)}, bf16[2,64,1024]{2,1,0:T(8,128)(2,1)S(1)}, u32[]{:S(2)}, u32[]{:S(2)}) collective-permute-start(bf16[2,64,1024]{2,1,0:T(8,128)(2,1)S(1)} %add_up.20.refs_3_), channel_id=1, source_target_pairs={{0,192},{1,65},{64,128},{65,1},{128,64},{129,193},{192,0},{193,129... | collective-permute-start | bytes 786440 | tf_op jit(solution)/shard_map/ppermute | solution.py:45
  121.6 10.4 %collective-permute-start.25 = (bf16[2,64,1024]{2,1,0:T(8,128)(2,1)S(1)}, bf16[2,64,1024]{2,1,0:T(8,128)(2,1)S(1)}, u32[]{:S(2)}, u32[]{:S(2)}) collective-permute-start(bf16[2,64,1024]{2,1,0:T(8,128)(2,1)S(1)} %add_up.21.refs_4_), channel_id=1, source_target_pairs={{0,192},{1,65},{64,128},{65,1},{128,64},{129,193},{192,0},{193,129... | collective-permute-start | bytes 786440 | tf_op jit(solution)/shard_map/ppermute | solution.py:45
  124.0 10.8 %collective-permute-start.24 = (bf16[2,32,1024]{2,1,0:T(8,128)(2,1)S(1)}, bf16[2,32,1024]{2,1,0:T(8,128)(2,1)S(1)}, u32[]{:S(2)}, u32[]{:S(2)}) collective-permute-start(bf16[2,32,1024]{2,1,0:T(8,128)(2,1)S(1)} %add_up.19.after), channel_id=1, source_target_pairs={{0,48},{1,17},{16,32},{17,1},{32,16},{33,49},{48,0},{49,33},{2,50}... | collective-permute-start | bytes 393224 | tf_op jit(solution)/shard_map/ppermute | solution.py:45
  128.2 9.1 %collective-permute-start.23 = (bf16[2,32,1024]{2,1,0:T(8,128)(2,1)S(1)}, bf16[2,32,1024]{2,1,0:T(8,128)(2,1)S(1)}, u32[]{:S(2)}, u32[]{:S(2)}) collective-permute-start(bf16[2,32,1024]{2,1,0:T(8,128)(2,1)S(1)} %add_up.22.refs_4_), channel_id=1, source_target_pairs={{0,48},{1,17},{16,32},{17,1},{32,16},{33,49},{48,0},{49,33},{2,50}... | collective-permute-start | bytes 393224 | tf_op jit(solution)/shard_map/ppermute | solution.py:45
  132.1 8.6 %collective-permute-start.28 = (bf16[2,32,1024]{2,1,0:T(8,128)(2,1)S(1)}, bf16[2,32,1024]{2,1,0:T(8,128)(2,1)S(1)}, u32[]{:S(2)}, u32[]{:S(2)}) collective-permute-start(bf16[2,32,1024]{2,1,0:T(8,128)(2,1)S(1)} %add_up.23.refs_5_), channel_id=1, source_target_pairs={{0,48},{1,17},{16,32},{17,1},{32,16},{33,49},{48,0},{49,33},{2,50}... | collective-permute-start | bytes 393224 | tf_op jit(solution)/shard_map/ppermute | solution.py:45
  135.8 8.8 %collective-permute-start.27 = (bf16[32,1024]{1,0:T(8,128)(2,1)S(1)}, bf16[32,1024]{1,0:T(8,128)(2,1)S(1)}, u32[]{:S(2)}, u32[]{:S(2)}) collective-permute-start(bf16[32,1024]{1,0:T(8,128)(2,1)S(1)} %merge.5.refs_5_.b), channel_id=1, source_target_pairs={{0,48},{1,17},{16,32},{17,1},{32,16},{33,49},{48,0},{49,33},{2,50}... | collective-permute-start | bytes 196616 | tf_op jit(solution)/shard_map/ppermute | solution.py:45
  137.5 12.2 %collective-permute-start.26 = (bf16[32,1024]{1,0:T(8,128)(2,1)S(1)}, bf16[32,1024]{1,0:T(8,128)(2,1)S(1)}, u32[]{:S(2)}, u32[]{:S(2)}) collective-permute-start(bf16[32,1024]{1,0:T(8,128)(2,1)S(1)} %merge.6.refs_5_.b), channel_id=1, source_target_pairs={{0,48},{1,17},{16,32},{17,1},{32,16},{33,49},{48,0},{49,33},{2,50}... | collective-permute-start | bytes 196616 | tf_op jit(solution)/shard_map/ppermute | solution.py:45
  140.8 10.4 %collective-permute-start.30 = (bf16[32,1024]{1,0:T(8,128)(2,1)S(1)}, bf16[32,1024]{1,0:T(8,128)(2,1)S(1)}, u32[]{:S(2)}, u32[]{:S(2)}) collective-permute-start(bf16[32,1024]{1,0:T(8,128)(2,1)S(1)} %merge.7.after.b), channel_id=1, source_target_pairs={{0,48},{1,17},{16,32},{17,1},{32,16},{33,49},{48,0},{49,33},{2,50}... | collective-permute-start | bytes 196616 | tf_op jit(solution)/shard_map/ppermute | solution.py:45
  151.2 13.8 %collective-permute-start.31 = (bf16[64,1024]{1,0:T(8,128)(2,1)S(1)}, bf16[64,1024]{1,0:T(8,128)(2,1)S(1)}, u32[]{:S(2)}, u32[]{:S(2)}) collective-permute-start(bf16[64,1024]{1,0:T(8,128)(2,1)S(1)} %join.16.b.after), channel_id=1, source_target_pairs={{0,192},{1,65},{64,128},{65,1},{128,64},{129,193},{192,0},{193,129... | collective-permute-start | bytes 393224 | tf_op jit(solution)/shard_map/ppermute | solution.py:45
  153.0 23.8 %collective-permute-start.33 = (bf16[128,1024]{1,0:T(8,128)(2,1)S(1)}, bf16[128,1024]{1,0:T(8,128)(2,1)S(1)}, u32[]{:S(2)}, u32[]{:S(2)}) collective-permute-start(bf16[128,1024]{1,0:T(8,128)(2,1)S(1)} %join.13.refs_3_.b), channel_id=1, source_target_pairs={{0,16},{1,49},{16,0},{17,33},{32,48},{33,17},{48,32},{49,1},{2,18}... | collective-permute-start | bytes 786440 | tf_op jit(solution)/shard_map/ppermute | solution.py:45
  165.1 17.6 %collective-permute-start.32 = (bf16[128,1024]{1,0:T(8,128)(2,1)S(1)}, bf16[128,1024]{1,0:T(8,128)(2,1)S(1)}, u32[]{:S(2)}, u32[]{:S(2)}) collective-permute-start(bf16[128,1024]{1,0:T(8,128)(2,1)S(1)} %join.17.after.b), channel_id=1, source_target_pairs={{0,16},{1,49},{16,0},{17,33},{32,48},{33,17},{48,32},{49,1},{2,18}... | collective-permute-start | bytes 786440 | tf_op jit(solution)/shard_map/ppermute | solution.py:45
  168.6 8.0 %collective-permute-start.34 = (bf16[64,1024]{1,0:T(8,128)(2,1)S(1)}, bf16[64,1024]{1,0:T(8,128)(2,1)S(1)}, u32[]{:S(2)}, u32[]{:S(2)}) collective-permute-start(bf16[64,1024]{1,0:T(8,128)(2,1)S(1)} %join.14.after.b), channel_id=1, source_target_pairs={{0,192},{1,65},{64,128},{65,1},{128,64},{129,193},{192,0},{193,129... | collective-permute-start | bytes 393224 | tf_op jit(solution)/shard_map/ppermute | solution.py:45
  172.2 10.5 %collective-permute-start.29 = (bf16[64,1024]{1,0:T(8,128)(2,1)S(1)}, bf16[64,1024]{1,0:T(8,128)(2,1)S(1)}, u32[]{:S(2)}, u32[]{:S(2)}) collective-permute-start(bf16[64,1024]{1,0:T(8,128)(2,1)S(1)} %join.15.after.b), channel_id=1, source_target_pairs={{0,192},{1,65},{64,128},{65,1},{128,64},{129,193},{192,0},{193,129... | collective-permute-start | bytes 393224 | tf_op jit(solution)/shard_map/ppermute | solution.py:45
  176.6 8.8 %collective-permute-start.36 = (bf16[128,1024]{1,0:T(8,128)(2,1)S(1)}, bf16[128,1024]{1,0:T(8,128)(2,1)S(1)}, u32[]{:S(2)}, u32[]{:S(2)}) collective-permute-start(bf16[128,1024]{1,0:T(8,128)(2,1)S(1)} %join.18.after.b), channel_id=1, source_target_pairs={{0,16},{1,49},{16,0},{17,33},{32,48},{33,17},{48,32},{49,1},{2,18}... | collective-permute-start | bytes 786440 | tf_op jit(solution)/shard_map/ppermute | solution.py:45
  182.7 7.4 %collective-permute-start.35 = (bf16[128,1024]{1,0:T(8,128)(2,1)S(1)}, bf16[128,1024]{1,0:T(8,128)(2,1)S(1)}, u32[]{:S(2)}, u32[]{:S(2)}) collective-permute-start(bf16[128,1024]{1,0:T(8,128)(2,1)S(1)} %join.21.after.b.refs_0_), channel_id=1, source_target_pairs={{0,16},{1,49},{16,0},{17,33},{32,48},{33,17},{48,32},{49,1},{2,18}... | collective-permute-start | bytes 786440 | tf_op jit(solution)/shard_map/ppermute | solution.py:45
  182.8 9.3 %collective-permute-start.40 = (bf16[256,1024]{1,0:T(8,128)(2,1)S(1)}, bf16[256,1024]{1,0:T(8,128)(2,1)S(1)}, u32[]{:S(2)}, u32[]{:S(2)}) collective-permute-start(bf16[256,1024]{1,0:T(8,128)(2,1)S(1)} %join.19.after.near), channel_id=1, source_target_pairs={{0,64},{1,193},{64,0},{65,129},{128,192},{129,65},{192,128},{193,1... | collective-permute-start | bytes 1572872 | tf_op jit(solution)/shard_map/ppermute | solution.py:45
  182.9 14.8 %collective-permute-start.39 = (bf16[256,1024]{1,0:T(8,128)(2,1)S(1)}, bf16[256,1024]{1,0:T(8,128)(2,1)S(1)}, u32[]{:S(2)}, u32[]{:S(2)}) collective-permute-start(bf16[256,1024]{1,0:T(8,128)(2,1)S(1)} %join.20.after.near), channel_id=1, source_target_pairs={{0,64},{1,193},{64,0},{65,129},{128,192},{129,65},{192,128},{193,1... | collective-permute-start | bytes 1572872 | tf_op jit(solution)/shard_map/ppermute | solution.py:45
  185.5 17.8 %collective-permute-start.38 = (bf16[256,1024]{1,0:T(8,128)(2,1)S(1)}, bf16[256,1024]{1,0:T(8,128)(2,1)S(1)}, u32[]{:S(2)}, u32[]{:S(2)}) collective-permute-start(bf16[256,1024]{1,0:T(8,128)(2,1)S(1)} %join.22.after.near), channel_id=1, source_target_pairs={{0,64},{1,193},{64,0},{65,129},{128,192},{129,65},{192,128},{193,1... | collective-permute-start | bytes 1572872 | tf_op jit(solution)/shard_map/ppermute | solution.py:45
  190.1 18.8 %collective-permute-start.37 = (bf16[256,1024]{1,0:T(8,128)(2,1)S(1)}, bf16[256,1024]{1,0:T(8,128)(2,1)S(1)}, u32[]{:S(2)}, u32[]{:S(2)}) collective-permute-start(bf16[256,1024]{1,0:T(8,128)(2,1)S(1)} %join.23.refs_0_.near), channel_id=1, source_target_pairs={{0,64},{1,193},{64,0},{65,129},{128,192},{129,65},{192,128},{193,1... | collective-permute-start | bytes 1572872 | tf_op jit(solution)/shard_map/ppermute | solution.py:45
  (4 other events, 7.5 us)

commit v2 on v1

v2 whole, which is shorter than its diff:
```python
import functools

import jax
import jax.numpy as jnp
from jax import lax
from jax.experimental import pallas as pl
from jax.experimental.pallas import tpu as pltpu
from jax.sharding import Mesh
from jax.sharding import PartitionSpec as P

BF = jnp.bfloat16
F32 = jnp.float32
TILE = 256
ROWS = 512
S = 32
MIB = 1024 * 1024
ORDER = (
    "SA A0 hB hV",
    "SC A1 B0 A2",
    "hD C0 B1 A3",
    "D0 B2 A4 B3",
    "C1 D1 C2 B4",
    "A5 D2 C3 A6",
    "D3 B5 C4 A7",
    "B6 D4 C5 D5",
    "C6 B7 D6 C7",
    "D7",
)
ORDER = [step for line in ORDER for step in line.split()]
EXCHANGES = (
    ("y", 0),
    ("y", 1),
    ("w", 0),
    ("w", 1),
    ("w", 0),
    ("y", 1),
    ("y", 0),
)
ANY = pl.BlockSpec(memory_space=pl.ANY)
TOKEN = jax.ShapeDtypeStruct((8, 128), F32)


def partner(i, core, which):
    swap = core if which == 0 else 1 - core
    return (i ^ 1) * (1 - swap) + (3 - i) * swap


def exchange(value, axis, which):
    pairs = [
        (i * 2 + core, partner(i, core, which) * 2 + core) for i in range(4) for core in range(2)
    ]
    return lax.ppermute(value, (axis, "c"), pairs)


def swap(value, axis):
    return lax.ppermute(value, axis, [(0, 1), (1, 0)])


def bits(i, core):
    flips = (i // 2 + i) % 2, i // 2
    return (
        flips[0] * (1 - core) + flips[1] * core,
        flips[1] * (1 - core) + flips[0] * core,
    )


def params(limit=8):
    return dict(
        compiler_params=pltpu.CompilerParams(vmem_limit_bytes=limit * MIB),
        cost_estimate=pl.CostEstimate(flops=1, bytes_accessed=1, transcendentals=0),
    )


def hold_kernel(value, after, out, token):
    pass


def hold(value, after):
    return pl.pallas_call(
        hold_kernel,
        out_shape=[jax.ShapeDtypeStruct(value.shape, value.dtype), TOKEN],
        in_specs=[ANY, ANY],
        out_specs=[ANY, ANY],
        input_output_aliases={0: 0},
        name="hold",
        **params(),
    )(value, after)


def stack_kernel(a, b, after, out, token):
    out[0] = a[...]
    out[1] = b[...]


def stack(a, b, after):
    whole = pl.BlockSpec(memory_space=pltpu.VMEM)
    return pl.pallas_call(
        stack_kernel,
        out_shape=[jax.ShapeDtypeStruct((2, *a.shape), BF), TOKEN],
        in_specs=[whole, whole, ANY],
        out_specs=[whole, ANY],
        name="stack",
        **params(),
    )(a, b, after)


def fisher_kernel(where, acts, mine, peer, weights, after, send, keep, token, total, tiles, sems):
    mark = where[0]
    chips = mine.shape[0]

    def fetch(tile):
        column = pl.multiple_of(where[1 + tile] * TILE, TILE)
        return pltpu.make_async_copy(
            weights.at[:, pl.ds(column, TILE)], tiles.at[tile], sems.at[tile]
        )

    for tile in range(2 * chips):
        fetch(tile).start()
    for tile in range(2 * chips):
        cots = (mine, peer)[tile % 2]
        for number in range(4):
            grad = jnp.dot(acts[number], cots[tile // 2, number], preferred_element_type=F32)
            if number == 0:
                total[...] = grad * grad
            else:
                total[...] += grad * grad
        fetch(tile).wait()
        cols = slice(tile * TILE, (tile + 1) * TILE)
        for k in range(16):
            part = pl.ds(pl.multiple_of((mark ^ (15 - k)) * S, S), S)
            value = total[part, :]
            ref, at = (send, k) if k < 8 else (keep, k - 8)
            out = slice(at * S, (at + 1) * S)
            ref[0, out, cols] = (value * tiles[tile, part, :].astype(F32)).astype(BF)
            ref[1, out, cols] = value.astype(BF)


def fisher_parts(acts, mine, peer, weights, where, after):
    chips = mine.shape[0]
    columns = 2 * TILE * chips
    whole = pl.BlockSpec(memory_space=pltpu.VMEM)
    return pl.pallas_call(
        fisher_kernel,
        out_shape=[jax.ShapeDtypeStruct((2, ROWS // 2, columns), BF)] * 2 + [TOKEN],
        in_specs=[
            pl.BlockSpec(memory_space=pltpu.SMEM),
            whole,
            whole,
            whole,
            pl.BlockSpec(memory_space=pltpu.HBM),
            ANY,
        ],
        out_specs=[whole, whole, ANY],
        scratch_shapes=[
            pltpu.VMEM((ROWS, TILE), F32),
            pltpu.VMEM((2 * chips, ROWS, TILE), BF),
            pltpu.SemaphoreType.DMA((2 * chips,)),
        ],
        name="fisher_parts",
        **params(14),
    )(where, acts, mine, peer, weights, after)


def total_of(refs):
    total = refs[0][...].astype(F32)
    for ref in refs[1:]:
        total = total + ref[...].astype(F32)
    return total


def add_kernel(*refs):
    refs[-2][...] = total_of(refs[:-3]).astype(BF)


def merge_kernel(*refs):
    total = total_of(refs[:-3])
    refs[-2][...] = (total[0] / total[1]).astype(BF)


def add_up(parts, rows, after, divide):
    columns = parts[0][0].shape[2]
    shape = (rows, columns) if divide else (2, rows, columns)

    def block(at):
        return pl.BlockSpec((2, rows, columns), lambda i: (0, at // rows, 0))

    return pl.pallas_call(
        merge_kernel if divide else add_kernel,
        out_shape=[jax.ShapeDtypeStruct(shape, BF), TOKEN],
        grid=(1,),
        in_specs=[block(at) for _, at in parts] + [ANY],
        out_specs=[pl.BlockSpec(shape, lambda i: (0,) * len(shape)), ANY],
        name="merge" if divide else "add_up",
        **params(),
    )(*[array for array, _ in parts], after)


def join_kernel(a, b, after, out, token):
    rows = a.shape[0]
    out[:rows] = a[...]
    out[rows:] = b[...]


def join(a, b, after):
    whole = pl.BlockSpec(memory_space=pltpu.VMEM)
    return pl.pallas_call(
        join_kernel,
        out_shape=[jax.ShapeDtypeStruct((2 * a.shape[0], a.shape[1]), BF), TOKEN],
        in_specs=[whole, whole, ANY],
        out_specs=[whole, ANY],
        name="join",
        **params(),
    )(a, b, after)


def place_kernel(where, far, near, *refs):
    out = refs[-2]
    mark = where[0]
    for k in range(16):
        ref, at = (far, k) if k < 8 else (near, k - 8)
        part = pl.ds(pl.multiple_of((mark ^ (15 - k)) * S, S), S)
        out[part, :] = ref[at * S : (at + 1) * S, :]


def place(out, far, near, where, weights, after):
    block = pl.BlockSpec((ROWS // 2, TILE), lambda i, s: (0, i))
    extra = [after] if out is None else [after, out]
    return pl.pallas_call(
        place_kernel,
        out_shape=[jax.ShapeDtypeStruct(weights.shape, BF), TOKEN],
        grid_spec=pltpu.PrefetchScalarGridSpec(
            num_scalar_prefetch=1,
            grid=(far.shape[1] // TILE,),
            in_specs=[block, block] + [ANY] * len(extra),
            out_specs=[pl.BlockSpec((ROWS, TILE), lambda i, s: (0, s[1 + i])), ANY],
        ),
        input_output_aliases={} if out is None else {4: 0},
        name="place",
        **params(),
    )(where, far, near, *extra)


def on_device(activations, cotangents, checkpoints):
    y, w, v, x, c = (lax.axis_index(axis) for axis in ("y", "w", "v", "x", "c"))
    weights = checkpoints[0]
    own = cotangents[0]
    y1, y2 = bits(y, c)
    w1, _ = bits(w, c)
    mark = y1 * 8 + y2 * 4 + w1 * 2

    near = exchange(own, "x", 0)
    other = swap(own, "v")
    acts = jnp.swapaxes(activations[0], 1, 2)

    def chip(which, core):
        first = partner(x, core, 0)
        second = partner(x, core, 1)
        return (x, first, second, partner(second, core, 0))[which]

    def places(layer, pair):
        tiles = [mark]
        for which in pair:
            for core in (c, 1 - c):
                tiles.append((layer * 4 + chip(which, core)) * 2 + core)
        return jnp.stack(tiles).astype(jnp.int32)

    where = {
        "A": places(v, (0, 1)),
        "B": places(v, (2, 3)),
        "C": places(1 - v, (0, 1)),
        "D": places(1 - v, (2, 3)),
    }
    mine, peer = {}, {}
    parts = {}
    made = {}
    last, out = acts, None

    for step in ORDER:
        if step == "SA":
            mine["A"], last = stack(own, near, last)
            peer["A"] = swap(mine["A"], "c")
            mine["B"] = exchange(mine["A"], "x", 1)
            continue
        if step == "hV":
            other, last = hold(other, last)
            beyond = exchange(other, "x", 0)
            continue
        if step == "SC":
            mine["C"], last = stack(other, beyond, last)
            peer["C"] = swap(mine["C"], "c")
            mine["D"] = exchange(mine["C"], "x", 1)
            continue
        if step in ("hB", "hD"):
            name = step[1]
            mine[name], last = hold(mine[name], last)
            peer[name] = swap(mine[name], "c")
            continue
        name, stage = step[0], int(step[1])
        if stage == 7:
            out, last = place(out, *made[name], where[name], weights, last)
            continue
        if stage == 0:
            send, keep, last = fisher_parts(
                acts, mine[name], peer[name], weights, where[name], last
            )
            parts[name] = [(keep, 0)]
        elif stage < 4:
            rows, start = ((128, 0), (64, 128), (64, 192))[stage - 1]
            pairs = [(a, start - f) for a, f in parts[name]]
            send, last = add_up(pairs, rows, last, False)
        elif stage == 4:
            send, last = add_up(made[name], 64, last, True)
        else:
            send, last = join(made[name][0], made[name][1], last)
        axis, which = EXCHANGES[stage]
        came = exchange(send, axis, which)
        if stage == 0:
            parts[name].append((came, 0))
        elif stage < 3:
            parts[name].append((came, start + rows))
        elif stage == 3:
            made[name] = [(send, 0), (came, 0)]
        else:
            made[name] = [came, send]
    return out


def solution(mesh):
    fine = Mesh(mesh.devices.reshape(4, 4, 2, 4, 2), ("y", "w", "v", "x", "c"))
    mp, tp = ("y", "w"), ("v", "x", "c")
    in_specs = (P(mp, None, None, tp), P(mp, None, None, tp), P(mp, tp, None))
    return jax.shard_map(
        on_device, mesh=fine, in_specs=in_specs, out_specs=P(tp, None), check_vma=False
    )
```

time: 212 us -> 193 us (0.910)
  the two profiles are of different devices: /device:TPU:24 before, /device:TPU:32 now
where the time goes in v2:
time: 193 us; the launch traced here: 192 us
  waiting for transfers between devices  71.9 us (37%)
  starting transfers between devices  64.7 us (34%)
  Pallas kernels  41.7 us (22%)
  local copies, waits for them, and re-layouts  13.9 us (7%)
    ppermute x32, waiting for transfers between devices, exchange(): return lax.ppermute(value, (axis, 'c'), pairs)  71.9 us
    ppermute x32, starting transfers between devices, exchange(): return lax.ppermute(value, (axis, 'c'), pairs)  63.6 us
    pallas_call x4, Pallas kernels, fisher_parts(): pl.pallas_call(fisher_kernel, out_shape=[jax.ShapeDtypeStruct((2, ROWS //...  16.8 us
    unnamed x21, local copies, waits for them, and re-layouts  13.5 us
    pallas_call x16, Pallas kernels, add_up(): pl.pallas_call(merge_kernel if divide else add_kernel, out_shape=[jax.Sha...  11.6 us
    pallas_call x4, Pallas kernels, place(): pl.pallas_call(place_kernel, out_shape=[jax.ShapeDtypeStruct(weights.shap...  8.97 us
    pallas_call x2, Pallas kernels, stack(): pl.pallas_call(stack_kernel, out_shape=[jax.ShapeDtypeStruct((2, *a.shape...  4.16 us
  transfers between devices with their start and end apart: 37, of which 16 were waited for; matrix products, arithmetic and copies ran while one was open for 1% of the time, Pallas kernels for 19%

profile of v2, /device:TPU:32, one launch (start us, length us, event | category | flops | bytes accessed | tf_op | source)
XLA Modules:
  0.0 192.5 jit_solution(14822332489843023859)
XLA Ops:
  0.0 1.5 collective-permute-start.1
  1.5 1.5 copy.10
  3.0 6.4 %collective-permute-done.1.b = bf16[4,256,256]{2,1,0:T(8,128)(2,1)S(1)} collective-permute-done((bf16[4,256,256]{2,1,0:T(8,128)(2,1)}, bf16[4,256,256]{2,1,0:T(8,128)(2,1)S(1)}, u32[]{:S(2)}, u32[]{:S(2)}) %collective-permute-start.1) | collective-permute-done | bytes 524320 | tf_op jit(solution)/shard_map/ppermute | solution.py:52
  9.4 2.1 %stack.89 = (bf16[2,4,256,256]{3,2,1,0:T(8,128)(2,1)}, f32[8,128]{1,0:T(8,128)S(1)}) custom-call(bf16[4,256,256]{2,1,0:T(8,128)(2,1)} %bitcast.7.a, bf16[4,256,256]{2,1,0:T(8,128)(2,1)S(1)} %collective-permute-done.1.b, bf16[4,512,256]{2,1,0:T(8,128)(2,1)S(1)} %bitcast.26), custom_call_target="tpu_custom_call" | custom-call | flops 1 | bytes 1 | tf_op jit(solution)/shard_map/stack/pallas_call | solution.py:97
  11.5 2.8 %collective-permute-start.2 = (bf16[2,4,256,256]{3,2,1,0:T(8,128)(2,1)}, bf16[2,4,256,256]{3,2,1,0:T(8,128)(2,1)}, u32[]{:S(2)}, u32[]{:S(2)}) collective-permute-start(bf16[2,4,256,256]{3,2,1,0:T(8,128)(2,1)} %get-tuple-element.82.mine), channel_id=1, source_target_pairs={{0,6},{1,3},{2,4},{3,1},{4,2},{5,7},{6,0},{7,5},{8,14},{9,11},{10,... | collective-permute-start | bytes 3145736 | tf_op jit(solution)/shard_map/ppermute | solution.py:52
  14.4 2.2 %copy-done = bf16[1,512,4096]{2,1,0:T(8,128)(2,1)S(1)} copy-done((bf16[1,512,4096]{2,1,0:T(8,128)(2,1)S(1)}, bf16[1,512,4096]{2,1,0:T(8,128)(2,1)}, u32[]{:S(2)}) %copy-start) | copy-done | bytes 4194328
  16.6 3.5 %fisher_parts.4 = (bf16[2,256,1024]{2,1,0:T(8,128)(2,1)S(1)}, bf16[2,256,1024]{2,1,0:T(8,128)(2,1)S(1)}, f32[8,128]{1,0:T(8,128)S(1)}) custom-call(s32[5]{0:T(128)S(1)} %stack.78.where, bf16[4,512,256]{2,1,0:T(8,128)(2,1)S(1)} %bitcast.27, bf16[2,4,256,256]{3,2,1,0:T(8,128)(2,1)} %get-tuple-element.82.mine, ...), custom_call_target="tpu_custom_call" | custom-call | flops 1 | bytes 1 | tf_op jit(solution)/shard_map/fisher_parts/pallas_call | solution.py:142
  20.1 1.7 collective-permute-start.6
  21.8 6.0 %collective-permute-done.2.value = bf16[2,4,256,256]{3,2,1,0:T(8,128)(2,1)} collective-permute-done((bf16[2,4,256,256]{3,2,1,0:T(8,128)(2,1)}, bf16[2,4,256,256]{3,2,1,0:T(8,128)(2,1)}, u32[]{:S(2)}, u32[]{:S(2)}) %collective-permute-start.2) | collective-permute-done | bytes 1048608 | tf_op jit(solution)/shard_map/ppermute | solution.py:52
  29.0 8.2 %collective-permute-done.4.b = bf16[4,256,256]{2,1,0:T(8,128)(2,1)S(1)} collective-permute-done((bf16[4,256,256]{2,1,0:T(8,128)(2,1)}, bf16[4,256,256]{2,1,0:T(8,128)(2,1)S(1)}, u32[]{:S(2)}, u32[]{:S(2)}) %collective-permute-start.4) | collective-permute-done | bytes 524320 | tf_op jit(solution)/shard_map/ppermute | solution.py:52
  37.2 2.1 %stack.90 = (bf16[2,4,256,256]{3,2,1,0:T(8,128)(2,1)}, f32[8,128]{1,0:T(8,128)S(1)}) custom-call(bf16[4,256,256]{2,1,0:T(8,128)(2,1)} %get-tuple-element.86.a, bf16[4,256,256]{2,1,0:T(8,128)(2,1)S(1)} %collective-permute-done.4.b, f32[8,128]{1,0:T(8,128)S(1)} %get-tuple-element.87.after), custom_call_target="tpu_custom_call" | custom-call | flops 1 | bytes 1 | tf_op jit(solution)/shard_map/stack/pallas_call | solution.py:97
  39.3 2.8 %collective-permute-start.5 = (bf16[2,4,256,256]{3,2,1,0:T(8,128)(2,1)}, bf16[2,4,256,256]{3,2,1,0:T(8,128)(2,1)}, u32[]{:S(2)}, u32[]{:S(2)}) collective-permute-start(bf16[2,4,256,256]{3,2,1,0:T(8,128)(2,1)} %get-tuple-element.88.mine), channel_id=1, source_target_pairs={{0,6},{1,3},{2,4},{3,1},{4,2},{5,7},{6,0},{7,5},{8,14},{9,11},{10,... | collective-permute-start | bytes 3145736 | tf_op jit(solution)/shard_map/ppermute | solution.py:52
  43.0 3.0 %collective-permute-start.7 = (bf16[2,128,1024]{2,1,0:T(8,128)(2,1)}, bf16[2,128,1024]{2,1,0:T(8,128)(2,1)}, u32[]{:S(2)}, u32[]{:S(2)}) collective-permute-start(bf16[2,128,1024]{2,1,0:T(8,128)(2,1)} %get-tuple-element.92), channel_id=1, source_target_pairs={{0,192},{1,65},{64,128},{65,1},{128,64},{129,193},{192,0},{193,129... | collective-permute-start | bytes 1572872 | tf_op jit(solution)/shard_map/ppermute | solution.py:52
  46.1 2.2 %copy-done.1 = bf16[1,512,4096]{2,1,0:T(8,128)(2,1)S(1)} copy-done((bf16[1,512,4096]{2,1,0:T(8,128)(2,1)S(1)}, bf16[1,512,4096]{2,1,0:T(8,128)(2,1)}, u32[]{:S(2)}) %copy-start.1) | copy-done | bytes 4194328
  48.3 4.7 %fisher_parts.5 = (bf16[2,256,1024]{2,1,0:T(8,128)(2,1)}, bf16[2,256,1024]{2,1,0:T(8,128)(2,1)S(1)}, f32[8,128]{1,0:T(8,128)S(1)}) custom-call(s32[5]{0:T(128)S(1)} %stack.83.where, bf16[4,512,256]{2,1,0:T(8,128)(2,1)S(1)} %bitcast.28, bf16[2,4,256,256]{3,2,1,0:T(8,128)(2,1)} %get-tuple-element.93.mine, ...), custom_call_target="tpu_custom_call" | custom-call | flops 1 | bytes 1 | tf_op jit(solution)/shard_map/fisher_parts/pallas_call | solution.py:142
  55.9 3.3 %collective-permute-start.10 = (bf16[2,64,1024]{2,1,0:T(8,128)(2,1)}, bf16[2,64,1024]{2,1,0:T(8,128)(2,1)S(1)}, u32[]{:S(2)}, u32[]{:S(2)}) collective-permute-start(bf16[2,64,1024]{2,1,0:T(8,128)(2,1)} %copy-done.9), channel_id=1, source_target_pairs={{0,16},{1,49},{16,0},{17,33},{32,48},{33,17},{48,32},{49,1},{2,18}... | collective-permute-start | bytes 786440 | tf_op jit(solution)/shard_map/ppermute | solution.py:52
  59.3 2.2 %copy-done.2 = bf16[1,512,4096]{2,1,0:T(8,128)(2,1)S(1)} copy-done((bf16[1,512,4096]{2,1,0:T(8,128)(2,1)S(1)}, bf16[1,512,4096]{2,1,0:T(8,128)(2,1)}, u32[]{:S(2)}) %copy-start.2) | copy-done | bytes 4194328
  61.5 4.8 %fisher_parts.6 = (bf16[2,256,1024]{2,1,0:T(8,128)(2,1)}, bf16[2,256,1024]{2,1,0:T(8,128)(2,1)S(1)}, f32[8,128]{1,0:T(8,128)S(1)}) custom-call(s32[5]{0:T(128)S(1)} %stack.88.where, bf16[4,512,256]{2,1,0:T(8,128)(2,1)S(1)} %bitcast.29, bf16[2,4,256,256]{3,2,1,0:T(8,128)(2,1)} %get-tuple-element.88.mine, ...), custom_call_target="tpu_custom_call" | custom-call | flops 1 | bytes 1 | tf_op jit(solution)/shard_map/fisher_parts/pallas_call | solution.py:142
  67.2 1.8 collective-permute-start.14
  69.1 1.2 copy-done.7
  70.3 2.0 %add_up.14 = (bf16[2,128,1024]{2,1,0:T(8,128)(2,1)}, f32[8,128]{1,0:T(8,128)S(1)}) custom-call(bf16[2,256,1024]{2,1,0:T(8,128)(2,1)S(1)} %copy-done.7, bf16[2,256,1024]{2,1,0:T(8,128)(2,1)} %collective-permute-done.11.refs_1_, f32[8,128]{1,0:T(8,128)S(1)} %get-tuple-element.102.refs_2_), custom_call_target="tpu_custom_call" | custom-call | flops 1 | bytes 1 | tf_op jit(solution)/shard_map/add_up/pallas_call | solution.py:187
  72.4 1.8 collective-permute-start.15
  75.5 2.2 %copy-done.3 = bf16[1,512,4096]{2,1,0:T(8,128)(2,1)S(1)} copy-done((bf16[1,512,4096]{2,1,0:T(8,128)(2,1)S(1)}, bf16[1,512,4096]{2,1,0:T(8,128)(2,1)}, u32[]{:S(2)}) %copy-start.3) | copy-done | bytes 4194328
  77.6 3.8 %fisher_parts.7 = (bf16[2,256,1024]{2,1,0:T(8,128)(2,1)S(1)}, bf16[2,256,1024]{2,1,0:T(8,128)(2,1)S(1)}, f32[8,128]{1,0:T(8,128)S(1)}) custom-call(s32[5]{0:T(128)S(1)} %stack.73.where, bf16[4,512,256]{2,1,0:T(8,128)(2,1)S(1)} %bitcast.30, bf16[2,4,256,256]{3,2,1,0:T(8,128)(2,1)} %get-tuple-element.97.mine, ...), custom_call_target="tpu_custom_call" | custom-call | flops 1 | bytes 1 | tf_op jit(solution)/shard_map/fisher_parts/pallas_call | solution.py:142
  82.2 3.6 %collective-permute-start.17 = (bf16[2,64,1024]{2,1,0:T(8,128)(2,1)S(1)}, bf16[2,64,1024]{2,1,0:T(8,128)(2,1)S(1)}, u32[]{:S(2)}, u32[]{:S(2)}) collective-permute-start(bf16[2,64,1024]{2,1,0:T(8,128)(2,1)S(1)} %get-tuple-element.112.refs_0_), channel_id=1, source_target_pairs={{0,48},{1,17},{16,32},{17,1},{32,16},{33,49},{48,0},{49,33},{2,50}... | collective-permute-start | bytes 786440 | tf_op jit(solution)/shard_map/ppermute | solution.py:52
  85.8 2.9 %collective-permute-done.15.refs_2_ = bf16[2,128,1024]{2,1,0:T(8,128)(2,1)} collective-permute-done((bf16[2,128,1024]{2,1,0:T(8,128)(2,1)}, bf16[2,128,1024]{2,1,0:T(8,128)(2,1)}, u32[]{:S(2)}, u32[]{:S(2)}) %collective-permute-start.15) | collective-permute-done | bytes 524320 | tf_op jit(solution)/shard_map/ppermute | solution.py:52
  89.9 3.4 %collective-permute-start.16 = (bf16[2,64,1024]{2,1,0:T(8,128)(2,1)S(1)}, bf16[2,64,1024]{2,1,0:T(8,128)(2,1)S(1)}, u32[]{:S(2)}, u32[]{:S(2)}) collective-permute-start(bf16[2,64,1024]{2,1,0:T(8,128)(2,1)S(1)} %get-tuple-element.111), channel_id=1, source_target_pairs={{0,16},{1,49},{16,0},{17,33},{32,48},{33,17},{48,32},{49,1},{2,18}... | collective-permute-start | bytes 786440 | tf_op jit(solution)/shard_map/ppermute | solution.py:52
  93.5 6.0 %collective-permute-done.16.refs_3_ = bf16[2,64,1024]{2,1,0:T(8,128)(2,1)S(1)} collective-permute-done((bf16[2,64,1024]{2,1,0:T(8,128)(2,1)S(1)}, bf16[2,64,1024]{2,1,0:T(8,128)(2,1)S(1)}, u32[]{:S(2)}, u32[]{:S(2)}) %collective-permute-start.16) | collective-permute-done | bytes 262176 | tf_op jit(solution)/shard_map/ppermute | solution.py:52
  101.9 2.3 %collective-permute-start.21 = (bf16[2,128,1024]{2,1,0:T(8,128)(2,1)S(1)}, bf16[2,128,1024]{2,1,0:T(8,128)(2,1)S(1)}, u32[]{:S(2)}, u32[]{:S(2)}) collective-permute-start(bf16[2,128,1024]{2,1,0:T(8,128)(2,1)S(1)} %get-tuple-element.120), channel_id=1, source_target_pairs={{0,192},{1,65},{64,128},{65,1},{128,64},{129,193},{192,0},{193,129... | collective-permute-start | bytes 1572872 | tf_op jit(solution)/shard_map/ppermute | solution.py:52
  105.4 5.8 %collective-permute-start.20 = (bf16[2,64,1024]{2,1,0:T(8,128)(2,1)S(1)}, bf16[2,64,1024]{2,1,0:T(8,128)(2,1)S(1)}, u32[]{:S(2)}, u32[]{:S(2)}) collective-permute-start(bf16[2,64,1024]{2,1,0:T(8,128)(2,1)S(1)} %get-tuple-element.119.refs_0_), channel_id=1, source_target_pairs={{0,48},{1,17},{16,32},{17,1},{32,16},{33,49},{48,0},{49,33},{2,50}... | collective-permute-start | bytes 786440 | tf_op jit(solution)/shard_map/ppermute | solution.py:52
  113.5 3.4 %collective-permute-start.24 = (bf16[2,64,1024]{2,1,0:T(8,128)(2,1)S(1)}, bf16[2,64,1024]{2,1,0:T(8,128)(2,1)S(1)}, u32[]{:S(2)}, u32[]{:S(2)}) collective-permute-start(bf16[2,64,1024]{2,1,0:T(8,128)(2,1)S(1)} %get-tuple-element.127), channel_id=1, source_target_pairs={{0,16},{1,49},{16,0},{17,33},{32,48},{33,17},{48,32},{49,1},{2,18}... | collective-permute-start | bytes 786440 | tf_op jit(solution)/shard_map/ppermute | solution.py:52
  116.9 5.8 %collective-permute-done.20.refs_1_ = bf16[2,64,1024]{2,1,0:T(8,128)(2,1)S(1)} collective-permute-done((bf16[2,64,1024]{2,1,0:T(8,128)(2,1)S(1)}, bf16[2,64,1024]{2,1,0:T(8,128)(2,1)S(1)}, u32[]{:S(2)}, u32[]{:S(2)}) %collective-permute-start.20) | collective-permute-done | bytes 262176 | tf_op jit(solution)/shard_map/ppermute | solution.py:52
  126.3 4.2 %collective-permute-done.23.a = bf16[128,1024]{1,0:T(8,128)(2,1)S(1)} collective-permute-done((bf16[128,1024]{1,0:T(8,128)(2,1)S(1)}, bf16[128,1024]{1,0:T(8,128)(2,1)S(1)}, u32[]{:S(2)}, u32[]{:S(2)}) %collective-permute-start.23) | collective-permute-done | bytes 262176 | tf_op jit(solution)/shard_map/ppermute | solution.py:52
  130.7 3.5 %collective-permute-start.26 = (bf16[64,1024]{1,0:T(8,128)(2,1)S(1)}, bf16[64,1024]{1,0:T(8,128)(2,1)S(1)}, u32[]{:S(2)}, u32[]{:S(2)}) collective-permute-start(bf16[64,1024]{1,0:T(8,128)(2,1)S(1)} %get-tuple-element.132.b), channel_id=1, source_target_pairs={{0,16},{1,49},{16,0},{17,33},{32,48},{33,17},{48,32},{49,1},{2,18}... | collective-permute-start | bytes 393224 | tf_op jit(solution)/shard_map/ppermute | solution.py:52
  134.2 5.2 %collective-permute-start.29 = (bf16[2,64,1024]{2,1,0:T(8,128)(2,1)S(1)}, bf16[2,64,1024]{2,1,0:T(8,128)(2,1)S(1)}, u32[]{:S(2)}, u32[]{:S(2)}) collective-permute-start(bf16[2,64,1024]{2,1,0:T(8,128)(2,1)S(1)} %get-tuple-element.136.refs_0_), channel_id=1, source_target_pairs={{0,48},{1,17},{16,32},{17,1},{32,16},{33,49},{48,0},{49,33},{2,50}... | collective-permute-start | bytes 786440 | tf_op jit(solution)/shard_map/ppermute | solution.py:52
  139.5 3.5 %collective-permute-done.26.a = bf16[64,1024]{1,0:T(8,128)(2,1)S(1)} collective-permute-done((bf16[64,1024]{1,0:T(8,128)(2,1)S(1)}, bf16[64,1024]{1,0:T(8,128)(2,1)S(1)}, u32[]{:S(2)}, u32[]{:S(2)}) %collective-permute-start.26) | collective-permute-done | bytes 131104 | tf_op jit(solution)/shard_map/ppermute | solution.py:52
  143.1 1.7 collective-permute-start.27
  144.8 7.1 %collective-permute-start.25 = (bf16[2,64,1024]{2,1,0:T(8,128)(2,1)S(1)}, bf16[2,64,1024]{2,1,0:T(8,128)(2,1)S(1)}, u32[]{:S(2)}, u32[]{:S(2)}) collective-permute-start(bf16[2,64,1024]{2,1,0:T(8,128)(2,1)S(1)} %get-tuple-element.131.refs_0_), channel_id=1, source_target_pairs={{0,48},{1,17},{16,32},{17,1},{32,16},{33,49},{48,0},{49,33},{2,50}... | collective-permute-start | bytes 786440 | tf_op jit(solution)/shard_map/ppermute | solution.py:52
  152.0 2.2 %place.4 = (bf16[512,4096]{1,0:T(8,128)(2,1)}, f32[8,128]{1,0:T(8,128)S(1)}) custom-call(s32[5]{0:T(128)S(1)} %stack.78.where, bf16[256,1024]{1,0:T(8,128)(2,1)S(1)} %collective-permute-done.28.far, bf16[256,1024]{1,0:T(8,128)(2,1)S(1)} %get-tuple-element.135.near, f32[8,128]{1,0:T(8,128)S(1)} %get-tuple-element.138.refs_0_), custom_call_target="tpu_custom_call" | custom-call | flops 1 | bytes 1 | tf_op jit(solution)/shard_map/place/pallas_call | solution.py:228
  154.3 1.2 collective-permute-start.31
  155.6 8.8 %collective-permute-done.25.refs_1_ = bf16[2,64,1024]{2,1,0:T(8,128)(2,1)S(1)} collective-permute-done((bf16[2,64,1024]{2,1,0:T(8,128)(2,1)S(1)}, bf16[2,64,1024]{2,1,0:T(8,128)(2,1)S(1)}, u32[]{:S(2)}, u32[]{:S(2)}) %collective-permute-start.25) | collective-permute-done | bytes 262176 | tf_op jit(solution)/shard_map/ppermute | solution.py:52
  165.4 5.0 %collective-permute-done.30.a = bf16[64,1024]{1,0:T(8,128)(2,1)S(1)} collective-permute-done((bf16[64,1024]{1,0:T(8,128)(2,1)S(1)}, bf16[64,1024]{1,0:T(8,128)(2,1)S(1)}, u32[]{:S(2)}, u32[]{:S(2)}) %collective-permute-start.30) | collective-permute-done | bytes 131104 | tf_op jit(solution)/shard_map/ppermute | solution.py:52
  171.2 1.7 collective-permute-done.34.a
  173.1 2.2 %place.5 = (bf16[512,4096]{1,0:T(8,128)(2,1)}, f32[8,128]{1,0:T(8,128)S(1)}) custom-call(s32[5]{0:T(128)S(1)} %stack.83.where, bf16[256,1024]{1,0:T(8,128)(2,1)S(1)} %collective-permute-done.33.far, bf16[256,1024]{1,0:T(8,128)(2,1)S(1)} %get-tuple-element.146.near, f32[8,128]{1,0:T(8,128)S(1)} %get-tuple-element.149.refs_0_, ...), custom_call_target="tpu_custom_call", output_to_operand_aliasing={{0}: (4, {})} | custom-call | flops 1 | bytes 1 | tf_op jit(solution)/shard_map/place/pallas_call | solution.py:228
  175.3 5.6 %collective-permute-done.32.a = bf16[128,1024]{1,0:T(8,128)(2,1)S(1)} collective-permute-done((bf16[128,1024]{1,0:T(8,128)(2,1)S(1)}, bf16[128,1024]{1,0:T(8,128)(2,1)S(1)}, u32[]{:S(2)}, u32[]{:S(2)}) %collective-permute-start.32) | collective-permute-done | bytes 262176 | tf_op jit(solution)/shard_map/ppermute | solution.py:52
  182.2 2.2 %place.6 = (bf16[512,4096]{1,0:T(8,128)(2,1)}, f32[8,128]{1,0:T(8,128)S(1)}) custom-call(s32[5]{0:T(128)S(1)} %stack.88.where, bf16[256,1024]{1,0:T(8,128)(2,1)S(1)} %collective-permute-done.36.far, bf16[256,1024]{1,0:T(8,128)(2,1)S(1)} %get-tuple-element.153.near, f32[8,128]{1,0:T(8,128)S(1)} %get-tuple-element.154.refs_0_, ...), custom_call_target="tpu_custom_call", output_to_operand_aliasing={{0}: (4, {})} | custom-call | flops 1 | bytes 1 | tf_op jit(solution)/shard_map/place/pallas_call | solution.py:228
  184.5 5.8 %collective-permute-done.35.far = bf16[256,1024]{1,0:T(8,128)(2,1)S(1)} collective-permute-done((bf16[256,1024]{1,0:T(8,128)(2,1)S(1)}, bf16[256,1024]{1,0:T(8,128)(2,1)S(1)}, u32[]{:S(2)}, u32[]{:S(2)}) %collective-permute-start.35) | collective-permute-done | bytes 524320 | tf_op jit(solution)/shard_map/ppermute | solution.py:52
  190.2 2.2 %place.7 = (bf16[512,4096]{1,0:T(8,128)(2,1)}, f32[8,128]{1,0:T(8,128)}) custom-call(s32[5]{0:T(128)S(1)} %stack.73.where, bf16[256,1024]{1,0:T(8,128)(2,1)S(1)} %collective-permute-done.35.far, bf16[256,1024]{1,0:T(8,128)(2,1)S(1)} %get-tuple-element.152.near, f32[8,128]{1,0:T(8,128)S(1)} %get-tuple-element.156.refs_0_, ...), custom_call_target="tpu_custom_call", output_to_operand_aliasing={{0}: (4, {})} | custom-call | flops 1 | bytes 1 | tf_op jit(solution)/shard_map/place/pallas_call | solution.py:228
  (88 shorter events, 22.9 us)
Async XLA Ops:
  0.0 9.4 %collective-permute-start.1 = (bf16[4,256,256]{2,1,0:T(8,128)(2,1)}, bf16[4,256,256]{2,1,0:T(8,128)(2,1)S(1)}, u32[]{:S(2)}, u32[]{:S(2)}) collective-permute-start(bf16[4,256,256]{2,1,0:T(8,128)(2,1)} %bitcast.7.a), channel_id=1, source_target_pairs={{0,2},{1,7},{2,0},{3,5},{4,6},{5,3},{6,4},{7,1},{8,10},{9,15},{10,... | collective-permute-start | bytes 1572872 | tf_op jit(solution)/shard_map/ppermute | solution.py:52
  11.5 3.0 %collective-permute-start.3 = (bf16[2,4,256,256]{3,2,1,0:T(8,128)(2,1)}, bf16[2,4,256,256]{3,2,1,0:T(8,128)(2,1)S(1)}, u32[]{:S(2)}, u32[]{:S(2)}) collective-permute-start(bf16[2,4,256,256]{3,2,1,0:T(8,128)(2,1)} %get-tuple-element.82.mine), channel_id=1, source_target_pairs={{0,1},{1,0},{2,3},{3,2},{4,5},{5,4},{6,7},{7,6},{8,9},{9,8},{10,11... | collective-permute-start | bytes 3145736 | tf_op jit(solution)/shard_map/ppermute | solution.py:56
  11.5 16.3 %collective-permute-start.2 = (bf16[2,4,256,256]{3,2,1,0:T(8,128)(2,1)}, bf16[2,4,256,256]{3,2,1,0:T(8,128)(2,1)}, u32[]{:S(2)}, u32[]{:S(2)}) collective-permute-start(bf16[2,4,256,256]{3,2,1,0:T(8,128)(2,1)} %get-tuple-element.82.mine), channel_id=1, source_target_pairs={{0,6},{1,3},{2,4},{3,1},{4,2},{5,7},{6,0},{7,5},{8,14},{9,11},{10,... | collective-permute-start | bytes 3145736 | tf_op jit(solution)/shard_map/ppermute | solution.py:52
  14.2 13.6 %collective-permute-start = (bf16[4,256,256]{2,1,0:T(8,128)(2,1)}, bf16[4,256,256]{2,1,0:T(8,128)(2,1)}, u32[]{:S(2)}, u32[]{:S(2)}) collective-permute-start(bf16[4,256,256]{2,1,0:T(8,128)(2,1)} %bitcast.7.a), channel_id=1, source_target_pairs={{0,8},{8,0},{1,9},{9,1},{2,10},{10,2},{3,11},{11,3},{4,12},{12,4},... | collective-permute-start | bytes 1572872 | tf_op jit(solution)/shard_map/ppermute | solution.py:56
  14.4 2.2 %copy-start = (bf16[1,512,4096]{2,1,0:T(8,128)(2,1)S(1)}, bf16[1,512,4096]{2,1,0:T(8,128)(2,1)}, u32[]{:S(2)}) copy-start(bf16[1,512,4096]{2,1,0:T(8,128)(2,1)} %param.5) | copy-start | bytes 12582916
  20.1 21.9 %collective-permute-start.6 = (bf16[2,256,1024]{2,1,0:T(8,128)(2,1)S(1)}, bf16[2,256,1024]{2,1,0:T(8,128)(2,1)S(1)}, u32[]{:S(2)}, u32[]{:S(2)}) collective-permute-start(bf16[2,256,1024]{2,1,0:T(8,128)(2,1)S(1)} %get-tuple-element.90), channel_id=1, source_target_pairs={{0,64},{1,193},{64,0},{65,129},{128,192},{129,65},{192,128},{193,1... | collective-permute-start | bytes 3145736 | tf_op jit(solution)/shard_map/ppermute | solution.py:52
  27.8 9.4 %collective-permute-start.4 = (bf16[4,256,256]{2,1,0:T(8,128)(2,1)}, bf16[4,256,256]{2,1,0:T(8,128)(2,1)S(1)}, u32[]{:S(2)}, u32[]{:S(2)}) collective-permute-start(bf16[4,256,256]{2,1,0:T(8,128)(2,1)} %get-tuple-element.86.a), channel_id=1, source_target_pairs={{0,2},{1,7},{2,0},{3,5},{4,6},{5,3},{6,4},{7,1},{8,10},{9,15},{10,... | collective-permute-start | bytes 1572872 | tf_op jit(solution)/shard_map/ppermute | solution.py:52
  28.1 18.0 %collective-permute-start.8 = (bf16[2,4,256,256]{3,2,1,0:T(8,128)(2,1)}, bf16[2,4,256,256]{3,2,1,0:T(8,128)(2,1)}, u32[]{:S(2)}, u32[]{:S(2)}) collective-permute-start(bf16[2,4,256,256]{3,2,1,0:T(8,128)(2,1)} %get-tuple-element.93.mine), channel_id=1, source_target_pairs={{0,1},{1,0},{2,3},{3,2},{4,5},{5,4},{6,7},{7,6},{8,9},{9,8},{10,11... | collective-permute-start | bytes 3145736 | tf_op jit(solution)/shard_map/ppermute | solution.py:56
  39.3 16.3 %collective-permute-start.5 = (bf16[2,4,256,256]{3,2,1,0:T(8,128)(2,1)}, bf16[2,4,256,256]{3,2,1,0:T(8,128)(2,1)}, u32[]{:S(2)}, u32[]{:S(2)}) collective-permute-start(bf16[2,4,256,256]{3,2,1,0:T(8,128)(2,1)} %get-tuple-element.88.mine), channel_id=1, source_target_pairs={{0,6},{1,3},{2,4},{3,1},{4,2},{5,7},{6,0},{7,5},{8,14},{9,11},{10,... | collective-permute-start | bytes 3145736 | tf_op jit(solution)/shard_map/ppermute | solution.py:52
  43.0 11.2 %collective-permute-start.7 = (bf16[2,128,1024]{2,1,0:T(8,128)(2,1)}, bf16[2,128,1024]{2,1,0:T(8,128)(2,1)}, u32[]{:S(2)}, u32[]{:S(2)}) collective-permute-start(bf16[2,128,1024]{2,1,0:T(8,128)(2,1)} %get-tuple-element.92), channel_id=1, source_target_pairs={{0,192},{1,65},{64,128},{65,1},{128,64},{129,193},{192,0},{193,129... | collective-permute-start | bytes 1572872 | tf_op jit(solution)/shard_map/ppermute | solution.py:52
  46.0 13.3 %collective-permute-start.12 = (bf16[2,4,256,256]{3,2,1,0:T(8,128)(2,1)}, bf16[2,4,256,256]{3,2,1,0:T(8,128)(2,1)}, u32[]{:S(2)}, u32[]{:S(2)}) collective-permute-start(bf16[2,4,256,256]{3,2,1,0:T(8,128)(2,1)} %get-tuple-element.88.mine), channel_id=1, source_target_pairs={{0,1},{1,0},{2,3},{3,2},{4,5},{5,4},{6,7},{7,6},{8,9},{9,8},{10,11... | collective-permute-start | bytes 3145736 | tf_op jit(solution)/shard_map/ppermute | solution.py:56
  46.1 2.2 %copy-start.1 = (bf16[1,512,4096]{2,1,0:T(8,128)(2,1)S(1)}, bf16[1,512,4096]{2,1,0:T(8,128)(2,1)}, u32[]{:S(2)}) copy-start(bf16[1,512,4096]{2,1,0:T(8,128)(2,1)} %param.5) | copy-start | bytes 12582916
  53.0 1.0 copy-start.6
  54.0 15.1 %collective-permute-start.11 = (bf16[2,256,1024]{2,1,0:T(8,128)(2,1)}, bf16[2,256,1024]{2,1,0:T(8,128)(2,1)}, u32[]{:S(2)}, u32[]{:S(2)}) collective-permute-start(bf16[2,256,1024]{2,1,0:T(8,128)(2,1)} %get-tuple-element.100), channel_id=1, source_target_pairs={{0,64},{1,193},{64,0},{65,129},{128,192},{129,65},{192,128},{193,1... | collective-permute-start | bytes 3145736 | tf_op jit(solution)/shard_map/ppermute | solution.py:52
  55.2 0.7 copy-start.9
  55.6 19.8 %collective-permute-start.9 = (bf16[2,4,256,256]{3,2,1,0:T(8,128)(2,1)}, bf16[2,4,256,256]{3,2,1,0:T(8,128)(2,1)}, u32[]{:S(2)}, u32[]{:S(2)}) collective-permute-start(bf16[2,4,256,256]{3,2,1,0:T(8,128)(2,1)} %get-tuple-element.97.mine), channel_id=1, source_target_pairs={{0,1},{1,0},{2,3},{3,2},{4,5},{5,4},{6,7},{7,6},{8,9},{9,8},{10,11... | collective-permute-start | bytes 3145736 | tf_op jit(solution)/shard_map/ppermute | solution.py:56
  55.9 18.3 %collective-permute-start.10 = (bf16[2,64,1024]{2,1,0:T(8,128)(2,1)}, bf16[2,64,1024]{2,1,0:T(8,128)(2,1)S(1)}, u32[]{:S(2)}, u32[]{:S(2)}) collective-permute-start(bf16[2,64,1024]{2,1,0:T(8,128)(2,1)} %copy-done.9), channel_id=1, source_target_pairs={{0,16},{1,49},{16,0},{17,33},{32,48},{33,17},{48,32},{49,1},{2,18}... | collective-permute-start | bytes 786440 | tf_op jit(solution)/shard_map/ppermute | solution.py:52
  59.3 2.2 %copy-start.2 = (bf16[1,512,4096]{2,1,0:T(8,128)(2,1)S(1)}, bf16[1,512,4096]{2,1,0:T(8,128)(2,1)}, u32[]{:S(2)}) copy-start(bf16[1,512,4096]{2,1,0:T(8,128)(2,1)} %param.5) | copy-start | bytes 12582916
  66.3 1.0 copy-start.4
  67.2 33.4 %collective-permute-start.14 = (bf16[2,256,1024]{2,1,0:T(8,128)(2,1)}, bf16[2,256,1024]{2,1,0:T(8,128)(2,1)}, u32[]{:S(2)}, u32[]{:S(2)}) collective-permute-start(bf16[2,256,1024]{2,1,0:T(8,128)(2,1)} %get-tuple-element.108), channel_id=1, source_target_pairs={{0,64},{1,193},{64,0},{65,129},{128,192},{129,65},{192,128},{193,1... | collective-permute-start | bytes 3145736 | tf_op jit(solution)/shard_map/ppermute | solution.py:52
  69.1 1.2 copy-start.7
  72.4 16.4 %collective-permute-start.15 = (bf16[2,128,1024]{2,1,0:T(8,128)(2,1)}, bf16[2,128,1024]{2,1,0:T(8,128)(2,1)}, u32[]{:S(2)}, u32[]{:S(2)}) collective-permute-start(bf16[2,128,1024]{2,1,0:T(8,128)(2,1)} %get-tuple-element.109), channel_id=1, source_target_pairs={{0,192},{1,65},{64,128},{65,1},{128,64},{129,193},{192,0},{193,129... | collective-permute-start | bytes 1572872 | tf_op jit(solution)/shard_map/ppermute | solution.py:52
  74.2 14.5 %copy-start.8 = (bf16[2,256,1024]{2,1,0:T(8,128)(2,1)S(1)}, bf16[2,256,1024]{2,1,0:T(8,128)(2,1)}, u32[]{:S(2)}) copy-start(bf16[2,256,1024]{2,1,0:T(8,128)(2,1)} %copy-done.6) | copy-start | bytes 3145732
  75.5 2.2 %copy-start.3 = (bf16[1,512,4096]{2,1,0:T(8,128)(2,1)S(1)}, bf16[1,512,4096]{2,1,0:T(8,128)(2,1)}, u32[]{:S(2)}) copy-start(bf16[1,512,4096]{2,1,0:T(8,128)(2,1)} %param.5) | copy-start | bytes 12582916
  81.4 19.3 %copy-start.5 = (bf16[2,256,1024]{2,1,0:T(8,128)(2,1)S(1)}, bf16[2,256,1024]{2,1,0:T(8,128)(2,1)}, u32[]{:S(2)}) copy-start(bf16[2,256,1024]{2,1,0:T(8,128)(2,1)} %copy-done.4) | copy-start | bytes 3145732
  81.4 22.8 %collective-permute-start.13 = (bf16[2,256,1024]{2,1,0:T(8,128)(2,1)S(1)}, bf16[2,256,1024]{2,1,0:T(8,128)(2,1)S(1)}, u32[]{:S(2)}, u32[]{:S(2)}) collective-permute-start(bf16[2,256,1024]{2,1,0:T(8,128)(2,1)S(1)} %get-tuple-element.106), channel_id=1, source_target_pairs={{0,64},{1,193},{64,0},{65,129},{128,192},{129,65},{192,128},{193,1... | collective-permute-start | bytes 3145736 | tf_op jit(solution)/shard_map/ppermute | solution.py:52
  82.2 11.2 %collective-permute-start.17 = (bf16[2,64,1024]{2,1,0:T(8,128)(2,1)S(1)}, bf16[2,64,1024]{2,1,0:T(8,128)(2,1)S(1)}, u32[]{:S(2)}, u32[]{:S(2)}) collective-permute-start(bf16[2,64,1024]{2,1,0:T(8,128)(2,1)S(1)} %get-tuple-element.112.refs_0_), channel_id=1, source_target_pairs={{0,48},{1,17},{16,32},{17,1},{32,16},{33,49},{48,0},{49,33},{2,50}... | collective-permute-start | bytes 786440 | tf_op jit(solution)/shard_map/ppermute | solution.py:52
  89.9 9.6 %collective-permute-start.16 = (bf16[2,64,1024]{2,1,0:T(8,128)(2,1)S(1)}, bf16[2,64,1024]{2,1,0:T(8,128)(2,1)S(1)}, u32[]{:S(2)}, u32[]{:S(2)}) collective-permute-start(bf16[2,64,1024]{2,1,0:T(8,128)(2,1)S(1)} %get-tuple-element.111), channel_id=1, source_target_pairs={{0,16},{1,49},{16,0},{17,33},{32,48},{33,17},{48,32},{49,1},{2,18}... | collective-permute-start | bytes 786440 | tf_op jit(solution)/shard_map/ppermute | solution.py:52
  101.9 10.5 %collective-permute-start.21 = (bf16[2,128,1024]{2,1,0:T(8,128)(2,1)S(1)}, bf16[2,128,1024]{2,1,0:T(8,128)(2,1)S(1)}, u32[]{:S(2)}, u32[]{:S(2)}) collective-permute-start(bf16[2,128,1024]{2,1,0:T(8,128)(2,1)S(1)} %get-tuple-element.120), channel_id=1, source_target_pairs={{0,192},{1,65},{64,128},{65,1},{128,64},{129,193},{192,0},{193,129... | collective-permute-start | bytes 1572872 | tf_op jit(solution)/shard_map/ppermute | solution.py:52
  104.3 19.6 %collective-permute-start.18 = (bf16[2,128,1024]{2,1,0:T(8,128)(2,1)S(1)}, bf16[2,128,1024]{2,1,0:T(8,128)(2,1)S(1)}, u32[]{:S(2)}, u32[]{:S(2)}) collective-permute-start(bf16[2,128,1024]{2,1,0:T(8,128)(2,1)S(1)} %get-tuple-element.117), channel_id=1, source_target_pairs={{0,192},{1,65},{64,128},{65,1},{128,64},{129,193},{192,0},{193,129... | collective-permute-start | bytes 1572872 | tf_op jit(solution)/shard_map/ppermute | solution.py:52
  105.4 17.3 %collective-permute-start.20 = (bf16[2,64,1024]{2,1,0:T(8,128)(2,1)S(1)}, bf16[2,64,1024]{2,1,0:T(8,128)(2,1)S(1)}, u32[]{:S(2)}, u32[]{:S(2)}) collective-permute-start(bf16[2,64,1024]{2,1,0:T(8,128)(2,1)S(1)} %get-tuple-element.119.refs_0_), channel_id=1, source_target_pairs={{0,48},{1,17},{16,32},{17,1},{32,16},{33,49},{48,0},{49,33},{2,50}... | collective-permute-start | bytes 786440 | tf_op jit(solution)/shard_map/ppermute | solution.py:52
  111.2 11.6 %collective-permute-start.19 = (bf16[64,1024]{1,0:T(8,128)(2,1)S(1)}, bf16[64,1024]{1,0:T(8,128)(2,1)S(1)}, u32[]{:S(2)}, u32[]{:S(2)}) collective-permute-start(bf16[64,1024]{1,0:T(8,128)(2,1)S(1)} %get-tuple-element.118.b), channel_id=1, source_target_pairs={{0,16},{1,49},{16,0},{17,33},{32,48},{33,17},{48,32},{49,1},{2,18}... | collective-permute-start | bytes 393224 | tf_op jit(solution)/shard_map/ppermute | solution.py:52
  113.5 11.7 %collective-permute-start.24 = (bf16[2,64,1024]{2,1,0:T(8,128)(2,1)S(1)}, bf16[2,64,1024]{2,1,0:T(8,128)(2,1)S(1)}, u32[]{:S(2)}, u32[]{:S(2)}) collective-permute-start(bf16[2,64,1024]{2,1,0:T(8,128)(2,1)S(1)} %get-tuple-element.127), channel_id=1, source_target_pairs={{0,16},{1,49},{16,0},{17,33},{32,48},{33,17},{48,32},{49,1},{2,18}... | collective-permute-start | bytes 786440 | tf_op jit(solution)/shard_map/ppermute | solution.py:52
  122.9 7.7 %collective-permute-start.23 = (bf16[128,1024]{1,0:T(8,128)(2,1)S(1)}, bf16[128,1024]{1,0:T(8,128)(2,1)S(1)}, u32[]{:S(2)}, u32[]{:S(2)}) collective-permute-start(bf16[128,1024]{1,0:T(8,128)(2,1)S(1)} %get-tuple-element.126.b), channel_id=1, source_target_pairs={{0,192},{1,65},{64,128},{65,1},{128,64},{129,193},{192,0},{193,129... | collective-permute-start | bytes 786440 | tf_op jit(solution)/shard_map/ppermute | solution.py:52
  124.1 15.3 %collective-permute-start.22 = (bf16[2,64,1024]{2,1,0:T(8,128)(2,1)S(1)}, bf16[2,64,1024]{2,1,0:T(8,128)(2,1)S(1)}, u32[]{:S(2)}, u32[]{:S(2)}) collective-permute-start(bf16[2,64,1024]{2,1,0:T(8,128)(2,1)S(1)} %get-tuple-element.125), channel_id=1, source_target_pairs={{0,16},{1,49},{16,0},{17,33},{32,48},{33,17},{48,32},{49,1},{2,18}... | collective-permute-start | bytes 786440 | tf_op jit(solution)/shard_map/ppermute | solution.py:52
  130.6 21.4 %collective-permute-start.28 = (bf16[256,1024]{1,0:T(8,128)(2,1)S(1)}, bf16[256,1024]{1,0:T(8,128)(2,1)S(1)}, u32[]{:S(2)}, u32[]{:S(2)}) collective-permute-start(bf16[256,1024]{1,0:T(8,128)(2,1)S(1)} %get-tuple-element.135.near), channel_id=1, source_target_pairs={{0,64},{1,193},{64,0},{65,129},{128,192},{129,65},{192,128},{193,1... | collective-permute-start | bytes 1572872 | tf_op jit(solution)/shard_map/ppermute | solution.py:52
  130.7 12.4 %collective-permute-start.26 = (bf16[64,1024]{1,0:T(8,128)(2,1)S(1)}, bf16[64,1024]{1,0:T(8,128)(2,1)S(1)}, u32[]{:S(2)}, u32[]{:S(2)}) collective-permute-start(bf16[64,1024]{1,0:T(8,128)(2,1)S(1)} %get-tuple-element.132.b), channel_id=1, source_target_pairs={{0,16},{1,49},{16,0},{17,33},{32,48},{33,17},{48,32},{49,1},{2,18}... | collective-permute-start | bytes 393224 | tf_op jit(solution)/shard_map/ppermute | solution.py:52
  134.2 17.7 %collective-permute-start.29 = (bf16[2,64,1024]{2,1,0:T(8,128)(2,1)S(1)}, bf16[2,64,1024]{2,1,0:T(8,128)(2,1)S(1)}, u32[]{:S(2)}, u32[]{:S(2)}) collective-permute-start(bf16[2,64,1024]{2,1,0:T(8,128)(2,1)S(1)} %get-tuple-element.136.refs_0_), channel_id=1, source_target_pairs={{0,48},{1,17},{16,32},{17,1},{32,16},{33,49},{48,0},{49,33},{2,50}... | collective-permute-start | bytes 786440 | tf_op jit(solution)/shard_map/ppermute | solution.py:52
  143.1 11.1 %collective-permute-start.27 = (bf16[128,1024]{1,0:T(8,128)(2,1)S(1)}, bf16[128,1024]{1,0:T(8,128)(2,1)S(1)}, u32[]{:S(2)}, u32[]{:S(2)}) collective-permute-start(bf16[128,1024]{1,0:T(8,128)(2,1)S(1)} %get-tuple-element.134.b), channel_id=1, source_target_pairs={{0,192},{1,65},{64,128},{65,1},{128,64},{129,193},{192,0},{193,129... | collective-permute-start | bytes 786440 | tf_op jit(solution)/shard_map/ppermute | solution.py:52
  144.8 19.5 %collective-permute-start.25 = (bf16[2,64,1024]{2,1,0:T(8,128)(2,1)S(1)}, bf16[2,64,1024]{2,1,0:T(8,128)(2,1)S(1)}, u32[]{:S(2)}, u32[]{:S(2)}) collective-permute-start(bf16[2,64,1024]{2,1,0:T(8,128)(2,1)S(1)} %get-tuple-element.131.refs_0_), channel_id=1, source_target_pairs={{0,48},{1,17},{16,32},{17,1},{32,16},{33,49},{48,0},{49,33},{2,50}... | collective-permute-start | bytes 786440 | tf_op jit(solution)/shard_map/ppermute | solution.py:52
  154.2 18.8 %collective-permute-start.33 = (bf16[256,1024]{1,0:T(8,128)(2,1)S(1)}, bf16[256,1024]{1,0:T(8,128)(2,1)S(1)}, u32[]{:S(2)}, u32[]{:S(2)}) collective-permute-start(bf16[256,1024]{1,0:T(8,128)(2,1)S(1)} %get-tuple-element.146.near), channel_id=1, source_target_pairs={{0,64},{1,193},{64,0},{65,129},{128,192},{129,65},{192,128},{193,1... | collective-permute-start | bytes 1572872 | tf_op jit(solution)/shard_map/ppermute | solution.py:52
  154.3 10.2 %collective-permute-start.31 = (bf16[64,1024]{1,0:T(8,128)(2,1)S(1)}, bf16[64,1024]{1,0:T(8,128)(2,1)S(1)}, u32[]{:S(2)}, u32[]{:S(2)}) collective-permute-start(bf16[64,1024]{1,0:T(8,128)(2,1)S(1)} %get-tuple-element.142.b), channel_id=1, source_target_pairs={{0,16},{1,49},{16,0},{17,33},{32,48},{33,17},{48,32},{49,1},{2,18}... | collective-permute-start | bytes 393224 | tf_op jit(solution)/shard_map/ppermute | solution.py:52
  164.4 6.0 %collective-permute-start.30 = (bf16[64,1024]{1,0:T(8,128)(2,1)S(1)}, bf16[64,1024]{1,0:T(8,128)(2,1)S(1)}, u32[]{:S(2)}, u32[]{:S(2)}) collective-permute-start(bf16[64,1024]{1,0:T(8,128)(2,1)S(1)} %get-tuple-element.141.b), channel_id=1, source_target_pairs={{0,16},{1,49},{16,0},{17,33},{32,48},{33,17},{48,32},{49,1},{2,18}... | collective-permute-start | bytes 393224 | tf_op jit(solution)/shard_map/ppermute | solution.py:52
  164.6 8.3 %collective-permute-start.34 = (bf16[128,1024]{1,0:T(8,128)(2,1)S(1)}, bf16[128,1024]{1,0:T(8,128)(2,1)S(1)}, u32[]{:S(2)}, u32[]{:S(2)}) collective-permute-start(bf16[128,1024]{1,0:T(8,128)(2,1)S(1)} %get-tuple-element.147.b), channel_id=1, source_target_pairs={{0,192},{1,65},{64,128},{65,1},{128,64},{129,193},{192,0},{193,129... | collective-permute-start | bytes 786440 | tf_op jit(solution)/shard_map/ppermute | solution.py:52
  170.4 10.5 %collective-permute-start.32 = (bf16[128,1024]{1,0:T(8,128)(2,1)S(1)}, bf16[128,1024]{1,0:T(8,128)(2,1)S(1)}, u32[]{:S(2)}, u32[]{:S(2)}) collective-permute-start(bf16[128,1024]{1,0:T(8,128)(2,1)S(1)} %get-tuple-element.145.b), channel_id=1, source_target_pairs={{0,192},{1,65},{64,128},{65,1},{128,64},{129,193},{192,0},{193,129... | collective-permute-start | bytes 786440 | tf_op jit(solution)/shard_map/ppermute | solution.py:52
  172.9 9.3 %collective-permute-start.36 = (bf16[256,1024]{1,0:T(8,128)(2,1)S(1)}, bf16[256,1024]{1,0:T(8,128)(2,1)S(1)}, u32[]{:S(2)}, u32[]{:S(2)}) collective-permute-start(bf16[256,1024]{1,0:T(8,128)(2,1)S(1)} %get-tuple-element.153.near), channel_id=1, source_target_pairs={{0,64},{1,193},{64,0},{65,129},{128,192},{129,65},{192,128},{193,1... | collective-permute-start | bytes 1572872 | tf_op jit(solution)/shard_map/ppermute | solution.py:52
  181.0 9.3 %collective-permute-start.35 = (bf16[256,1024]{1,0:T(8,128)(2,1)S(1)}, bf16[256,1024]{1,0:T(8,128)(2,1)S(1)}, u32[]{:S(2)}, u32[]{:S(2)}) collective-permute-start(bf16[256,1024]{1,0:T(8,128)(2,1)S(1)} %get-tuple-element.152.near), channel_id=1, source_target_pairs={{0,64},{1,193},{64,0},{65,129},{128,192},{129,65},{192,128},{193,1... | collective-permute-start | bytes 1572872 | tf_op jit(solution)/shard_map/ppermute | solution.py:52

commit v3 on v2

--- a/solution.py
+++ b/solution.py
@@ -18,13 +18,13 @@
     "SA A0 hB hV",
     "SC A1 B0 A2",
     "hD C0 B1 A3",
-    "D0 B2 A4 B3",
-    "C1 D1 C2 B4",
-    "A5 D2 C3 A6",
-    "D3 B5 C4 A7",
-    "B6 D4 C5 D5",
-    "C6 B7 D6 C7",
-    "D7",
+    "D0 C1 B2 D1",
+    "A4 B3 A5 D2",
+    "B4 A6 C2 B5",
+    "D3 C3 A7 D4",
+    "B6 C4 D5 C5",
+    "D6 B7 C6 D7",
+    "C7",
 )
 ORDER = [step for line in ORDER for step in line.split()]
 EXCHANGES = (
@@ -158,7 +158,7 @@
         ],
         name="fisher_parts",
         **params(14),
-    )(where, acts, mine, peer, weights, after)
+    )(where, acts, mine, peer, pltpu.with_memory_space_constraint(weights, pltpu.HBM), after)
 
 
 def total_of(refs):

time: 193 us -> 190 us (0.984)
  the two profiles are of different devices: /device:TPU:32 before, /device:TPU:22 now
where the time goes in v3:
time: 190 us; the launch traced here: 189 us
  waiting for transfers between devices  85.9 us (45%)
  starting transfers between devices  61.3 us (32%)
  Pallas kernels  38.9 us (20%)
  local copies, waits for them, and re-layouts  2.77 us (1%)
    ppermute x32, waiting for transfers between devices, exchange(): return lax.ppermute(value, (axis, 'c'), pairs)  85.5 us
    ppermute x32, starting transfers between devices, exchange(): return lax.ppermute(value, (axis, 'c'), pairs)  59.3 us
    pallas_call x4, Pallas kernels, fisher_parts(): pl.pallas_call(fisher_kernel, out_shape=[jax.ShapeDtypeStruct((2, ROWS //...  17.4 us
    pallas_call x4, Pallas kernels, place(): pl.pallas_call(place_kernel, out_shape=[jax.ShapeDtypeStruct(weights.shap...  8.96 us
    pallas_call x16, Pallas kernels, add_up(): pl.pallas_call(merge_kernel if divide else add_kernel, out_shape=[jax.Sha...  8.23 us
    pallas_call x2, Pallas kernels, stack(): pl.pallas_call(stack_kernel, out_shape=[jax.ShapeDtypeStruct((2, *a.shape...  4.16 us
  transfers between devices with their start and end apart: 37, of which 19 were waited for; matrix products, arithmetic and copies ran while one was open for 1% of the time, Pallas kernels for 18%

profile of v3, /device:TPU:22, one launch (start us, length us, event | category | flops | bytes accessed | tf_op | source)
XLA Modules:
  0.0 189.2 jit_solution(14887663544763119274)
XLA Ops:
  0.8 1.5 copy.10
  2.3 7.1 %collective-permute-done.1.b = bf16[4,256,256]{2,1,0:T(8,128)(2,1)S(1)} collective-permute-done((bf16[4,256,256]{2,1,0:T(8,128)(2,1)}, bf16[4,256,256]{2,1,0:T(8,128)(2,1)S(1)}, u32[]{:S(2)}, u32[]{:S(2)}) %collective-permute-start.1) | collective-permute-done | bytes 524320 | tf_op jit(solution)/shard_map/ppermute | solution.py:52
  9.4 2.1 %stack.89 = (bf16[2,4,256,256]{3,2,1,0:T(8,128)(2,1)}, f32[8,128]{1,0:T(8,128)S(1)}) custom-call(bf16[4,256,256]{2,1,0:T(8,128)(2,1)} %bitcast.7.a, bf16[4,256,256]{2,1,0:T(8,128)(2,1)S(1)} %collective-permute-done.1.b, bf16[4,512,256]{2,1,0:T(8,128)(2,1)S(1)} %bitcast.22), custom_call_target="tpu_custom_call" | custom-call | flops 1 | bytes 1 | tf_op jit(solution)/shard_map/stack/pallas_call | solution.py:97
  12.0 1.9 %collective-permute-start = (bf16[4,256,256]{2,1,0:T(8,128)(2,1)}, bf16[4,256,256]{2,1,0:T(8,128)(2,1)}, u32[]{:S(2)}, u32[]{:S(2)}) collective-permute-start(bf16[4,256,256]{2,1,0:T(8,128)(2,1)} %bitcast.7.a), channel_id=1, source_target_pairs={{0,8},{8,0},{1,9},{9,1},{2,10},{10,2},{3,11},{11,3},{4,12},{12,4},... | collective-permute-start | bytes 1572872 | tf_op jit(solution)/shard_map/ppermute | solution.py:56
  14.3 3.8 %fisher_parts.4 = (bf16[2,256,1024]{2,1,0:T(8,128)(2,1)S(1)}, bf16[2,256,1024]{2,1,0:T(8,128)(2,1)S(1)}, f32[8,128]{1,0:T(8,128)S(1)}) custom-call(s32[5]{0:T(128)S(1)} %stack.78.where, bf16[4,512,256]{2,1,0:T(8,128)(2,1)S(1)} %bitcast.23, bf16[2,4,256,256]{3,2,1,0:T(8,128)(2,1)} %get-tuple-element.82.mine, ...), custom_call_target="tpu_custom_call" | custom-call | flops 1 | bytes 1 | tf_op jit(solution)/shard_map/fisher_parts/pallas_call | solution.py:142
  18.2 1.4 collective-permute-start.7
  19.6 8.2 %collective-permute-done.2.value = bf16[2,4,256,256]{3,2,1,0:T(8,128)(2,1)} collective-permute-done((bf16[2,4,256,256]{3,2,1,0:T(8,128)(2,1)}, bf16[2,4,256,256]{3,2,1,0:T(8,128)(2,1)}, u32[]{:S(2)}, u32[]{:S(2)}) %collective-permute-start.2) | collective-permute-done | bytes 1048608 | tf_op jit(solution)/shard_map/ppermute | solution.py:52
  27.9 9.3 %collective-permute-done.4.b = bf16[4,256,256]{2,1,0:T(8,128)(2,1)S(1)} collective-permute-done((bf16[4,256,256]{2,1,0:T(8,128)(2,1)}, bf16[4,256,256]{2,1,0:T(8,128)(2,1)S(1)}, u32[]{:S(2)}, u32[]{:S(2)}) %collective-permute-start.4) | collective-permute-done | bytes 524320 | tf_op jit(solution)/shard_map/ppermute | solution.py:52
  37.2 2.1 %stack.90 = (bf16[2,4,256,256]{3,2,1,0:T(8,128)(2,1)}, f32[8,128]{1,0:T(8,128)S(1)}) custom-call(bf16[4,256,256]{2,1,0:T(8,128)(2,1)} %get-tuple-element.86.a, bf16[4,256,256]{2,1,0:T(8,128)(2,1)S(1)} %collective-permute-done.4.b, f32[8,128]{1,0:T(8,128)S(1)} %get-tuple-element.87.after), custom_call_target="tpu_custom_call" | custom-call | flops 1 | bytes 1 | tf_op jit(solution)/shard_map/stack/pallas_call | solution.py:97
  41.3 5.1 %fisher_parts.5 = (bf16[2,256,1024]{2,1,0:T(8,128)(2,1)}, bf16[2,256,1024]{2,1,0:T(8,128)(2,1)S(1)}, f32[8,128]{1,0:T(8,128)S(1)}) custom-call(s32[5]{0:T(128)S(1)} %stack.83.where, bf16[4,512,256]{2,1,0:T(8,128)(2,1)S(1)} %bitcast.24, bf16[2,4,256,256]{3,2,1,0:T(8,128)(2,1)} %get-tuple-element.93.mine, ...), custom_call_target="tpu_custom_call" | custom-call | flops 1 | bytes 1 | tf_op jit(solution)/shard_map/fisher_parts/pallas_call | solution.py:142
  47.4 2.8 %collective-permute-start.13 = (bf16[2,256,1024]{2,1,0:T(8,128)(2,1)}, bf16[2,256,1024]{2,1,0:T(8,128)(2,1)}, u32[]{:S(2)}, u32[]{:S(2)}) collective-permute-start(bf16[2,256,1024]{2,1,0:T(8,128)(2,1)} %get-tuple-element.103), channel_id=1, source_target_pairs={{0,64},{1,193},{64,0},{65,129},{128,192},{129,65},{192,128},{193,1... | collective-permute-start | bytes 3145736 | tf_op jit(solution)/shard_map/ppermute | solution.py:52
  50.2 1.8 add_up.13
  52.0 3.6 %collective-permute-done.6.value = bf16[2,4,256,256]{3,2,1,0:T(8,128)(2,1)} collective-permute-done((bf16[2,4,256,256]{3,2,1,0:T(8,128)(2,1)}, bf16[2,4,256,256]{3,2,1,0:T(8,128)(2,1)}, u32[]{:S(2)}, u32[]{:S(2)}) %collective-permute-start.6) | collective-permute-done | bytes 1048608 | tf_op jit(solution)/shard_map/ppermute | solution.py:52
  55.6 3.3 %collective-permute-start.12 = (bf16[2,64,1024]{2,1,0:T(8,128)(2,1)}, bf16[2,64,1024]{2,1,0:T(8,128)(2,1)S(1)}, u32[]{:S(2)}, u32[]{:S(2)}) collective-permute-start(bf16[2,64,1024]{2,1,0:T(8,128)(2,1)} %get-tuple-element.101), channel_id=1, source_target_pairs={{0,16},{1,49},{16,0},{17,33},{32,48},{33,17},{48,32},{49,1},{2,18}... | collective-permute-start | bytes 786440 | tf_op jit(solution)/shard_map/ppermute | solution.py:52
  59.1 4.2 %fisher_parts.6 = (bf16[2,256,1024]{2,1,0:T(8,128)(2,1)S(1)}, bf16[2,256,1024]{2,1,0:T(8,128)(2,1)S(1)}, f32[8,128]{1,0:T(8,128)S(1)}) custom-call(s32[5]{0:T(128)S(1)} %stack.73.where, bf16[4,512,256]{2,1,0:T(8,128)(2,1)S(1)} %bitcast.25, bf16[2,4,256,256]{3,2,1,0:T(8,128)(2,1)} %get-tuple-element.88.mine, ...), custom_call_target="tpu_custom_call" | custom-call | flops 1 | bytes 1 | tf_op jit(solution)/shard_map/fisher_parts/pallas_call | solution.py:142
  63.3 1.4 collective-permute-start.10
  64.7 1.2 add_up.14
  66.3 1.1 add_up.15
  67.4 4.2 %fisher_parts.7 = (bf16[2,256,1024]{2,1,0:T(8,128)(2,1)S(1)}, bf16[2,256,1024]{2,1,0:T(8,128)(2,1)S(1)}, f32[8,128]{1,0:T(8,128)S(1)}) custom-call(s32[5]{0:T(128)S(1)} %stack.88.where, bf16[4,512,256]{2,1,0:T(8,128)(2,1)S(1)} %bitcast.26, bf16[2,4,256,256]{3,2,1,0:T(8,128)(2,1)} %get-tuple-element.100.mine, ...), custom_call_target="tpu_custom_call" | custom-call | flops 1 | bytes 1 | tf_op jit(solution)/shard_map/fisher_parts/pallas_call | solution.py:142
  71.5 1.4 collective-permute-start.16
  72.9 6.0 %collective-permute-start.15 = (bf16[2,64,1024]{2,1,0:T(8,128)(2,1)S(1)}, bf16[2,64,1024]{2,1,0:T(8,128)(2,1)S(1)}, u32[]{:S(2)}, u32[]{:S(2)}) collective-permute-start(bf16[2,64,1024]{2,1,0:T(8,128)(2,1)S(1)} %get-tuple-element.109.refs_0_), channel_id=1, source_target_pairs={{0,48},{1,17},{16,32},{17,1},{32,16},{33,49},{48,0},{49,33},{2,50}... | collective-permute-start | bytes 786440 | tf_op jit(solution)/shard_map/ppermute | solution.py:52
  79.0 8.7 %collective-permute-done.17.refs_2_ = bf16[2,128,1024]{2,1,0:T(8,128)(2,1)S(1)} collective-permute-done((bf16[2,128,1024]{2,1,0:T(8,128)(2,1)S(1)}, bf16[2,128,1024]{2,1,0:T(8,128)(2,1)S(1)}, u32[]{:S(2)}, u32[]{:S(2)}) %collective-permute-start.17) | collective-permute-done | bytes 524320 | tf_op jit(solution)/shard_map/ppermute | solution.py:52
  89.8 5.2 %collective-permute-done.16.refs_1_ = bf16[2,256,1024]{2,1,0:T(8,128)(2,1)S(1)} collective-permute-done((bf16[2,256,1024]{2,1,0:T(8,128)(2,1)S(1)}, bf16[2,256,1024]{2,1,0:T(8,128)(2,1)S(1)}, u32[]{:S(2)}, u32[]{:S(2)}) %collective-permute-start.16) | collective-permute-done | bytes 1048608 | tf_op jit(solution)/shard_map/ppermute | solution.py:52
  95.9 1.6 collective-permute-start.14
  97.6 1.6 collective-permute-done.19.refs_3_
  100.2 5.2 %collective-permute-start.21 = (bf16[2,64,1024]{2,1,0:T(8,128)(2,1)S(1)}, bf16[2,64,1024]{2,1,0:T(8,128)(2,1)S(1)}, u32[]{:S(2)}, u32[]{:S(2)}) collective-permute-start(bf16[2,64,1024]{2,1,0:T(8,128)(2,1)S(1)} %get-tuple-element.121.refs_0_), channel_id=1, source_target_pairs={{0,48},{1,17},{16,32},{17,1},{32,16},{33,49},{48,0},{49,33},{2,50}... | collective-permute-start | bytes 786440 | tf_op jit(solution)/shard_map/ppermute | solution.py:52
  105.9 2.0 %collective-permute-start.24 = (bf16[2,64,1024]{2,1,0:T(8,128)(2,1)S(1)}, bf16[2,64,1024]{2,1,0:T(8,128)(2,1)S(1)}, u32[]{:S(2)}, u32[]{:S(2)}) collective-permute-start(bf16[2,64,1024]{2,1,0:T(8,128)(2,1)S(1)} %get-tuple-element.128), channel_id=1, source_target_pairs={{0,16},{1,49},{16,0},{17,33},{32,48},{33,17},{48,32},{49,1},{2,18}... | collective-permute-start | bytes 786440 | tf_op jit(solution)/shard_map/ppermute | solution.py:52
  107.9 8.9 %collective-permute-done.21.refs_1_ = bf16[2,64,1024]{2,1,0:T(8,128)(2,1)S(1)} collective-permute-done((bf16[2,64,1024]{2,1,0:T(8,128)(2,1)S(1)}, bf16[2,64,1024]{2,1,0:T(8,128)(2,1)S(1)}, u32[]{:S(2)}, u32[]{:S(2)}) %collective-permute-start.21) | collective-permute-done | bytes 262176 | tf_op jit(solution)/shard_map/ppermute | solution.py:52
  116.9 5.0 %collective-permute-start.29 = (bf16[256,1024]{1,0:T(8,128)(2,1)S(1)}, bf16[256,1024]{1,0:T(8,128)(2,1)S(1)}, u32[]{:S(2)}, u32[]{:S(2)}) collective-permute-start(bf16[256,1024]{1,0:T(8,128)(2,1)S(1)} %get-tuple-element.136.near), channel_id=1, source_target_pairs={{0,64},{1,193},{64,0},{65,129},{128,192},{129,65},{192,128},{193,1... | collective-permute-start | bytes 1572872 | tf_op jit(solution)/shard_map/ppermute | solution.py:52
  122.0 3.0 %collective-permute-start.23 = (bf16[2,64,1024]{2,1,0:T(8,128)(2,1)S(1)}, bf16[2,64,1024]{2,1,0:T(8,128)(2,1)S(1)}, u32[]{:S(2)}, u32[]{:S(2)}) collective-permute-start(bf16[2,64,1024]{2,1,0:T(8,128)(2,1)S(1)} %get-tuple-element.127), channel_id=1, source_target_pairs={{0,16},{1,49},{16,0},{17,33},{32,48},{33,17},{48,32},{49,1},{2,18}... | collective-permute-start | bytes 786440 | tf_op jit(solution)/shard_map/ppermute | solution.py:52
  125.0 4.0 %collective-permute-done.25.a = bf16[64,1024]{1,0:T(8,128)(2,1)S(1)} collective-permute-done((bf16[64,1024]{1,0:T(8,128)(2,1)S(1)}, bf16[64,1024]{1,0:T(8,128)(2,1)S(1)}, u32[]{:S(2)}, u32[]{:S(2)}) %collective-permute-start.25) | collective-permute-done | bytes 131104 | tf_op jit(solution)/shard_map/ppermute | solution.py:52
  129.2 10.6 %collective-permute-start.28 = (bf16[2,64,1024]{2,1,0:T(8,128)(2,1)S(1)}, bf16[2,64,1024]{2,1,0:T(8,128)(2,1)S(1)}, u32[]{:S(2)}, u32[]{:S(2)}) collective-permute-start(bf16[2,64,1024]{2,1,0:T(8,128)(2,1)S(1)} %get-tuple-element.135.refs_0_), channel_id=1, source_target_pairs={{0,48},{1,17},{16,32},{17,1},{32,16},{33,49},{48,0},{49,33},{2,50}... | collective-permute-start | bytes 786440 | tf_op jit(solution)/shard_map/ppermute | solution.py:52
  139.9 2.0 %collective-permute-done.23.refs_3_ = bf16[2,64,1024]{2,1,0:T(8,128)(2,1)S(1)} collective-permute-done((bf16[2,64,1024]{2,1,0:T(8,128)(2,1)S(1)}, bf16[2,64,1024]{2,1,0:T(8,128)(2,1)S(1)}, u32[]{:S(2)}, u32[]{:S(2)}) %collective-permute-start.23) | collective-permute-done | bytes 262176 | tf_op jit(solution)/shard_map/ppermute | solution.py:52
  142.0 3.6 %collective-permute-start.26 = (bf16[2,64,1024]{2,1,0:T(8,128)(2,1)S(1)}, bf16[2,64,1024]{2,1,0:T(8,128)(2,1)S(1)}, u32[]{:S(2)}, u32[]{:S(2)}) collective-permute-start(bf16[2,64,1024]{2,1,0:T(8,128)(2,1)S(1)} %get-tuple-element.133.refs_0_), channel_id=1, source_target_pairs={{0,48},{1,17},{16,32},{17,1},{32,16},{33,49},{48,0},{49,33},{2,50}... | collective-permute-start | bytes 786440 | tf_op jit(solution)/shard_map/ppermute | solution.py:52
  145.6 2.2 %place.4 = (bf16[512,4096]{1,0:T(8,128)(2,1)}, f32[8,128]{1,0:T(8,128)S(1)}) custom-call(s32[5]{0:T(128)S(1)} %stack.78.where, bf16[256,1024]{1,0:T(8,128)(2,1)S(1)} %collective-permute-done.29.far, bf16[256,1024]{1,0:T(8,128)(2,1)S(1)} %get-tuple-element.136.near, f32[8,128]{1,0:T(8,128)S(1)} %get-tuple-element.137.refs_0_), custom_call_target="tpu_custom_call" | custom-call | flops 1 | bytes 1 | tf_op jit(solution)/shard_map/place/pallas_call | solution.py:228
  147.9 5.5 %collective-permute-done.28.refs_1_ = bf16[2,64,1024]{2,1,0:T(8,128)(2,1)S(1)} collective-permute-done((bf16[2,64,1024]{2,1,0:T(8,128)(2,1)S(1)}, bf16[2,64,1024]{2,1,0:T(8,128)(2,1)S(1)}, u32[]{:S(2)}, u32[]{:S(2)}) %collective-permute-start.28) | collective-permute-done | bytes 262176 | tf_op jit(solution)/shard_map/ppermute | solution.py:52
  153.7 4.3 %collective-permute-done.26.refs_1_ = bf16[2,64,1024]{2,1,0:T(8,128)(2,1)S(1)} collective-permute-done((bf16[2,64,1024]{2,1,0:T(8,128)(2,1)S(1)}, bf16[2,64,1024]{2,1,0:T(8,128)(2,1)S(1)}, u32[]{:S(2)}, u32[]{:S(2)}) %collective-permute-start.26) | collective-permute-done | bytes 262176 | tf_op jit(solution)/shard_map/ppermute | solution.py:52
  158.1 4.7 %collective-permute-start.30 = (bf16[64,1024]{1,0:T(8,128)(2,1)S(1)}, bf16[64,1024]{1,0:T(8,128)(2,1)S(1)}, u32[]{:S(2)}, u32[]{:S(2)}) collective-permute-start(bf16[64,1024]{1,0:T(8,128)(2,1)S(1)} %get-tuple-element.141.b), channel_id=1, source_target_pairs={{0,16},{1,49},{16,0},{17,33},{32,48},{33,17},{48,32},{49,1},{2,18}... | collective-permute-start | bytes 393224 | tf_op jit(solution)/shard_map/ppermute | solution.py:52
  162.9 2.8 %collective-permute-done.30.a = bf16[64,1024]{1,0:T(8,128)(2,1)S(1)} collective-permute-done((bf16[64,1024]{1,0:T(8,128)(2,1)S(1)}, bf16[64,1024]{1,0:T(8,128)(2,1)S(1)}, u32[]{:S(2)}, u32[]{:S(2)}) %collective-permute-start.30) | collective-permute-done | bytes 131104 | tf_op jit(solution)/shard_map/ppermute | solution.py:52
  165.9 6.1 %collective-permute-done.34.a = bf16[128,1024]{1,0:T(8,128)(2,1)S(1)} collective-permute-done((bf16[128,1024]{1,0:T(8,128)(2,1)S(1)}, bf16[128,1024]{1,0:T(8,128)(2,1)S(1)}, u32[]{:S(2)}, u32[]{:S(2)}) %collective-permute-start.34) | collective-permute-done | bytes 262176 | tf_op jit(solution)/shard_map/ppermute | solution.py:52
  172.0 1.4 collective-permute-start.36
  173.4 2.2 %place.5 = (bf16[512,4096]{1,0:T(8,128)(2,1)}, f32[8,128]{1,0:T(8,128)S(1)}) custom-call(s32[5]{0:T(128)S(1)} %stack.83.where, bf16[256,1024]{1,0:T(8,128)(2,1)S(1)} %collective-permute-done.33.far, bf16[256,1024]{1,0:T(8,128)(2,1)S(1)} %get-tuple-element.146.near, f32[8,128]{1,0:T(8,128)S(1)} %get-tuple-element.149.refs_0_, ...), custom_call_target="tpu_custom_call", output_to_operand_aliasing={{0}: (4, {})} | custom-call | flops 1 | bytes 1 | tf_op jit(solution)/shard_map/place/pallas_call | solution.py:228
  175.6 2.0 %collective-permute-done.32.a = bf16[128,1024]{1,0:T(8,128)(2,1)S(1)} collective-permute-done((bf16[128,1024]{1,0:T(8,128)(2,1)S(1)}, bf16[128,1024]{1,0:T(8,128)(2,1)S(1)}, u32[]{:S(2)}, u32[]{:S(2)}) %collective-permute-start.32) | collective-permute-done | bytes 262176 | tf_op jit(solution)/shard_map/ppermute | solution.py:52
  177.7 1.4 collective-permute-start.35
  179.0 2.3 %collective-permute-done.36.far = bf16[256,1024]{1,0:T(8,128)(2,1)S(1)} collective-permute-done((bf16[256,1024]{1,0:T(8,128)(2,1)S(1)}, bf16[256,1024]{1,0:T(8,128)(2,1)S(1)}, u32[]{:S(2)}, u32[]{:S(2)}) %collective-permute-start.36) | collective-permute-done | bytes 524320 | tf_op jit(solution)/shard_map/ppermute | solution.py:52
  181.3 2.2 %place.6 = (bf16[512,4096]{1,0:T(8,128)(2,1)}, f32[8,128]{1,0:T(8,128)S(1)}) custom-call(s32[5]{0:T(128)S(1)} %stack.88.where, bf16[256,1024]{1,0:T(8,128)(2,1)S(1)} %collective-permute-done.36.far, bf16[256,1024]{1,0:T(8,128)(2,1)S(1)} %get-tuple-element.153.near, f32[8,128]{1,0:T(8,128)S(1)} %get-tuple-element.154.refs_0_, ...), custom_call_target="tpu_custom_call", output_to_operand_aliasing={{0}: (4, {})} | custom-call | flops 1 | bytes 1 | tf_op jit(solution)/shard_map/place/pallas_call | solution.py:228
  183.6 3.4 %collective-permute-done.35.far = bf16[256,1024]{1,0:T(8,128)(2,1)S(1)} collective-permute-done((bf16[256,1024]{1,0:T(8,128)(2,1)S(1)}, bf16[256,1024]{1,0:T(8,128)(2,1)S(1)}, u32[]{:S(2)}, u32[]{:S(2)}) %collective-permute-start.35) | collective-permute-done | bytes 524320 | tf_op jit(solution)/shard_map/ppermute | solution.py:52
  186.9 2.2 %place.7 = (bf16[512,4096]{1,0:T(8,128)(2,1)}, f32[8,128]{1,0:T(8,128)}) custom-call(s32[5]{0:T(128)S(1)} %stack.73.where, bf16[256,1024]{1,0:T(8,128)(2,1)S(1)} %collective-permute-done.35.far, bf16[256,1024]{1,0:T(8,128)(2,1)S(1)} %get-tuple-element.152.near, f32[8,128]{1,0:T(8,128)S(1)} %get-tuple-element.156.refs_0_, ...), custom_call_target="tpu_custom_call", output_to_operand_aliasing={{0}: (4, {})} | custom-call | flops 1 | bytes 1 | tf_op jit(solution)/shard_map/place/pallas_call | solution.py:228
  (72 shorter events, 11.3 us)
Async XLA Ops:
  0.0 9.4 %collective-permute-start.1 = (bf16[4,256,256]{2,1,0:T(8,128)(2,1)}, bf16[4,256,256]{2,1,0:T(8,128)(2,1)S(1)}, u32[]{:S(2)}, u32[]{:S(2)}) collective-permute-start(bf16[4,256,256]{2,1,0:T(8,128)(2,1)} %bitcast.7.a), channel_id=1, source_target_pairs={{0,2},{1,7},{2,0},{3,5},{4,6},{5,3},{6,4},{7,1},{8,10},{9,15},{10,... | collective-permute-start | bytes 1572872 | tf_op jit(solution)/shard_map/ppermute | solution.py:52
  11.5 2.9 %collective-permute-start.3 = (bf16[2,4,256,256]{3,2,1,0:T(8,128)(2,1)}, bf16[2,4,256,256]{3,2,1,0:T(8,128)(2,1)S(1)}, u32[]{:S(2)}, u32[]{:S(2)}) collective-permute-start(bf16[2,4,256,256]{3,2,1,0:T(8,128)(2,1)} %get-tuple-element.82.mine), channel_id=1, source_target_pairs={{0,1},{1,0},{2,3},{3,2},{4,5},{5,4},{6,7},{7,6},{8,9},{9,8},{10,11... | collective-permute-start | bytes 3145736 | tf_op jit(solution)/shard_map/ppermute | solution.py:56
  11.5 16.3 %collective-permute-start.2 = (bf16[2,4,256,256]{3,2,1,0:T(8,128)(2,1)}, bf16[2,4,256,256]{3,2,1,0:T(8,128)(2,1)}, u32[]{:S(2)}, u32[]{:S(2)}) collective-permute-start(bf16[2,4,256,256]{3,2,1,0:T(8,128)(2,1)} %get-tuple-element.82.mine), channel_id=1, source_target_pairs={{0,6},{1,3},{2,4},{3,1},{4,2},{5,7},{6,0},{7,5},{8,14},{9,11},{10,... | collective-permute-start | bytes 3145736 | tf_op jit(solution)/shard_map/ppermute | solution.py:52
  12.0 15.9 %collective-permute-start = (bf16[4,256,256]{2,1,0:T(8,128)(2,1)}, bf16[4,256,256]{2,1,0:T(8,128)(2,1)}, u32[]{:S(2)}, u32[]{:S(2)}) collective-permute-start(bf16[4,256,256]{2,1,0:T(8,128)(2,1)} %bitcast.7.a), channel_id=1, source_target_pairs={{0,8},{8,0},{1,9},{9,1},{2,10},{10,2},{3,11},{11,3},{4,12},{12,4},... | collective-permute-start | bytes 1572872 | tf_op jit(solution)/shard_map/ppermute | solution.py:56
  18.2 21.6 %collective-permute-start.7 = (bf16[2,256,1024]{2,1,0:T(8,128)(2,1)S(1)}, bf16[2,256,1024]{2,1,0:T(8,128)(2,1)S(1)}, u32[]{:S(2)}, u32[]{:S(2)}) collective-permute-start(bf16[2,256,1024]{2,1,0:T(8,128)(2,1)S(1)} %get-tuple-element.90), channel_id=1, source_target_pairs={{0,64},{1,193},{64,0},{65,129},{128,192},{129,65},{192,128},{193,1... | collective-permute-start | bytes 3145736 | tf_op jit(solution)/shard_map/ppermute | solution.py:52
  27.8 9.4 %collective-permute-start.4 = (bf16[4,256,256]{2,1,0:T(8,128)(2,1)}, bf16[4,256,256]{2,1,0:T(8,128)(2,1)S(1)}, u32[]{:S(2)}, u32[]{:S(2)}) collective-permute-start(bf16[4,256,256]{2,1,0:T(8,128)(2,1)} %get-tuple-element.86.a), channel_id=1, source_target_pairs={{0,2},{1,7},{2,0},{3,5},{4,6},{5,3},{6,4},{7,1},{8,10},{9,15},{10,... | collective-permute-start | bytes 1572872 | tf_op jit(solution)/shard_map/ppermute | solution.py:52
  27.9 13.4 %collective-permute-start.9 = (bf16[2,4,256,256]{3,2,1,0:T(8,128)(2,1)}, bf16[2,4,256,256]{3,2,1,0:T(8,128)(2,1)}, u32[]{:S(2)}, u32[]{:S(2)}) collective-permute-start(bf16[2,4,256,256]{3,2,1,0:T(8,128)(2,1)} %get-tuple-element.93.mine), channel_id=1, source_target_pairs={{0,1},{1,0},{2,3},{3,2},{4,5},{5,4},{6,7},{7,6},{8,9},{9,8},{10,11... | collective-permute-start | bytes 3145736 | tf_op jit(solution)/shard_map/ppermute | solution.py:56
  39.3 16.3 %collective-permute-start.6 = (bf16[2,4,256,256]{3,2,1,0:T(8,128)(2,1)}, bf16[2,4,256,256]{3,2,1,0:T(8,128)(2,1)}, u32[]{:S(2)}, u32[]{:S(2)}) collective-permute-start(bf16[2,4,256,256]{3,2,1,0:T(8,128)(2,1)} %get-tuple-element.88.mine), channel_id=1, source_target_pairs={{0,6},{1,3},{2,4},{3,1},{4,2},{5,7},{6,0},{7,5},{8,14},{9,11},{10,... | collective-permute-start | bytes 3145736 | tf_op jit(solution)/shard_map/ppermute | solution.py:52
  40.7 9.5 %collective-permute-start.8 = (bf16[2,128,1024]{2,1,0:T(8,128)(2,1)}, bf16[2,128,1024]{2,1,0:T(8,128)(2,1)}, u32[]{:S(2)}, u32[]{:S(2)}) collective-permute-start(bf16[2,128,1024]{2,1,0:T(8,128)(2,1)} %get-tuple-element.92), channel_id=1, source_target_pairs={{0,192},{1,65},{64,128},{65,1},{128,64},{129,193},{192,0},{193,129... | collective-permute-start | bytes 1572872 | tf_op jit(solution)/shard_map/ppermute | solution.py:52
  41.2 17.8 %collective-permute-start.5 = (bf16[2,4,256,256]{3,2,1,0:T(8,128)(2,1)}, bf16[2,4,256,256]{3,2,1,0:T(8,128)(2,1)}, u32[]{:S(2)}, u32[]{:S(2)}) collective-permute-start(bf16[2,4,256,256]{3,2,1,0:T(8,128)(2,1)} %get-tuple-element.88.mine), channel_id=1, source_target_pairs={{0,1},{1,0},{2,3},{3,2},{4,5},{5,4},{6,7},{7,6},{8,9},{9,8},{10,11... | collective-permute-start | bytes 3145736 | tf_op jit(solution)/shard_map/ppermute | solution.py:56
  46.4 1.0 copy-start
  47.4 17.3 %collective-permute-start.13 = (bf16[2,256,1024]{2,1,0:T(8,128)(2,1)}, bf16[2,256,1024]{2,1,0:T(8,128)(2,1)}, u32[]{:S(2)}, u32[]{:S(2)}) collective-permute-start(bf16[2,256,1024]{2,1,0:T(8,128)(2,1)} %get-tuple-element.103), channel_id=1, source_target_pairs={{0,64},{1,193},{64,0},{65,129},{128,192},{129,65},{192,128},{193,1... | collective-permute-start | bytes 3145736 | tf_op jit(solution)/shard_map/ppermute | solution.py:52
  55.6 11.8 %collective-permute-start.11 = (bf16[2,4,256,256]{3,2,1,0:T(8,128)(2,1)}, bf16[2,4,256,256]{3,2,1,0:T(8,128)(2,1)}, u32[]{:S(2)}, u32[]{:S(2)}) collective-permute-start(bf16[2,4,256,256]{3,2,1,0:T(8,128)(2,1)} %get-tuple-element.100.mine), channel_id=1, source_target_pairs={{0,1},{1,0},{2,3},{3,2},{4,5},{5,4},{6,7},{7,6},{8,9},{9,8},{10,11... | collective-permute-start | bytes 3145736 | tf_op jit(solution)/shard_map/ppermute | solution.py:56
  55.6 10.6 %collective-permute-start.12 = (bf16[2,64,1024]{2,1,0:T(8,128)(2,1)}, bf16[2,64,1024]{2,1,0:T(8,128)(2,1)S(1)}, u32[]{:S(2)}, u32[]{:S(2)}) collective-permute-start(bf16[2,64,1024]{2,1,0:T(8,128)(2,1)} %get-tuple-element.101), channel_id=1, source_target_pairs={{0,16},{1,49},{16,0},{17,33},{32,48},{33,17},{48,32},{49,1},{2,18}... | collective-permute-start | bytes 786440 | tf_op jit(solution)/shard_map/ppermute | solution.py:52
  59.0 5.6 %copy-start.1 = (bf16[2,256,1024]{2,1,0:T(8,128)(2,1)S(1)}, bf16[2,256,1024]{2,1,0:T(8,128)(2,1)}, u32[]{:S(2)}) copy-start(bf16[2,256,1024]{2,1,0:T(8,128)(2,1)} %copy-done) | copy-start | bytes 3145732
  63.3 15.6 %collective-permute-start.10 = (bf16[2,256,1024]{2,1,0:T(8,128)(2,1)S(1)}, bf16[2,256,1024]{2,1,0:T(8,128)(2,1)S(1)}, u32[]{:S(2)}, u32[]{:S(2)}) collective-permute-start(bf16[2,256,1024]{2,1,0:T(8,128)(2,1)S(1)} %get-tuple-element.99), channel_id=1, source_target_pairs={{0,64},{1,193},{64,0},{65,129},{128,192},{129,65},{192,128},{193,1... | collective-permute-start | bytes 3145736 | tf_op jit(solution)/shard_map/ppermute | solution.py:52
  71.5 23.5 %collective-permute-start.16 = (bf16[2,256,1024]{2,1,0:T(8,128)(2,1)S(1)}, bf16[2,256,1024]{2,1,0:T(8,128)(2,1)S(1)}, u32[]{:S(2)}, u32[]{:S(2)}) collective-permute-start(bf16[2,256,1024]{2,1,0:T(8,128)(2,1)S(1)} %get-tuple-element.111), channel_id=1, source_target_pairs={{0,64},{1,193},{64,0},{65,129},{128,192},{129,65},{192,128},{193,1... | collective-permute-start | bytes 3145736 | tf_op jit(solution)/shard_map/ppermute | solution.py:52
  72.9 14.9 %collective-permute-start.17 = (bf16[2,128,1024]{2,1,0:T(8,128)(2,1)S(1)}, bf16[2,128,1024]{2,1,0:T(8,128)(2,1)S(1)}, u32[]{:S(2)}, u32[]{:S(2)}) collective-permute-start(bf16[2,128,1024]{2,1,0:T(8,128)(2,1)S(1)} %get-tuple-element.112), channel_id=1, source_target_pairs={{0,192},{1,65},{64,128},{65,1},{128,64},{129,193},{192,0},{193,129... | collective-permute-start | bytes 1572872 | tf_op jit(solution)/shard_map/ppermute | solution.py:52
  72.9 22.8 %collective-permute-start.15 = (bf16[2,64,1024]{2,1,0:T(8,128)(2,1)S(1)}, bf16[2,64,1024]{2,1,0:T(8,128)(2,1)S(1)}, u32[]{:S(2)}, u32[]{:S(2)}) collective-permute-start(bf16[2,64,1024]{2,1,0:T(8,128)(2,1)S(1)} %get-tuple-element.109.refs_0_), channel_id=1, source_target_pairs={{0,48},{1,17},{16,32},{17,1},{32,16},{33,49},{48,0},{49,33},{2,50}... | collective-permute-start | bytes 786440 | tf_op jit(solution)/shard_map/ppermute | solution.py:52
  88.8 10.3 %collective-permute-start.19 = (bf16[2,64,1024]{2,1,0:T(8,128)(2,1)S(1)}, bf16[2,64,1024]{2,1,0:T(8,128)(2,1)S(1)}, u32[]{:S(2)}, u32[]{:S(2)}) collective-permute-start(bf16[2,64,1024]{2,1,0:T(8,128)(2,1)S(1)} %get-tuple-element.117), channel_id=1, source_target_pairs={{0,16},{1,49},{16,0},{17,33},{32,48},{33,17},{48,32},{49,1},{2,18}... | collective-permute-start | bytes 786440 | tf_op jit(solution)/shard_map/ppermute | solution.py:52
  95.2 10.7 %collective-permute-start.22 = (bf16[2,128,1024]{2,1,0:T(8,128)(2,1)S(1)}, bf16[2,128,1024]{2,1,0:T(8,128)(2,1)S(1)}, u32[]{:S(2)}, u32[]{:S(2)}) collective-permute-start(bf16[2,128,1024]{2,1,0:T(8,128)(2,1)S(1)} %get-tuple-element.122), channel_id=1, source_target_pairs={{0,192},{1,65},{64,128},{65,1},{128,64},{129,193},{192,0},{193,129... | collective-permute-start | bytes 1572872 | tf_op jit(solution)/shard_map/ppermute | solution.py:52
  95.8 9.6 %collective-permute-start.18 = (bf16[64,1024]{1,0:T(8,128)(2,1)S(1)}, bf16[64,1024]{1,0:T(8,128)(2,1)S(1)}, u32[]{:S(2)}, u32[]{:S(2)}) collective-permute-start(bf16[64,1024]{1,0:T(8,128)(2,1)S(1)} %get-tuple-element.116.b), channel_id=1, source_target_pairs={{0,16},{1,49},{16,0},{17,33},{32,48},{33,17},{48,32},{49,1},{2,18}... | collective-permute-start | bytes 393224 | tf_op jit(solution)/shard_map/ppermute | solution.py:52
  95.9 26.0 %collective-permute-start.14 = (bf16[2,128,1024]{2,1,0:T(8,128)(2,1)S(1)}, bf16[2,128,1024]{2,1,0:T(8,128)(2,1)S(1)}, u32[]{:S(2)}, u32[]{:S(2)}) collective-permute-start(bf16[2,128,1024]{2,1,0:T(8,128)(2,1)S(1)} %get-tuple-element.108), channel_id=1, source_target_pairs={{0,192},{1,65},{64,128},{65,1},{128,64},{129,193},{192,0},{193,129... | collective-permute-start | bytes 1572872 | tf_op jit(solution)/shard_map/ppermute | solution.py:52
  100.2 16.6 %collective-permute-start.21 = (bf16[2,64,1024]{2,1,0:T(8,128)(2,1)S(1)}, bf16[2,64,1024]{2,1,0:T(8,128)(2,1)S(1)}, u32[]{:S(2)}, u32[]{:S(2)}) collective-permute-start(bf16[2,64,1024]{2,1,0:T(8,128)(2,1)S(1)} %get-tuple-element.121.refs_0_), channel_id=1, source_target_pairs={{0,48},{1,17},{16,32},{17,1},{32,16},{33,49},{48,0},{49,33},{2,50}... | collective-permute-start | bytes 786440 | tf_op jit(solution)/shard_map/ppermute | solution.py:52
  105.4 11.4 %collective-permute-start.20 = (bf16[128,1024]{1,0:T(8,128)(2,1)S(1)}, bf16[128,1024]{1,0:T(8,128)(2,1)S(1)}, u32[]{:S(2)}, u32[]{:S(2)}) collective-permute-start(bf16[128,1024]{1,0:T(8,128)(2,1)S(1)} %get-tuple-element.120.b), channel_id=1, source_target_pairs={{0,192},{1,65},{64,128},{65,1},{128,64},{129,193},{192,0},{193,129... | collective-permute-start | bytes 786440 | tf_op jit(solution)/shard_map/ppermute | solution.py:52
  105.9 23.1 %collective-permute-start.24 = (bf16[2,64,1024]{2,1,0:T(8,128)(2,1)S(1)}, bf16[2,64,1024]{2,1,0:T(8,128)(2,1)S(1)}, u32[]{:S(2)}, u32[]{:S(2)}) collective-permute-start(bf16[2,64,1024]{2,1,0:T(8,128)(2,1)S(1)} %get-tuple-element.128), channel_id=1, source_target_pairs={{0,16},{1,49},{16,0},{17,33},{32,48},{33,17},{48,32},{49,1},{2,18}... | collective-permute-start | bytes 786440 | tf_op jit(solution)/shard_map/ppermute | solution.py:52
  116.9 28.7 %collective-permute-start.29 = (bf16[256,1024]{1,0:T(8,128)(2,1)S(1)}, bf16[256,1024]{1,0:T(8,128)(2,1)S(1)}, u32[]{:S(2)}, u32[]{:S(2)}) collective-permute-start(bf16[256,1024]{1,0:T(8,128)(2,1)S(1)} %get-tuple-element.136.near), channel_id=1, source_target_pairs={{0,64},{1,193},{64,0},{65,129},{128,192},{129,65},{192,128},{193,1... | collective-permute-start | bytes 1572872 | tf_op jit(solution)/shard_map/ppermute | solution.py:52
  121.9 7.1 %collective-permute-start.25 = (bf16[64,1024]{1,0:T(8,128)(2,1)S(1)}, bf16[64,1024]{1,0:T(8,128)(2,1)S(1)}, u32[]{:S(2)}, u32[]{:S(2)}) collective-permute-start(bf16[64,1024]{1,0:T(8,128)(2,1)S(1)} %get-tuple-element.129.b), channel_id=1, source_target_pairs={{0,16},{1,49},{16,0},{17,33},{32,48},{33,17},{48,32},{49,1},{2,18}... | collective-permute-start | bytes 393224 | tf_op jit(solution)/shard_map/ppermute | solution.py:52
  122.0 19.8 %collective-permute-start.23 = (bf16[2,64,1024]{2,1,0:T(8,128)(2,1)S(1)}, bf16[2,64,1024]{2,1,0:T(8,128)(2,1)S(1)}, u32[]{:S(2)}, u32[]{:S(2)}) collective-permute-start(bf16[2,64,1024]{2,1,0:T(8,128)(2,1)S(1)} %get-tuple-element.127), channel_id=1, source_target_pairs={{0,16},{1,49},{16,0},{17,33},{32,48},{33,17},{48,32},{49,1},{2,18}... | collective-permute-start | bytes 786440 | tf_op jit(solution)/shard_map/ppermute | solution.py:52
  129.2 24.1 %collective-permute-start.28 = (bf16[2,64,1024]{2,1,0:T(8,128)(2,1)S(1)}, bf16[2,64,1024]{2,1,0:T(8,128)(2,1)S(1)}, u32[]{:S(2)}, u32[]{:S(2)}) collective-permute-start(bf16[2,64,1024]{2,1,0:T(8,128)(2,1)S(1)} %get-tuple-element.135.refs_0_), channel_id=1, source_target_pairs={{0,48},{1,17},{16,32},{17,1},{32,16},{33,49},{48,0},{49,33},{2,50}... | collective-permute-start | bytes 786440 | tf_op jit(solution)/shard_map/ppermute | solution.py:52
  139.8 13.6 %collective-permute-start.27 = (bf16[128,1024]{1,0:T(8,128)(2,1)S(1)}, bf16[128,1024]{1,0:T(8,128)(2,1)S(1)}, u32[]{:S(2)}, u32[]{:S(2)}) collective-permute-start(bf16[128,1024]{1,0:T(8,128)(2,1)S(1)} %get-tuple-element.134.b), channel_id=1, source_target_pairs={{0,192},{1,65},{64,128},{65,1},{128,64},{129,193},{192,0},{193,129... | collective-permute-start | bytes 786440 | tf_op jit(solution)/shard_map/ppermute | solution.py:52
  142.0 16.0 %collective-permute-start.26 = (bf16[2,64,1024]{2,1,0:T(8,128)(2,1)S(1)}, bf16[2,64,1024]{2,1,0:T(8,128)(2,1)S(1)}, u32[]{:S(2)}, u32[]{:S(2)}) collective-permute-start(bf16[2,64,1024]{2,1,0:T(8,128)(2,1)S(1)} %get-tuple-element.133.refs_0_), channel_id=1, source_target_pairs={{0,48},{1,17},{16,32},{17,1},{32,16},{33,49},{48,0},{49,33},{2,50}... | collective-permute-start | bytes 786440 | tf_op jit(solution)/shard_map/ppermute | solution.py:52
  153.5 19.9 %collective-permute-start.33 = (bf16[256,1024]{1,0:T(8,128)(2,1)S(1)}, bf16[256,1024]{1,0:T(8,128)(2,1)S(1)}, u32[]{:S(2)}, u32[]{:S(2)}) collective-permute-start(bf16[256,1024]{1,0:T(8,128)(2,1)S(1)} %get-tuple-element.146.near), channel_id=1, source_target_pairs={{0,64},{1,193},{64,0},{65,129},{128,192},{129,65},{192,128},{193,1... | collective-permute-start | bytes 1572872 | tf_op jit(solution)/shard_map/ppermute | solution.py:52
  153.6 9.2 %collective-permute-start.31 = (bf16[64,1024]{1,0:T(8,128)(2,1)S(1)}, bf16[64,1024]{1,0:T(8,128)(2,1)S(1)}, u32[]{:S(2)}, u32[]{:S(2)}) collective-permute-start(bf16[64,1024]{1,0:T(8,128)(2,1)S(1)} %get-tuple-element.142.b), channel_id=1, source_target_pairs={{0,16},{1,49},{16,0},{17,33},{32,48},{33,17},{48,32},{49,1},{2,18}... | collective-permute-start | bytes 393224 | tf_op jit(solution)/shard_map/ppermute | solution.py:52
  158.1 7.7 %collective-permute-start.30 = (bf16[64,1024]{1,0:T(8,128)(2,1)S(1)}, bf16[64,1024]{1,0:T(8,128)(2,1)S(1)}, u32[]{:S(2)}, u32[]{:S(2)}) collective-permute-start(bf16[64,1024]{1,0:T(8,128)(2,1)S(1)} %get-tuple-element.141.b), channel_id=1, source_target_pairs={{0,16},{1,49},{16,0},{17,33},{32,48},{33,17},{48,32},{49,1},{2,18}... | collective-permute-start | bytes 393224 | tf_op jit(solution)/shard_map/ppermute | solution.py:52
  162.8 9.2 %collective-permute-start.34 = (bf16[128,1024]{1,0:T(8,128)(2,1)S(1)}, bf16[128,1024]{1,0:T(8,128)(2,1)S(1)}, u32[]{:S(2)}, u32[]{:S(2)}) collective-permute-start(bf16[128,1024]{1,0:T(8,128)(2,1)S(1)} %get-tuple-element.147.b), channel_id=1, source_target_pairs={{0,192},{1,65},{64,128},{65,1},{128,64},{129,193},{192,0},{193,129... | collective-permute-start | bytes 786440 | tf_op jit(solution)/shard_map/ppermute | solution.py:52
  165.8 11.9 %collective-permute-start.32 = (bf16[128,1024]{1,0:T(8,128)(2,1)S(1)}, bf16[128,1024]{1,0:T(8,128)(2,1)S(1)}, u32[]{:S(2)}, u32[]{:S(2)}) collective-permute-start(bf16[128,1024]{1,0:T(8,128)(2,1)S(1)} %get-tuple-element.145.b), channel_id=1, source_target_pairs={{0,192},{1,65},{64,128},{65,1},{128,64},{129,193},{192,0},{193,129... | collective-permute-start | bytes 786440 | tf_op jit(solution)/shard_map/ppermute | solution.py:52
  172.0 9.3 %collective-permute-start.36 = (bf16[256,1024]{1,0:T(8,128)(2,1)S(1)}, bf16[256,1024]{1,0:T(8,128)(2,1)S(1)}, u32[]{:S(2)}, u32[]{:S(2)}) collective-permute-start(bf16[256,1024]{1,0:T(8,128)(2,1)S(1)} %get-tuple-element.153.near), channel_id=1, source_target_pairs={{0,64},{1,193},{64,0},{65,129},{128,192},{129,65},{192,128},{193,1... | collective-permute-start | bytes 1572872 | tf_op jit(solution)/shard_map/ppermute | solution.py:52
  177.7 9.3 %collective-permute-start.35 = (bf16[256,1024]{1,0:T(8,128)(2,1)S(1)}, bf16[256,1024]{1,0:T(8,128)(2,1)S(1)}, u32[]{:S(2)}, u32[]{:S(2)}) collective-permute-start(bf16[256,1024]{1,0:T(8,128)(2,1)S(1)} %get-tuple-element.152.near), channel_id=1, source_target_pairs={{0,64},{1,193},{64,0},{65,129},{128,192},{129,65},{192,128},{193,1... | collective-permute-start | bytes 1572872 | tf_op jit(solution)/shard_map/ppermute | solution.py:52

commit v4 on v3

--- a/solution.py
+++ b/solution.py
@@ -87,18 +87,23 @@
     )(value, after)
 
 
-def stack_kernel(a, b, after, out, token):
-    out[0] = a[...]
-    out[1] = b[...]
+def stack_kernel(a, b, after, out, token, sems):
+    copies = [
+        pltpu.make_async_copy(ref, out.at[at], sems.at[at]) for at, ref in enumerate((a, b))
+    ]
+    for copy in copies:
+        copy.start()
+    for copy in copies:
+        copy.wait()
 
 
 def stack(a, b, after):
-    whole = pl.BlockSpec(memory_space=pltpu.VMEM)
     return pl.pallas_call(
         stack_kernel,
         out_shape=[jax.ShapeDtypeStruct((2, *a.shape), BF), TOKEN],
-        in_specs=[whole, whole, ANY],
-        out_specs=[whole, ANY],
+        in_specs=[ANY, ANY, ANY],
+        out_specs=[ANY, ANY],
+        scratch_shapes=[pltpu.SemaphoreType.DMA((2,))],
         name="stack",
         **params(),
     )(a, b, after)
@@ -214,26 +219,40 @@
 
 
 def place_kernel(where, far, near, *refs):
-    out = refs[-2]
+    out, _, tiles, sems = refs[-4:]
     mark = where[0]
-    for k in range(16):
-        ref, at = (far, k) if k < 8 else (near, k - 8)
-        part = pl.ds(pl.multiple_of((mark ^ (15 - k)) * S, S), S)
-        out[part, :] = ref[at * S : (at + 1) * S, :]
+    count = tiles.shape[0]
+
+    def store(tile):
+        column = pl.multiple_of(where[1 + tile] * TILE, TILE)
+        return pltpu.make_async_copy(
+            tiles.at[tile], out.at[:, pl.ds(column, TILE)], sems.at[tile]
+        )
+
+    for tile in range(count):
+        cols = slice(tile * TILE, (tile + 1) * TILE)
+        for k in range(16):
+            ref, at = (far, k) if k < 8 else (near, k - 8)
+            part = pl.ds(pl.multiple_of((mark ^ (15 - k)) * S, S), S)
+            tiles[tile, part, :] = ref[at * S : (at + 1) * S, cols]
+        store(tile).start()
+    for tile in range(count):
+        store(tile).wait()
 
 
 def place(out, far, near, where, weights, after):
-    block = pl.BlockSpec((ROWS // 2, TILE), lambda i, s: (0, i))
+    whole = pl.BlockSpec(memory_space=pltpu.VMEM)
+    count = far.shape[1] // TILE
     extra = [after] if out is None else [after, out]
     return pl.pallas_call(
         place_kernel,
         out_shape=[jax.ShapeDtypeStruct(weights.shape, BF), TOKEN],
-        grid_spec=pltpu.PrefetchScalarGridSpec(
-            num_scalar_prefetch=1,
-            grid=(far.shape[1] // TILE,),
-            in_specs=[block, block] + [ANY] * len(extra),
-            out_specs=[pl.BlockSpec((ROWS, TILE), lambda i, s: (0, s[1 + i])), ANY],
-        ),
+        in_specs=[pl.BlockSpec(memory_space=pltpu.SMEM), whole, whole] + [ANY] * len(extra),
+        out_specs=[ANY, ANY],
+        scratch_shapes=[
+            pltpu.VMEM((count, ROWS, TILE), BF),
+            pltpu.SemaphoreType.DMA((count,)),
+        ],
         input_output_aliases={} if out is None else {4: 0},
         name="place",
         **params(),

time: 190 us -> 219 us (1.15)
  Pallas kernels: 38.9 us -> 66.1 us
    pallas_call x2, Pallas kernels: 4.16 us -> 34 us  [stack(): pl.pallas_call(stack_kernel, out_shape=[jax.ShapeDtypeStruct((2, *a.shape...]
    pallas_call x4, Pallas kernels: 8.96 us -> 6.28 us  [place(): pl.pallas_call(place_kernel, out_shape=[jax.ShapeDtypeStruct(weights.shap...]
  transfers between devices with their start and end apart: 37 -> 37, of which waited for: 19 -> 19; matrix products, arithmetic and copies ran while one was open for 1% -> 1% of each run, Pallas kernels for 18% -> 22%
where the time goes in v4:
time: 219 us
  waiting for transfers between devices  87.8 us (40%)
  Pallas kernels  66.1 us (30%)
  starting transfers between devices  61.6 us (28%)
  local copies, waits for them, and re-layouts  2.77 us (1%)
    ppermute x32, waiting for transfers between devices, exchange(): return lax.ppermute(value, (axis, 'c'), pairs)  87.5 us
    ppermute x32, starting transfers between devices, exchange(): return lax.ppermute(value, (axis, 'c'), pairs)  59.6 us
    pallas_call x2, Pallas kernels, stack(): pl.pallas_call(stack_kernel, out_shape=[jax.ShapeDtypeStruct((2, *a.shape...  34 us
    pallas_call x4, Pallas kernels, fisher_parts(): pl.pallas_call(fisher_kernel, out_shape=[jax.ShapeDtypeStruct((2, ROWS //...  17.4 us
    pallas_call x16, Pallas kernels, add_up(): pl.pallas_call(merge_kernel if divide else add_kernel, out_shape=[jax.Sha...  8.23 us
    pallas_call x4, Pallas kernels, place(): pl.pallas_call(place_kernel, out_shape=[jax.ShapeDtypeStruct(weights.shap...  6.28 us
  transfers between devices with their start and end apart: 37, of which 19 were waited for; matrix products, arithmetic and copies ran while one was open for 1% of the time, Pallas kernels for 22%

profile of v4, /device:TPU:22, one launch (start us, length us, event | category | flops | bytes accessed | tf_op | source)
XLA Modules:
  0.0 218.8 jit_solution(1338576951909365821)
XLA Ops:
  0.8 1.5 copy.10
  2.3 7.1 %collective-permute-done.1.b = bf16[4,256,256]{2,1,0:T(8,128)(2,1)S(1)} collective-permute-done((bf16[4,256,256]{2,1,0:T(8,128)(2,1)}, bf16[4,256,256]{2,1,0:T(8,128)(2,1)S(1)}, u32[]{:S(2)}, u32[]{:S(2)}) %collective-permute-start.1) | collective-permute-done | bytes 524320 | tf_op jit(solution)/shard_map/ppermute | solution.py:52
  9.4 17.0 %stack.89 = (bf16[2,4,256,256]{3,2,1,0:T(8,128)(2,1)}, f32[8,128]{1,0:T(8,128)S(1)}) custom-call(bf16[4,256,256]{2,1,0:T(8,128)(2,1)} %bitcast.7.a, bf16[4,256,256]{2,1,0:T(8,128)(2,1)S(1)} %collective-permute-done.1.b, bf16[4,512,256]{2,1,0:T(8,128)(2,1)S(1)} %bitcast.22), custom_call_target="tpu_custom_call" | custom-call | flops 1 | bytes 1 | tf_op jit(solution)/shard_map/stack/pallas_call | solution.py:101
  27.1 1.9 collective-permute-start
  29.4 3.8 %fisher_parts.4 = (bf16[2,256,1024]{2,1,0:T(8,128)(2,1)S(1)}, bf16[2,256,1024]{2,1,0:T(8,128)(2,1)S(1)}, f32[8,128]{1,0:T(8,128)S(1)}) custom-call(s32[5]{0:T(128)S(1)} %stack.78.where, bf16[4,512,256]{2,1,0:T(8,128)(2,1)S(1)} %bitcast.23, bf16[2,4,256,256]{3,2,1,0:T(8,128)(2,1)} %get-tuple-element.82.mine, ...), custom_call_target="tpu_custom_call" | custom-call | flops 1 | bytes 1 | tf_op jit(solution)/shard_map/fisher_parts/pallas_call | solution.py:147
  33.2 1.4 collective-permute-start.7
  34.6 8.3 %collective-permute-done.2.value = bf16[2,4,256,256]{3,2,1,0:T(8,128)(2,1)} collective-permute-done((bf16[2,4,256,256]{3,2,1,0:T(8,128)(2,1)}, bf16[2,4,256,256]{3,2,1,0:T(8,128)(2,1)}, u32[]{:S(2)}, u32[]{:S(2)}) %collective-permute-start.2) | collective-permute-done | bytes 1048608 | tf_op jit(solution)/shard_map/ppermute | solution.py:52
  43.1 9.2 %collective-permute-done.4.b = bf16[4,256,256]{2,1,0:T(8,128)(2,1)S(1)} collective-permute-done((bf16[4,256,256]{2,1,0:T(8,128)(2,1)}, bf16[4,256,256]{2,1,0:T(8,128)(2,1)S(1)}, u32[]{:S(2)}, u32[]{:S(2)}) %collective-permute-start.4) | collective-permute-done | bytes 524320 | tf_op jit(solution)/shard_map/ppermute | solution.py:52
  52.3 17.0 %stack.90 = (bf16[2,4,256,256]{3,2,1,0:T(8,128)(2,1)}, f32[8,128]{1,0:T(8,128)S(1)}) custom-call(bf16[4,256,256]{2,1,0:T(8,128)(2,1)} %get-tuple-element.86.a, bf16[4,256,256]{2,1,0:T(8,128)(2,1)S(1)} %collective-permute-done.4.b, f32[8,128]{1,0:T(8,128)S(1)} %get-tuple-element.87.after), custom_call_target="tpu_custom_call" | custom-call | flops 1 | bytes 1 | tf_op jit(solution)/shard_map/stack/pallas_call | solution.py:101
  71.4 5.1 %fisher_parts.5 = (bf16[2,256,1024]{2,1,0:T(8,128)(2,1)}, bf16[2,256,1024]{2,1,0:T(8,128)(2,1)S(1)}, f32[8,128]{1,0:T(8,128)S(1)}) custom-call(s32[5]{0:T(128)S(1)} %stack.83.where, bf16[4,512,256]{2,1,0:T(8,128)(2,1)S(1)} %bitcast.24, bf16[2,4,256,256]{3,2,1,0:T(8,128)(2,1)} %get-tuple-element.93.mine, ...), custom_call_target="tpu_custom_call" | custom-call | flops 1 | bytes 1 | tf_op jit(solution)/shard_map/fisher_parts/pallas_call | solution.py:147
  77.5 2.8 %collective-permute-start.13 = (bf16[2,256,1024]{2,1,0:T(8,128)(2,1)}, bf16[2,256,1024]{2,1,0:T(8,128)(2,1)}, u32[]{:S(2)}, u32[]{:S(2)}) collective-permute-start(bf16[2,256,1024]{2,1,0:T(8,128)(2,1)} %get-tuple-element.103), channel_id=1, source_target_pairs={{0,64},{1,193},{64,0},{65,129},{128,192},{129,65},{192,128},{193,1... | collective-permute-start | bytes 3145736 | tf_op jit(solution)/shard_map/ppermute | solution.py:52
  80.3 1.8 add_up.13
  82.1 3.6 %collective-permute-done.6.value = bf16[2,4,256,256]{3,2,1,0:T(8,128)(2,1)} collective-permute-done((bf16[2,4,256,256]{3,2,1,0:T(8,128)(2,1)}, bf16[2,4,256,256]{3,2,1,0:T(8,128)(2,1)}, u32[]{:S(2)}, u32[]{:S(2)}) %collective-permute-start.6) | collective-permute-done | bytes 1048608 | tf_op jit(solution)/shard_map/ppermute | solution.py:52
  85.7 3.3 %collective-permute-start.12 = (bf16[2,64,1024]{2,1,0:T(8,128)(2,1)}, bf16[2,64,1024]{2,1,0:T(8,128)(2,1)S(1)}, u32[]{:S(2)}, u32[]{:S(2)}) collective-permute-start(bf16[2,64,1024]{2,1,0:T(8,128)(2,1)} %get-tuple-element.101), channel_id=1, source_target_pairs={{0,16},{1,49},{16,0},{17,33},{32,48},{33,17},{48,32},{49,1},{2,18}... | collective-permute-start | bytes 786440 | tf_op jit(solution)/shard_map/ppermute | solution.py:52
  89.2 4.2 %fisher_parts.6 = (bf16[2,256,1024]{2,1,0:T(8,128)(2,1)S(1)}, bf16[2,256,1024]{2,1,0:T(8,128)(2,1)S(1)}, f32[8,128]{1,0:T(8,128)S(1)}) custom-call(s32[5]{0:T(128)S(1)} %stack.73.where, bf16[4,512,256]{2,1,0:T(8,128)(2,1)S(1)} %bitcast.25, bf16[2,4,256,256]{3,2,1,0:T(8,128)(2,1)} %get-tuple-element.88.mine, ...), custom_call_target="tpu_custom_call" | custom-call | flops 1 | bytes 1 | tf_op jit(solution)/shard_map/fisher_parts/pallas_call | solution.py:147
  93.4 1.4 collective-permute-start.10
  94.8 1.2 add_up.14
  96.4 1.1 add_up.15
  97.5 4.2 %fisher_parts.7 = (bf16[2,256,1024]{2,1,0:T(8,128)(2,1)S(1)}, bf16[2,256,1024]{2,1,0:T(8,128)(2,1)S(1)}, f32[8,128]{1,0:T(8,128)S(1)}) custom-call(s32[5]{0:T(128)S(1)} %stack.88.where, bf16[4,512,256]{2,1,0:T(8,128)(2,1)S(1)} %bitcast.26, bf16[2,4,256,256]{3,2,1,0:T(8,128)(2,1)} %get-tuple-element.100.mine, ...), custom_call_target="tpu_custom_call" | custom-call | flops 1 | bytes 1 | tf_op jit(solution)/shard_map/fisher_parts/pallas_call | solution.py:147
  101.7 1.4 collective-permute-start.16
  103.0 6.0 %collective-permute-start.15 = (bf16[2,64,1024]{2,1,0:T(8,128)(2,1)S(1)}, bf16[2,64,1024]{2,1,0:T(8,128)(2,1)S(1)}, u32[]{:S(2)}, u32[]{:S(2)}) collective-permute-start(bf16[2,64,1024]{2,1,0:T(8,128)(2,1)S(1)} %get-tuple-element.109.refs_0_), channel_id=1, source_target_pairs={{0,48},{1,17},{16,32},{17,1},{32,16},{33,49},{48,0},{49,33},{2,50}... | collective-permute-start | bytes 786440 | tf_op jit(solution)/shard_map/ppermute | solution.py:52
  109.2 8.7 %collective-permute-done.17.refs_2_ = bf16[2,128,1024]{2,1,0:T(8,128)(2,1)S(1)} collective-permute-done((bf16[2,128,1024]{2,1,0:T(8,128)(2,1)S(1)}, bf16[2,128,1024]{2,1,0:T(8,128)(2,1)S(1)}, u32[]{:S(2)}, u32[]{:S(2)}) %collective-permute-start.17) | collective-permute-done | bytes 524320 | tf_op jit(solution)/shard_map/ppermute | solution.py:52
  120.0 5.2 %collective-permute-done.16.refs_1_ = bf16[2,256,1024]{2,1,0:T(8,128)(2,1)S(1)} collective-permute-done((bf16[2,256,1024]{2,1,0:T(8,128)(2,1)S(1)}, bf16[2,256,1024]{2,1,0:T(8,128)(2,1)S(1)}, u32[]{:S(2)}, u32[]{:S(2)}) %collective-permute-start.16) | collective-permute-done | bytes 1048608 | tf_op jit(solution)/shard_map/ppermute | solution.py:52
  126.1 1.6 collective-permute-start.14
  127.7 1.6 collective-permute-done.19.refs_3_
  130.3 5.2 %collective-permute-start.21 = (bf16[2,64,1024]{2,1,0:T(8,128)(2,1)S(1)}, bf16[2,64,1024]{2,1,0:T(8,128)(2,1)S(1)}, u32[]{:S(2)}, u32[]{:S(2)}) collective-permute-start(bf16[2,64,1024]{2,1,0:T(8,128)(2,1)S(1)} %get-tuple-element.121.refs_0_), channel_id=1, source_target_pairs={{0,48},{1,17},{16,32},{17,1},{32,16},{33,49},{48,0},{49,33},{2,50}... | collective-permute-start | bytes 786440 | tf_op jit(solution)/shard_map/ppermute | solution.py:52
  136.0 2.0 collective-permute-start.24
  138.0 8.9 %collective-permute-done.21.refs_1_ = bf16[2,64,1024]{2,1,0:T(8,128)(2,1)S(1)} collective-permute-done((bf16[2,64,1024]{2,1,0:T(8,128)(2,1)S(1)}, bf16[2,64,1024]{2,1,0:T(8,128)(2,1)S(1)}, u32[]{:S(2)}, u32[]{:S(2)}) %collective-permute-start.21) | collective-permute-done | bytes 262176 | tf_op jit(solution)/shard_map/ppermute | solution.py:52
  147.1 5.0 %collective-permute-start.29 = (bf16[256,1024]{1,0:T(8,128)(2,1)S(1)}, bf16[256,1024]{1,0:T(8,128)(2,1)S(1)}, u32[]{:S(2)}, u32[]{:S(2)}) collective-permute-start(bf16[256,1024]{1,0:T(8,128)(2,1)S(1)} %get-tuple-element.136.near), channel_id=1, source_target_pairs={{0,64},{1,193},{64,0},{65,129},{128,192},{129,65},{192,128},{193,1... | collective-permute-start | bytes 1572872 | tf_op jit(solution)/shard_map/ppermute | solution.py:52
  152.1 3.0 %collective-permute-start.23 = (bf16[2,64,1024]{2,1,0:T(8,128)(2,1)S(1)}, bf16[2,64,1024]{2,1,0:T(8,128)(2,1)S(1)}, u32[]{:S(2)}, u32[]{:S(2)}) collective-permute-start(bf16[2,64,1024]{2,1,0:T(8,128)(2,1)S(1)} %get-tuple-element.127), channel_id=1, source_target_pairs={{0,16},{1,49},{16,0},{17,33},{32,48},{33,17},{48,32},{49,1},{2,18}... | collective-permute-start | bytes 786440 | tf_op jit(solution)/shard_map/ppermute | solution.py:52
  155.2 4.0 %collective-permute-done.25.a = bf16[64,1024]{1,0:T(8,128)(2,1)S(1)} collective-permute-done((bf16[64,1024]{1,0:T(8,128)(2,1)S(1)}, bf16[64,1024]{1,0:T(8,128)(2,1)S(1)}, u32[]{:S(2)}, u32[]{:S(2)}) %collective-permute-start.25) | collective-permute-done | bytes 131104 | tf_op jit(solution)/shard_map/ppermute | solution.py:52
  159.3 10.7 %collective-permute-start.28 = (bf16[2,64,1024]{2,1,0:T(8,128)(2,1)S(1)}, bf16[2,64,1024]{2,1,0:T(8,128)(2,1)S(1)}, u32[]{:S(2)}, u32[]{:S(2)}) collective-permute-start(bf16[2,64,1024]{2,1,0:T(8,128)(2,1)S(1)} %get-tuple-element.135.refs_0_), channel_id=1, source_target_pairs={{0,48},{1,17},{16,32},{17,1},{32,16},{33,49},{48,0},{49,33},{2,50}... | collective-permute-start | bytes 786440 | tf_op jit(solution)/shard_map/ppermute | solution.py:52
  170.0 2.0 collective-permute-done.23.refs_3_
  172.1 3.6 %collective-permute-start.26 = (bf16[2,64,1024]{2,1,0:T(8,128)(2,1)S(1)}, bf16[2,64,1024]{2,1,0:T(8,128)(2,1)S(1)}, u32[]{:S(2)}, u32[]{:S(2)}) collective-permute-start(bf16[2,64,1024]{2,1,0:T(8,128)(2,1)S(1)} %get-tuple-element.133.refs_0_), channel_id=1, source_target_pairs={{0,48},{1,17},{16,32},{17,1},{32,16},{33,49},{48,0},{49,33},{2,50}... | collective-permute-start | bytes 786440 | tf_op jit(solution)/shard_map/ppermute | solution.py:52
  175.7 1.6 place.4
  177.3 6.1 %collective-permute-done.28.refs_1_ = bf16[2,64,1024]{2,1,0:T(8,128)(2,1)S(1)} collective-permute-done((bf16[2,64,1024]{2,1,0:T(8,128)(2,1)S(1)}, bf16[2,64,1024]{2,1,0:T(8,128)(2,1)S(1)}, u32[]{:S(2)}, u32[]{:S(2)}) %collective-permute-start.28) | collective-permute-done | bytes 262176 | tf_op jit(solution)/shard_map/ppermute | solution.py:52
  183.8 4.3 %collective-permute-done.26.refs_1_ = bf16[2,64,1024]{2,1,0:T(8,128)(2,1)S(1)} collective-permute-done((bf16[2,64,1024]{2,1,0:T(8,128)(2,1)S(1)}, bf16[2,64,1024]{2,1,0:T(8,128)(2,1)S(1)}, u32[]{:S(2)}, u32[]{:S(2)}) %collective-permute-start.26) | collective-permute-done | bytes 262176 | tf_op jit(solution)/shard_map/ppermute | solution.py:52
  188.2 4.7 %collective-permute-start.30 = (bf16[64,1024]{1,0:T(8,128)(2,1)S(1)}, bf16[64,1024]{1,0:T(8,128)(2,1)S(1)}, u32[]{:S(2)}, u32[]{:S(2)}) collective-permute-start(bf16[64,1024]{1,0:T(8,128)(2,1)S(1)} %get-tuple-element.141.b), channel_id=1, source_target_pairs={{0,16},{1,49},{16,0},{17,33},{32,48},{33,17},{48,32},{49,1},{2,18}... | collective-permute-start | bytes 393224 | tf_op jit(solution)/shard_map/ppermute | solution.py:52
  193.0 2.8 %collective-permute-done.30.a = bf16[64,1024]{1,0:T(8,128)(2,1)S(1)} collective-permute-done((bf16[64,1024]{1,0:T(8,128)(2,1)S(1)}, bf16[64,1024]{1,0:T(8,128)(2,1)S(1)}, u32[]{:S(2)}, u32[]{:S(2)}) %collective-permute-start.30) | collective-permute-done | bytes 131104 | tf_op jit(solution)/shard_map/ppermute | solution.py:52
  196.0 6.1 %collective-permute-done.34.a = bf16[128,1024]{1,0:T(8,128)(2,1)S(1)} collective-permute-done((bf16[128,1024]{1,0:T(8,128)(2,1)S(1)}, bf16[128,1024]{1,0:T(8,128)(2,1)S(1)}, u32[]{:S(2)}, u32[]{:S(2)}) %collective-permute-start.34) | collective-permute-done | bytes 262176 | tf_op jit(solution)/shard_map/ppermute | solution.py:52
  202.2 1.4 collective-permute-start.36
  203.5 1.6 place.5
  205.1 2.6 %collective-permute-done.32.a = bf16[128,1024]{1,0:T(8,128)(2,1)S(1)} collective-permute-done((bf16[128,1024]{1,0:T(8,128)(2,1)S(1)}, bf16[128,1024]{1,0:T(8,128)(2,1)S(1)}, u32[]{:S(2)}, u32[]{:S(2)}) %collective-permute-start.32) | collective-permute-done | bytes 262176 | tf_op jit(solution)/shard_map/ppermute | solution.py:52
  207.8 1.4 collective-permute-start.35
  209.1 2.3 %collective-permute-done.36.far = bf16[256,1024]{1,0:T(8,128)(2,1)S(1)} collective-permute-done((bf16[256,1024]{1,0:T(8,128)(2,1)S(1)}, bf16[256,1024]{1,0:T(8,128)(2,1)S(1)}, u32[]{:S(2)}, u32[]{:S(2)}) %collective-permute-start.36) | collective-permute-done | bytes 524320 | tf_op jit(solution)/shard_map/ppermute | solution.py:52
  211.4 1.6 place.6
  213.0 4.0 %collective-permute-done.35.far = bf16[256,1024]{1,0:T(8,128)(2,1)S(1)} collective-permute-done((bf16[256,1024]{1,0:T(8,128)(2,1)S(1)}, bf16[256,1024]{1,0:T(8,128)(2,1)S(1)}, u32[]{:S(2)}, u32[]{:S(2)}) %collective-permute-start.35) | collective-permute-done | bytes 524320 | tf_op jit(solution)/shard_map/ppermute | solution.py:52
  217.1 1.6 place.7
  (72 shorter events, 11.5 us)
Async XLA Ops:
  0.0 9.4 %collective-permute-start.1 = (bf16[4,256,256]{2,1,0:T(8,128)(2,1)}, bf16[4,256,256]{2,1,0:T(8,128)(2,1)S(1)}, u32[]{:S(2)}, u32[]{:S(2)}) collective-permute-start(bf16[4,256,256]{2,1,0:T(8,128)(2,1)} %bitcast.7.a), channel_id=1, source_target_pairs={{0,2},{1,7},{2,0},{3,5},{4,6},{5,3},{6,4},{7,1},{8,10},{9,15},{10,... | collective-permute-start | bytes 1572872 | tf_op jit(solution)/shard_map/ppermute | solution.py:52
  26.4 3.0 %collective-permute-start.3 = (bf16[2,4,256,256]{3,2,1,0:T(8,128)(2,1)}, bf16[2,4,256,256]{3,2,1,0:T(8,128)(2,1)S(1)}, u32[]{:S(2)}, u32[]{:S(2)}) collective-permute-start(bf16[2,4,256,256]{3,2,1,0:T(8,128)(2,1)} %get-tuple-element.82.mine), channel_id=1, source_target_pairs={{0,1},{1,0},{2,3},{3,2},{4,5},{5,4},{6,7},{7,6},{8,9},{9,8},{10,11... | collective-permute-start | bytes 3145736 | tf_op jit(solution)/shard_map/ppermute | solution.py:56
  26.5 16.4 %collective-permute-start.2 = (bf16[2,4,256,256]{3,2,1,0:T(8,128)(2,1)}, bf16[2,4,256,256]{3,2,1,0:T(8,128)(2,1)}, u32[]{:S(2)}, u32[]{:S(2)}) collective-permute-start(bf16[2,4,256,256]{3,2,1,0:T(8,128)(2,1)} %get-tuple-element.82.mine), channel_id=1, source_target_pairs={{0,6},{1,3},{2,4},{3,1},{4,2},{5,7},{6,0},{7,5},{8,14},{9,11},{10,... | collective-permute-start | bytes 3145736 | tf_op jit(solution)/shard_map/ppermute | solution.py:52
  27.1 15.9 %collective-permute-start = (bf16[4,256,256]{2,1,0:T(8,128)(2,1)}, bf16[4,256,256]{2,1,0:T(8,128)(2,1)}, u32[]{:S(2)}, u32[]{:S(2)}) collective-permute-start(bf16[4,256,256]{2,1,0:T(8,128)(2,1)} %bitcast.7.a), channel_id=1, source_target_pairs={{0,8},{8,0},{1,9},{9,1},{2,10},{10,2},{3,11},{11,3},{4,12},{12,4},... | collective-permute-start | bytes 1572872 | tf_op jit(solution)/shard_map/ppermute | solution.py:56
  33.2 36.7 %collective-permute-start.7 = (bf16[2,256,1024]{2,1,0:T(8,128)(2,1)S(1)}, bf16[2,256,1024]{2,1,0:T(8,128)(2,1)S(1)}, u32[]{:S(2)}, u32[]{:S(2)}) collective-permute-start(bf16[2,256,1024]{2,1,0:T(8,128)(2,1)S(1)} %get-tuple-element.90), channel_id=1, source_target_pairs={{0,64},{1,193},{64,0},{65,129},{128,192},{129,65},{192,128},{193,1... | collective-permute-start | bytes 3145736 | tf_op jit(solution)/shard_map/ppermute | solution.py:52
  42.9 9.4 %collective-permute-start.4 = (bf16[4,256,256]{2,1,0:T(8,128)(2,1)}, bf16[4,256,256]{2,1,0:T(8,128)(2,1)S(1)}, u32[]{:S(2)}, u32[]{:S(2)}) collective-permute-start(bf16[4,256,256]{2,1,0:T(8,128)(2,1)} %get-tuple-element.86.a), channel_id=1, source_target_pairs={{0,2},{1,7},{2,0},{3,5},{4,6},{5,3},{6,4},{7,1},{8,10},{9,15},{10,... | collective-permute-start | bytes 1572872 | tf_op jit(solution)/shard_map/ppermute | solution.py:52
  43.1 28.3 %collective-permute-start.9 = (bf16[2,4,256,256]{3,2,1,0:T(8,128)(2,1)}, bf16[2,4,256,256]{3,2,1,0:T(8,128)(2,1)}, u32[]{:S(2)}, u32[]{:S(2)}) collective-permute-start(bf16[2,4,256,256]{3,2,1,0:T(8,128)(2,1)} %get-tuple-element.93.mine), channel_id=1, source_target_pairs={{0,1},{1,0},{2,3},{3,2},{4,5},{5,4},{6,7},{7,6},{8,9},{9,8},{10,11... | collective-permute-start | bytes 3145736 | tf_op jit(solution)/shard_map/ppermute | solution.py:56
  69.3 16.4 %collective-permute-start.6 = (bf16[2,4,256,256]{3,2,1,0:T(8,128)(2,1)}, bf16[2,4,256,256]{3,2,1,0:T(8,128)(2,1)}, u32[]{:S(2)}, u32[]{:S(2)}) collective-permute-start(bf16[2,4,256,256]{3,2,1,0:T(8,128)(2,1)} %get-tuple-element.88.mine), channel_id=1, source_target_pairs={{0,6},{1,3},{2,4},{3,1},{4,2},{5,7},{6,0},{7,5},{8,14},{9,11},{10,... | collective-permute-start | bytes 3145736 | tf_op jit(solution)/shard_map/ppermute | solution.py:52
  70.8 9.5 %collective-permute-start.8 = (bf16[2,128,1024]{2,1,0:T(8,128)(2,1)}, bf16[2,128,1024]{2,1,0:T(8,128)(2,1)}, u32[]{:S(2)}, u32[]{:S(2)}) collective-permute-start(bf16[2,128,1024]{2,1,0:T(8,128)(2,1)} %get-tuple-element.92), channel_id=1, source_target_pairs={{0,192},{1,65},{64,128},{65,1},{128,64},{129,193},{192,0},{193,129... | collective-permute-start | bytes 1572872 | tf_op jit(solution)/shard_map/ppermute | solution.py:52
  71.4 17.8 %collective-permute-start.5 = (bf16[2,4,256,256]{3,2,1,0:T(8,128)(2,1)}, bf16[2,4,256,256]{3,2,1,0:T(8,128)(2,1)}, u32[]{:S(2)}, u32[]{:S(2)}) collective-permute-start(bf16[2,4,256,256]{3,2,1,0:T(8,128)(2,1)} %get-tuple-element.88.mine), channel_id=1, source_target_pairs={{0,1},{1,0},{2,3},{3,2},{4,5},{5,4},{6,7},{7,6},{8,9},{9,8},{10,11... | collective-permute-start | bytes 3145736 | tf_op jit(solution)/shard_map/ppermute | solution.py:56
  76.5 1.0 copy-start
  77.5 17.3 %collective-permute-start.13 = (bf16[2,256,1024]{2,1,0:T(8,128)(2,1)}, bf16[2,256,1024]{2,1,0:T(8,128)(2,1)}, u32[]{:S(2)}, u32[]{:S(2)}) collective-permute-start(bf16[2,256,1024]{2,1,0:T(8,128)(2,1)} %get-tuple-element.103), channel_id=1, source_target_pairs={{0,64},{1,193},{64,0},{65,129},{128,192},{129,65},{192,128},{193,1... | collective-permute-start | bytes 3145736 | tf_op jit(solution)/shard_map/ppermute | solution.py:52
  85.7 11.8 %collective-permute-start.11 = (bf16[2,4,256,256]{3,2,1,0:T(8,128)(2,1)}, bf16[2,4,256,256]{3,2,1,0:T(8,128)(2,1)}, u32[]{:S(2)}, u32[]{:S(2)}) collective-permute-start(bf16[2,4,256,256]{3,2,1,0:T(8,128)(2,1)} %get-tuple-element.100.mine), channel_id=1, source_target_pairs={{0,1},{1,0},{2,3},{3,2},{4,5},{5,4},{6,7},{7,6},{8,9},{9,8},{10,11... | collective-permute-start | bytes 3145736 | tf_op jit(solution)/shard_map/ppermute | solution.py:56
  85.7 10.6 %collective-permute-start.12 = (bf16[2,64,1024]{2,1,0:T(8,128)(2,1)}, bf16[2,64,1024]{2,1,0:T(8,128)(2,1)S(1)}, u32[]{:S(2)}, u32[]{:S(2)}) collective-permute-start(bf16[2,64,1024]{2,1,0:T(8,128)(2,1)} %get-tuple-element.101), channel_id=1, source_target_pairs={{0,16},{1,49},{16,0},{17,33},{32,48},{33,17},{48,32},{49,1},{2,18}... | collective-permute-start | bytes 786440 | tf_op jit(solution)/shard_map/ppermute | solution.py:52
  89.2 5.6 %copy-start.1 = (bf16[2,256,1024]{2,1,0:T(8,128)(2,1)S(1)}, bf16[2,256,1024]{2,1,0:T(8,128)(2,1)}, u32[]{:S(2)}) copy-start(bf16[2,256,1024]{2,1,0:T(8,128)(2,1)} %copy-done) | copy-start | bytes 3145732
  93.4 15.6 %collective-permute-start.10 = (bf16[2,256,1024]{2,1,0:T(8,128)(2,1)S(1)}, bf16[2,256,1024]{2,1,0:T(8,128)(2,1)S(1)}, u32[]{:S(2)}, u32[]{:S(2)}) collective-permute-start(bf16[2,256,1024]{2,1,0:T(8,128)(2,1)S(1)} %get-tuple-element.99), channel_id=1, source_target_pairs={{0,64},{1,193},{64,0},{65,129},{128,192},{129,65},{192,128},{193,1... | collective-permute-start | bytes 3145736 | tf_op jit(solution)/shard_map/ppermute | solution.py:52
  101.7 23.5 %collective-permute-start.16 = (bf16[2,256,1024]{2,1,0:T(8,128)(2,1)S(1)}, bf16[2,256,1024]{2,1,0:T(8,128)(2,1)S(1)}, u32[]{:S(2)}, u32[]{:S(2)}) collective-permute-start(bf16[2,256,1024]{2,1,0:T(8,128)(2,1)S(1)} %get-tuple-element.111), channel_id=1, source_target_pairs={{0,64},{1,193},{64,0},{65,129},{128,192},{129,65},{192,128},{193,1... | collective-permute-start | bytes 3145736 | tf_op jit(solution)/shard_map/ppermute | solution.py:52
  103.0 14.9 %collective-permute-start.17 = (bf16[2,128,1024]{2,1,0:T(8,128)(2,1)S(1)}, bf16[2,128,1024]{2,1,0:T(8,128)(2,1)S(1)}, u32[]{:S(2)}, u32[]{:S(2)}) collective-permute-start(bf16[2,128,1024]{2,1,0:T(8,128)(2,1)S(1)} %get-tuple-element.112), channel_id=1, source_target_pairs={{0,192},{1,65},{64,128},{65,1},{128,64},{129,193},{192,0},{193,129... | collective-permute-start | bytes 1572872 | tf_op jit(solution)/shard_map/ppermute | solution.py:52
  103.0 22.8 %collective-permute-start.15 = (bf16[2,64,1024]{2,1,0:T(8,128)(2,1)S(1)}, bf16[2,64,1024]{2,1,0:T(8,128)(2,1)S(1)}, u32[]{:S(2)}, u32[]{:S(2)}) collective-permute-start(bf16[2,64,1024]{2,1,0:T(8,128)(2,1)S(1)} %get-tuple-element.109.refs_0_), channel_id=1, source_target_pairs={{0,48},{1,17},{16,32},{17,1},{32,16},{33,49},{48,0},{49,33},{2,50}... | collective-permute-start | bytes 786440 | tf_op jit(solution)/shard_map/ppermute | solution.py:52
  119.0 10.3 %collective-permute-start.19 = (bf16[2,64,1024]{2,1,0:T(8,128)(2,1)S(1)}, bf16[2,64,1024]{2,1,0:T(8,128)(2,1)S(1)}, u32[]{:S(2)}, u32[]{:S(2)}) collective-permute-start(bf16[2,64,1024]{2,1,0:T(8,128)(2,1)S(1)} %get-tuple-element.117), channel_id=1, source_target_pairs={{0,16},{1,49},{16,0},{17,33},{32,48},{33,17},{48,32},{49,1},{2,18}... | collective-permute-start | bytes 786440 | tf_op jit(solution)/shard_map/ppermute | solution.py:52
  125.3 10.7 %collective-permute-start.22 = (bf16[2,128,1024]{2,1,0:T(8,128)(2,1)S(1)}, bf16[2,128,1024]{2,1,0:T(8,128)(2,1)S(1)}, u32[]{:S(2)}, u32[]{:S(2)}) collective-permute-start(bf16[2,128,1024]{2,1,0:T(8,128)(2,1)S(1)} %get-tuple-element.122), channel_id=1, source_target_pairs={{0,192},{1,65},{64,128},{65,1},{128,64},{129,193},{192,0},{193,129... | collective-permute-start | bytes 1572872 | tf_op jit(solution)/shard_map/ppermute | solution.py:52
  125.9 9.6 %collective-permute-start.18 = (bf16[64,1024]{1,0:T(8,128)(2,1)S(1)}, bf16[64,1024]{1,0:T(8,128)(2,1)S(1)}, u32[]{:S(2)}, u32[]{:S(2)}) collective-permute-start(bf16[64,1024]{1,0:T(8,128)(2,1)S(1)} %get-tuple-element.116.b), channel_id=1, source_target_pairs={{0,16},{1,49},{16,0},{17,33},{32,48},{33,17},{48,32},{49,1},{2,18}... | collective-permute-start | bytes 393224 | tf_op jit(solution)/shard_map/ppermute | solution.py:52
  126.1 26.0 %collective-permute-start.14 = (bf16[2,128,1024]{2,1,0:T(8,128)(2,1)S(1)}, bf16[2,128,1024]{2,1,0:T(8,128)(2,1)S(1)}, u32[]{:S(2)}, u32[]{:S(2)}) collective-permute-start(bf16[2,128,1024]{2,1,0:T(8,128)(2,1)S(1)} %get-tuple-element.108), channel_id=1, source_target_pairs={{0,192},{1,65},{64,128},{65,1},{128,64},{129,193},{192,0},{193,129... | collective-permute-start | bytes 1572872 | tf_op jit(solution)/shard_map/ppermute | solution.py:52
  130.3 16.6 %collective-permute-start.21 = (bf16[2,64,1024]{2,1,0:T(8,128)(2,1)S(1)}, bf16[2,64,1024]{2,1,0:T(8,128)(2,1)S(1)}, u32[]{:S(2)}, u32[]{:S(2)}) collective-permute-start(bf16[2,64,1024]{2,1,0:T(8,128)(2,1)S(1)} %get-tuple-element.121.refs_0_), channel_id=1, source_target_pairs={{0,48},{1,17},{16,32},{17,1},{32,16},{33,49},{48,0},{49,33},{2,50}... | collective-permute-start | bytes 786440 | tf_op jit(solution)/shard_map/ppermute | solution.py:52
  135.6 11.4 %collective-permute-start.20 = (bf16[128,1024]{1,0:T(8,128)(2,1)S(1)}, bf16[128,1024]{1,0:T(8,128)(2,1)S(1)}, u32[]{:S(2)}, u32[]{:S(2)}) collective-permute-start(bf16[128,1024]{1,0:T(8,128)(2,1)S(1)} %get-tuple-element.120.b), channel_id=1, source_target_pairs={{0,192},{1,65},{64,128},{65,1},{128,64},{129,193},{192,0},{193,129... | collective-permute-start | bytes 786440 | tf_op jit(solution)/shard_map/ppermute | solution.py:52
  136.0 23.1 %collective-permute-start.24 = (bf16[2,64,1024]{2,1,0:T(8,128)(2,1)S(1)}, bf16[2,64,1024]{2,1,0:T(8,128)(2,1)S(1)}, u32[]{:S(2)}, u32[]{:S(2)}) collective-permute-start(bf16[2,64,1024]{2,1,0:T(8,128)(2,1)S(1)} %get-tuple-element.128), channel_id=1, source_target_pairs={{0,16},{1,49},{16,0},{17,33},{32,48},{33,17},{48,32},{49,1},{2,18}... | collective-permute-start | bytes 786440 | tf_op jit(solution)/shard_map/ppermute | solution.py:52
  147.1 28.7 %collective-permute-start.29 = (bf16[256,1024]{1,0:T(8,128)(2,1)S(1)}, bf16[256,1024]{1,0:T(8,128)(2,1)S(1)}, u32[]{:S(2)}, u32[]{:S(2)}) collective-permute-start(bf16[256,1024]{1,0:T(8,128)(2,1)S(1)} %get-tuple-element.136.near), channel_id=1, source_target_pairs={{0,64},{1,193},{64,0},{65,129},{128,192},{129,65},{192,128},{193,1... | collective-permute-start | bytes 1572872 | tf_op jit(solution)/shard_map/ppermute | solution.py:52
  152.0 7.1 %collective-permute-start.25 = (bf16[64,1024]{1,0:T(8,128)(2,1)S(1)}, bf16[64,1024]{1,0:T(8,128)(2,1)S(1)}, u32[]{:S(2)}, u32[]{:S(2)}) collective-permute-start(bf16[64,1024]{1,0:T(8,128)(2,1)S(1)} %get-tuple-element.129.b), channel_id=1, source_target_pairs={{0,16},{1,49},{16,0},{17,33},{32,48},{33,17},{48,32},{49,1},{2,18}... | collective-permute-start | bytes 393224 | tf_op jit(solution)/shard_map/ppermute | solution.py:52
  152.1 19.8 %collective-permute-start.23 = (bf16[2,64,1024]{2,1,0:T(8,128)(2,1)S(1)}, bf16[2,64,1024]{2,1,0:T(8,128)(2,1)S(1)}, u32[]{:S(2)}, u32[]{:S(2)}) collective-permute-start(bf16[2,64,1024]{2,1,0:T(8,128)(2,1)S(1)} %get-tuple-element.127), channel_id=1, source_target_pairs={{0,16},{1,49},{16,0},{17,33},{32,48},{33,17},{48,32},{49,1},{2,18}... | collective-permute-start | bytes 786440 | tf_op jit(solution)/shard_map/ppermute | solution.py:52
  159.3 24.1 %collective-permute-start.28 = (bf16[2,64,1024]{2,1,0:T(8,128)(2,1)S(1)}, bf16[2,64,1024]{2,1,0:T(8,128)(2,1)S(1)}, u32[]{:S(2)}, u32[]{:S(2)}) collective-permute-start(bf16[2,64,1024]{2,1,0:T(8,128)(2,1)S(1)} %get-tuple-element.135.refs_0_), channel_id=1, source_target_pairs={{0,48},{1,17},{16,32},{17,1},{32,16},{33,49},{48,0},{49,33},{2,50}... | collective-permute-start | bytes 786440 | tf_op jit(solution)/shard_map/ppermute | solution.py:52
  170.0 13.5 %collective-permute-start.27 = (bf16[128,1024]{1,0:T(8,128)(2,1)S(1)}, bf16[128,1024]{1,0:T(8,128)(2,1)S(1)}, u32[]{:S(2)}, u32[]{:S(2)}) collective-permute-start(bf16[128,1024]{1,0:T(8,128)(2,1)S(1)} %get-tuple-element.134.b), channel_id=1, source_target_pairs={{0,192},{1,65},{64,128},{65,1},{128,64},{129,193},{192,0},{193,129... | collective-permute-start | bytes 786440 | tf_op jit(solution)/shard_map/ppermute | solution.py:52
  172.1 16.0 %collective-permute-start.26 = (bf16[2,64,1024]{2,1,0:T(8,128)(2,1)S(1)}, bf16[2,64,1024]{2,1,0:T(8,128)(2,1)S(1)}, u32[]{:S(2)}, u32[]{:S(2)}) collective-permute-start(bf16[2,64,1024]{2,1,0:T(8,128)(2,1)S(1)} %get-tuple-element.133.refs_0_), channel_id=1, source_target_pairs={{0,48},{1,17},{16,32},{17,1},{32,16},{33,49},{48,0},{49,33},{2,50}... | collective-permute-start | bytes 786440 | tf_op jit(solution)/shard_map/ppermute | solution.py:52
  183.6 19.9 %collective-permute-start.33 = (bf16[256,1024]{1,0:T(8,128)(2,1)S(1)}, bf16[256,1024]{1,0:T(8,128)(2,1)S(1)}, u32[]{:S(2)}, u32[]{:S(2)}) collective-permute-start(bf16[256,1024]{1,0:T(8,128)(2,1)S(1)} %get-tuple-element.146.near), channel_id=1, source_target_pairs={{0,64},{1,193},{64,0},{65,129},{128,192},{129,65},{192,128},{193,1... | collective-permute-start | bytes 1572872 | tf_op jit(solution)/shard_map/ppermute | solution.py:52
  183.7 9.2 %collective-permute-start.31 = (bf16[64,1024]{1,0:T(8,128)(2,1)S(1)}, bf16[64,1024]{1,0:T(8,128)(2,1)S(1)}, u32[]{:S(2)}, u32[]{:S(2)}) collective-permute-start(bf16[64,1024]{1,0:T(8,128)(2,1)S(1)} %get-tuple-element.142.b), channel_id=1, source_target_pairs={{0,16},{1,49},{16,0},{17,33},{32,48},{33,17},{48,32},{49,1},{2,18}... | collective-permute-start | bytes 393224 | tf_op jit(solution)/shard_map/ppermute | solution.py:52
  188.2 7.7 %collective-permute-start.30 = (bf16[64,1024]{1,0:T(8,128)(2,1)S(1)}, bf16[64,1024]{1,0:T(8,128)(2,1)S(1)}, u32[]{:S(2)}, u32[]{:S(2)}) collective-permute-start(bf16[64,1024]{1,0:T(8,128)(2,1)S(1)} %get-tuple-element.141.b), channel_id=1, source_target_pairs={{0,16},{1,49},{16,0},{17,33},{32,48},{33,17},{48,32},{49,1},{2,18}... | collective-permute-start | bytes 393224 | tf_op jit(solution)/shard_map/ppermute | solution.py:52
  192.9 9.2 %collective-permute-start.34 = (bf16[128,1024]{1,0:T(8,128)(2,1)S(1)}, bf16[128,1024]{1,0:T(8,128)(2,1)S(1)}, u32[]{:S(2)}, u32[]{:S(2)}) collective-permute-start(bf16[128,1024]{1,0:T(8,128)(2,1)S(1)} %get-tuple-element.147.b), channel_id=1, source_target_pairs={{0,192},{1,65},{64,128},{65,1},{128,64},{129,193},{192,0},{193,129... | collective-permute-start | bytes 786440 | tf_op jit(solution)/shard_map/ppermute | solution.py:52
  195.9 11.9 %collective-permute-start.32 = (bf16[128,1024]{1,0:T(8,128)(2,1)S(1)}, bf16[128,1024]{1,0:T(8,128)(2,1)S(1)}, u32[]{:S(2)}, u32[]{:S(2)}) collective-permute-start(bf16[128,1024]{1,0:T(8,128)(2,1)S(1)} %get-tuple-element.145.b), channel_id=1, source_target_pairs={{0,192},{1,65},{64,128},{65,1},{128,64},{129,193},{192,0},{193,129... | collective-permute-start | bytes 786440 | tf_op jit(solution)/shard_map/ppermute | solution.py:52
  202.2 9.3 %collective-permute-start.36 = (bf16[256,1024]{1,0:T(8,128)(2,1)S(1)}, bf16[256,1024]{1,0:T(8,128)(2,1)S(1)}, u32[]{:S(2)}, u32[]{:S(2)}) collective-permute-start(bf16[256,1024]{1,0:T(8,128)(2,1)S(1)} %get-tuple-element.153.near), channel_id=1, source_target_pairs={{0,64},{1,193},{64,0},{65,129},{128,192},{129,65},{192,128},{193,1... | collective-permute-start | bytes 1572872 | tf_op jit(solution)/shard_map/ppermute | solution.py:52
  207.8 9.3 %collective-permute-start.35 = (bf16[256,1024]{1,0:T(8,128)(2,1)S(1)}, bf16[256,1024]{1,0:T(8,128)(2,1)S(1)}, u32[]{:S(2)}, u32[]{:S(2)}) collective-permute-start(bf16[256,1024]{1,0:T(8,128)(2,1)S(1)} %get-tuple-element.152.near), channel_id=1, source_target_pairs={{0,64},{1,193},{64,0},{65,129},{128,192},{129,65},{192,128},{193,1... | collective-permute-start | bytes 1572872 | tf_op jit(solution)/shard_map/ppermute | solution.py:52

commit v5 on v4

--- a/solution.py
+++ b/solution.py
@@ -87,23 +87,18 @@
     )(value, after)
 
 
-def stack_kernel(a, b, after, out, token, sems):
-    copies = [
-        pltpu.make_async_copy(ref, out.at[at], sems.at[at]) for at, ref in enumerate((a, b))
-    ]
-    for copy in copies:
-        copy.start()
-    for copy in copies:
-        copy.wait()
+def stack_kernel(a, b, after, out, token):
+    out[0] = a[...]
+    out[1] = b[...]
 
 
 def stack(a, b, after):
+    whole = pl.BlockSpec(memory_space=pltpu.VMEM)
     return pl.pallas_call(
         stack_kernel,
         out_shape=[jax.ShapeDtypeStruct((2, *a.shape), BF), TOKEN],
-        in_specs=[ANY, ANY, ANY],
-        out_specs=[ANY, ANY],
-        scratch_shapes=[pltpu.SemaphoreType.DMA((2,))],
+        in_specs=[whole, whole, ANY],
+        out_specs=[whole, ANY],
         name="stack",
         **params(),
     )(a, b, after)

time: 219 us -> 189 us (0.86)
  Pallas kernels: 66.1 us -> 36.2 us
    pallas_call x2, Pallas kernels: 34 us -> 4.16 us  [stack(): pl.pallas_call(stack_kernel, out_shape=[jax.ShapeDtypeStruct((2, *a.shape...]
  transfers between devices with their start and end apart: 37 -> 37, of which waited for: 19 -> 19; matrix products, arithmetic and copies ran while one was open for 1% -> 1% of each run, Pallas kernels for 22% -> 17%
where the time goes in v5:
time: 189 us
  waiting for transfers between devices  87.9 us (47%)
  starting transfers between devices  61.3 us (32%)
  Pallas kernels  36.2 us (19%)
  local copies, waits for them, and re-layouts  2.77 us (1%)
    ppermute x32, waiting for transfers between devices, exchange(): return lax.ppermute(value, (axis, 'c'), pairs)  87.5 us
    ppermute x32, starting transfers between devices, exchange(): return lax.ppermute(value, (axis, 'c'), pairs)  59.3 us
    pallas_call x4, Pallas kernels, fisher_parts(): pl.pallas_call(fisher_kernel, out_shape=[jax.ShapeDtypeStruct((2, ROWS //...  17.4 us
    pallas_call x16, Pallas kernels, add_up(): pl.pallas_call(merge_kernel if divide else add_kernel, out_shape=[jax.Sha...  8.23 us
    pallas_call x4, Pallas kernels, place(): pl.pallas_call(place_kernel, out_shape=[jax.ShapeDtypeStruct(weights.shap...  6.28 us
    pallas_call x2, Pallas kernels, stack(): pl.pallas_call(stack_kernel, out_shape=[jax.ShapeDtypeStruct((2, *a.shape...  4.16 us
  transfers between devices with their start and end apart: 37, of which 19 were waited for; matrix products, arithmetic and copies ran while one was open for 1% of the time, Pallas kernels for 17%

profile of v5, /device:TPU:22, one launch (start us, length us, event | category | flops | bytes accessed | tf_op | source)
XLA Modules:
  0.0 188.7 jit_solution(3239839709017328919)
XLA Ops:
  0.8 1.5 copy.10
  2.3 7.1 %collective-permute-done.1.b = bf16[4,256,256]{2,1,0:T(8,128)(2,1)S(1)} collective-permute-done((bf16[4,256,256]{2,1,0:T(8,128)(2,1)}, bf16[4,256,256]{2,1,0:T(8,128)(2,1)S(1)}, u32[]{:S(2)}, u32[]{:S(2)}) %collective-permute-start.1) | collective-permute-done | bytes 524320 | tf_op jit(solution)/shard_map/ppermute | solution.py:52
  9.4 2.1 %stack.89 = (bf16[2,4,256,256]{3,2,1,0:T(8,128)(2,1)}, f32[8,128]{1,0:T(8,128)S(1)}) custom-call(bf16[4,256,256]{2,1,0:T(8,128)(2,1)} %bitcast.7.a, bf16[4,256,256]{2,1,0:T(8,128)(2,1)S(1)} %collective-permute-done.1.b, bf16[4,512,256]{2,1,0:T(8,128)(2,1)S(1)} %bitcast.22), custom_call_target="tpu_custom_call" | custom-call | flops 1 | bytes 1 | tf_op jit(solution)/shard_map/stack/pallas_call | solution.py:97
  12.0 1.9 %collective-permute-start = (bf16[4,256,256]{2,1,0:T(8,128)(2,1)}, bf16[4,256,256]{2,1,0:T(8,128)(2,1)}, u32[]{:S(2)}, u32[]{:S(2)}) collective-permute-start(bf16[4,256,256]{2,1,0:T(8,128)(2,1)} %bitcast.7.a), channel_id=1, source_target_pairs={{0,8},{8,0},{1,9},{9,1},{2,10},{10,2},{3,11},{11,3},{4,12},{12,4},... | collective-permute-start | bytes 1572872 | tf_op jit(solution)/shard_map/ppermute | solution.py:56
  14.3 3.8 %fisher_parts.4 = (bf16[2,256,1024]{2,1,0:T(8,128)(2,1)S(1)}, bf16[2,256,1024]{2,1,0:T(8,128)(2,1)S(1)}, f32[8,128]{1,0:T(8,128)S(1)}) custom-call(s32[5]{0:T(128)S(1)} %stack.78.where, bf16[4,512,256]{2,1,0:T(8,128)(2,1)S(1)} %bitcast.23, bf16[2,4,256,256]{3,2,1,0:T(8,128)(2,1)} %get-tuple-element.82.mine, ...), custom_call_target="tpu_custom_call" | custom-call | flops 1 | bytes 1 | tf_op jit(solution)/shard_map/fisher_parts/pallas_call | solution.py:142
  18.2 1.4 collective-permute-start.7
  19.6 8.2 %collective-permute-done.2.value = bf16[2,4,256,256]{3,2,1,0:T(8,128)(2,1)} collective-permute-done((bf16[2,4,256,256]{3,2,1,0:T(8,128)(2,1)}, bf16[2,4,256,256]{3,2,1,0:T(8,128)(2,1)}, u32[]{:S(2)}, u32[]{:S(2)}) %collective-permute-start.2) | collective-permute-done | bytes 1048608 | tf_op jit(solution)/shard_map/ppermute | solution.py:52
  27.9 9.3 %collective-permute-done.4.b = bf16[4,256,256]{2,1,0:T(8,128)(2,1)S(1)} collective-permute-done((bf16[4,256,256]{2,1,0:T(8,128)(2,1)}, bf16[4,256,256]{2,1,0:T(8,128)(2,1)S(1)}, u32[]{:S(2)}, u32[]{:S(2)}) %collective-permute-start.4) | collective-permute-done | bytes 524320 | tf_op jit(solution)/shard_map/ppermute | solution.py:52
  37.2 2.1 %stack.90 = (bf16[2,4,256,256]{3,2,1,0:T(8,128)(2,1)}, f32[8,128]{1,0:T(8,128)S(1)}) custom-call(bf16[4,256,256]{2,1,0:T(8,128)(2,1)} %get-tuple-element.86.a, bf16[4,256,256]{2,1,0:T(8,128)(2,1)S(1)} %collective-permute-done.4.b, f32[8,128]{1,0:T(8,128)S(1)} %get-tuple-element.87.after), custom_call_target="tpu_custom_call" | custom-call | flops 1 | bytes 1 | tf_op jit(solution)/shard_map/stack/pallas_call | solution.py:97
  41.3 5.1 %fisher_parts.5 = (bf16[2,256,1024]{2,1,0:T(8,128)(2,1)}, bf16[2,256,1024]{2,1,0:T(8,128)(2,1)S(1)}, f32[8,128]{1,0:T(8,128)S(1)}) custom-call(s32[5]{0:T(128)S(1)} %stack.83.where, bf16[4,512,256]{2,1,0:T(8,128)(2,1)S(1)} %bitcast.24, bf16[2,4,256,256]{3,2,1,0:T(8,128)(2,1)} %get-tuple-element.93.mine, ...), custom_call_target="tpu_custom_call" | custom-call | flops 1 | bytes 1 | tf_op jit(solution)/shard_map/fisher_parts/pallas_call | solution.py:142
  47.4 2.8 %collective-permute-start.13 = (bf16[2,256,1024]{2,1,0:T(8,128)(2,1)}, bf16[2,256,1024]{2,1,0:T(8,128)(2,1)}, u32[]{:S(2)}, u32[]{:S(2)}) collective-permute-start(bf16[2,256,1024]{2,1,0:T(8,128)(2,1)} %get-tuple-element.103), channel_id=1, source_target_pairs={{0,64},{1,193},{64,0},{65,129},{128,192},{129,65},{192,128},{193,1... | collective-permute-start | bytes 3145736 | tf_op jit(solution)/shard_map/ppermute | solution.py:52
  50.2 1.8 add_up.13
  52.0 3.6 %collective-permute-done.6.value = bf16[2,4,256,256]{3,2,1,0:T(8,128)(2,1)} collective-permute-done((bf16[2,4,256,256]{3,2,1,0:T(8,128)(2,1)}, bf16[2,4,256,256]{3,2,1,0:T(8,128)(2,1)}, u32[]{:S(2)}, u32[]{:S(2)}) %collective-permute-start.6) | collective-permute-done | bytes 1048608 | tf_op jit(solution)/shard_map/ppermute | solution.py:52
  55.6 3.3 %collective-permute-start.12 = (bf16[2,64,1024]{2,1,0:T(8,128)(2,1)}, bf16[2,64,1024]{2,1,0:T(8,128)(2,1)S(1)}, u32[]{:S(2)}, u32[]{:S(2)}) collective-permute-start(bf16[2,64,1024]{2,1,0:T(8,128)(2,1)} %get-tuple-element.101), channel_id=1, source_target_pairs={{0,16},{1,49},{16,0},{17,33},{32,48},{33,17},{48,32},{49,1},{2,18}... | collective-permute-start | bytes 786440 | tf_op jit(solution)/shard_map/ppermute | solution.py:52
  59.1 4.2 %fisher_parts.6 = (bf16[2,256,1024]{2,1,0:T(8,128)(2,1)S(1)}, bf16[2,256,1024]{2,1,0:T(8,128)(2,1)S(1)}, f32[8,128]{1,0:T(8,128)S(1)}) custom-call(s32[5]{0:T(128)S(1)} %stack.73.where, bf16[4,512,256]{2,1,0:T(8,128)(2,1)S(1)} %bitcast.25, bf16[2,4,256,256]{3,2,1,0:T(8,128)(2,1)} %get-tuple-element.88.mine, ...), custom_call_target="tpu_custom_call" | custom-call | flops 1 | bytes 1 | tf_op jit(solution)/shard_map/fisher_parts/pallas_call | solution.py:142
  63.3 1.4 collective-permute-start.10
  64.7 1.2 add_up.14
  66.3 1.1 add_up.15
  67.4 4.2 %fisher_parts.7 = (bf16[2,256,1024]{2,1,0:T(8,128)(2,1)S(1)}, bf16[2,256,1024]{2,1,0:T(8,128)(2,1)S(1)}, f32[8,128]{1,0:T(8,128)S(1)}) custom-call(s32[5]{0:T(128)S(1)} %stack.88.where, bf16[4,512,256]{2,1,0:T(8,128)(2,1)S(1)} %bitcast.26, bf16[2,4,256,256]{3,2,1,0:T(8,128)(2,1)} %get-tuple-element.100.mine, ...), custom_call_target="tpu_custom_call" | custom-call | flops 1 | bytes 1 | tf_op jit(solution)/shard_map/fisher_parts/pallas_call | solution.py:142
  71.5 1.4 collective-permute-start.16
  72.9 6.0 %collective-permute-start.15 = (bf16[2,64,1024]{2,1,0:T(8,128)(2,1)S(1)}, bf16[2,64,1024]{2,1,0:T(8,128)(2,1)S(1)}, u32[]{:S(2)}, u32[]{:S(2)}) collective-permute-start(bf16[2,64,1024]{2,1,0:T(8,128)(2,1)S(1)} %get-tuple-element.109.refs_0_), channel_id=1, source_target_pairs={{0,48},{1,17},{16,32},{17,1},{32,16},{33,49},{48,0},{49,33},{2,50}... | collective-permute-start | bytes 786440 | tf_op jit(solution)/shard_map/ppermute | solution.py:52
  79.0 8.7 %collective-permute-done.17.refs_2_ = bf16[2,128,1024]{2,1,0:T(8,128)(2,1)S(1)} collective-permute-done((bf16[2,128,1024]{2,1,0:T(8,128)(2,1)S(1)}, bf16[2,128,1024]{2,1,0:T(8,128)(2,1)S(1)}, u32[]{:S(2)}, u32[]{:S(2)}) %collective-permute-start.17) | collective-permute-done | bytes 524320 | tf_op jit(solution)/shard_map/ppermute | solution.py:52
  89.8 5.2 %collective-permute-done.16.refs_1_ = bf16[2,256,1024]{2,1,0:T(8,128)(2,1)S(1)} collective-permute-done((bf16[2,256,1024]{2,1,0:T(8,128)(2,1)S(1)}, bf16[2,256,1024]{2,1,0:T(8,128)(2,1)S(1)}, u32[]{:S(2)}, u32[]{:S(2)}) %collective-permute-start.16) | collective-permute-done | bytes 1048608 | tf_op jit(solution)/shard_map/ppermute | solution.py:52
  95.9 1.6 collective-permute-start.14
  97.6 1.6 collective-permute-done.19.refs_3_
  100.2 5.2 %collective-permute-start.21 = (bf16[2,64,1024]{2,1,0:T(8,128)(2,1)S(1)}, bf16[2,64,1024]{2,1,0:T(8,128)(2,1)S(1)}, u32[]{:S(2)}, u32[]{:S(2)}) collective-permute-start(bf16[2,64,1024]{2,1,0:T(8,128)(2,1)S(1)} %get-tuple-element.121.refs_0_), channel_id=1, source_target_pairs={{0,48},{1,17},{16,32},{17,1},{32,16},{33,49},{48,0},{49,33},{2,50}... | collective-permute-start | bytes 786440 | tf_op jit(solution)/shard_map/ppermute | solution.py:52
  105.9 2.0 %collective-permute-start.24 = (bf16[2,64,1024]{2,1,0:T(8,128)(2,1)S(1)}, bf16[2,64,1024]{2,1,0:T(8,128)(2,1)S(1)}, u32[]{:S(2)}, u32[]{:S(2)}) collective-permute-start(bf16[2,64,1024]{2,1,0:T(8,128)(2,1)S(1)} %get-tuple-element.128), channel_id=1, source_target_pairs={{0,16},{1,49},{16,0},{17,33},{32,48},{33,17},{48,32},{49,1},{2,18}... | collective-permute-start | bytes 786440 | tf_op jit(solution)/shard_map/ppermute | solution.py:52
  107.9 8.9 %collective-permute-done.21.refs_1_ = bf16[2,64,1024]{2,1,0:T(8,128)(2,1)S(1)} collective-permute-done((bf16[2,64,1024]{2,1,0:T(8,128)(2,1)S(1)}, bf16[2,64,1024]{2,1,0:T(8,128)(2,1)S(1)}, u32[]{:S(2)}, u32[]{:S(2)}) %collective-permute-start.21) | collective-permute-done | bytes 262176 | tf_op jit(solution)/shard_map/ppermute | solution.py:52
  116.9 5.0 %collective-permute-start.29 = (bf16[256,1024]{1,0:T(8,128)(2,1)S(1)}, bf16[256,1024]{1,0:T(8,128)(2,1)S(1)}, u32[]{:S(2)}, u32[]{:S(2)}) collective-permute-start(bf16[256,1024]{1,0:T(8,128)(2,1)S(1)} %get-tuple-element.136.near), channel_id=1, source_target_pairs={{0,64},{1,193},{64,0},{65,129},{128,192},{129,65},{192,128},{193,1... | collective-permute-start | bytes 1572872 | tf_op jit(solution)/shard_map/ppermute | solution.py:52
  122.0 3.0 %collective-permute-start.23 = (bf16[2,64,1024]{2,1,0:T(8,128)(2,1)S(1)}, bf16[2,64,1024]{2,1,0:T(8,128)(2,1)S(1)}, u32[]{:S(2)}, u32[]{:S(2)}) collective-permute-start(bf16[2,64,1024]{2,1,0:T(8,128)(2,1)S(1)} %get-tuple-element.127), channel_id=1, source_target_pairs={{0,16},{1,49},{16,0},{17,33},{32,48},{33,17},{48,32},{49,1},{2,18}... | collective-permute-start | bytes 786440 | tf_op jit(solution)/shard_map/ppermute | solution.py:52
  125.0 4.0 %collective-permute-done.25.a = bf16[64,1024]{1,0:T(8,128)(2,1)S(1)} collective-permute-done((bf16[64,1024]{1,0:T(8,128)(2,1)S(1)}, bf16[64,1024]{1,0:T(8,128)(2,1)S(1)}, u32[]{:S(2)}, u32[]{:S(2)}) %collective-permute-start.25) | collective-permute-done | bytes 131104 | tf_op jit(solution)/shard_map/ppermute | solution.py:52
  129.2 10.6 %collective-permute-start.28 = (bf16[2,64,1024]{2,1,0:T(8,128)(2,1)S(1)}, bf16[2,64,1024]{2,1,0:T(8,128)(2,1)S(1)}, u32[]{:S(2)}, u32[]{:S(2)}) collective-permute-start(bf16[2,64,1024]{2,1,0:T(8,128)(2,1)S(1)} %get-tuple-element.135.refs_0_), channel_id=1, source_target_pairs={{0,48},{1,17},{16,32},{17,1},{32,16},{33,49},{48,0},{49,33},{2,50}... | collective-permute-start | bytes 786440 | tf_op jit(solution)/shard_map/ppermute | solution.py:52
  139.9 2.0 %collective-permute-done.23.refs_3_ = bf16[2,64,1024]{2,1,0:T(8,128)(2,1)S(1)} collective-permute-done((bf16[2,64,1024]{2,1,0:T(8,128)(2,1)S(1)}, bf16[2,64,1024]{2,1,0:T(8,128)(2,1)S(1)}, u32[]{:S(2)}, u32[]{:S(2)}) %collective-permute-start.23) | collective-permute-done | bytes 262176 | tf_op jit(solution)/shard_map/ppermute | solution.py:52
  142.0 3.6 %collective-permute-start.26 = (bf16[2,64,1024]{2,1,0:T(8,128)(2,1)S(1)}, bf16[2,64,1024]{2,1,0:T(8,128)(2,1)S(1)}, u32[]{:S(2)}, u32[]{:S(2)}) collective-permute-start(bf16[2,64,1024]{2,1,0:T(8,128)(2,1)S(1)} %get-tuple-element.133.refs_0_), channel_id=1, source_target_pairs={{0,48},{1,17},{16,32},{17,1},{32,16},{33,49},{48,0},{49,33},{2,50}... | collective-permute-start | bytes 786440 | tf_op jit(solution)/shard_map/ppermute | solution.py:52
  145.6 1.6 place.4
  147.2 6.1 %collective-permute-done.28.refs_1_ = bf16[2,64,1024]{2,1,0:T(8,128)(2,1)S(1)} collective-permute-done((bf16[2,64,1024]{2,1,0:T(8,128)(2,1)S(1)}, bf16[2,64,1024]{2,1,0:T(8,128)(2,1)S(1)}, u32[]{:S(2)}, u32[]{:S(2)}) %collective-permute-start.28) | collective-permute-done | bytes 262176 | tf_op jit(solution)/shard_map/ppermute | solution.py:52
  153.7 4.3 %collective-permute-done.26.refs_1_ = bf16[2,64,1024]{2,1,0:T(8,128)(2,1)S(1)} collective-permute-done((bf16[2,64,1024]{2,1,0:T(8,128)(2,1)S(1)}, bf16[2,64,1024]{2,1,0:T(8,128)(2,1)S(1)}, u32[]{:S(2)}, u32[]{:S(2)}) %collective-permute-start.26) | collective-permute-done | bytes 262176 | tf_op jit(solution)/shard_map/ppermute | solution.py:52
  158.1 4.7 %collective-permute-start.30 = (bf16[64,1024]{1,0:T(8,128)(2,1)S(1)}, bf16[64,1024]{1,0:T(8,128)(2,1)S(1)}, u32[]{:S(2)}, u32[]{:S(2)}) collective-permute-start(bf16[64,1024]{1,0:T(8,128)(2,1)S(1)} %get-tuple-element.141.b), channel_id=1, source_target_pairs={{0,16},{1,49},{16,0},{17,33},{32,48},{33,17},{48,32},{49,1},{2,18}... | collective-permute-start | bytes 393224 | tf_op jit(solution)/shard_map/ppermute | solution.py:52
  162.9 2.8 %collective-permute-done.30.a = bf16[64,1024]{1,0:T(8,128)(2,1)S(1)} collective-permute-done((bf16[64,1024]{1,0:T(8,128)(2,1)S(1)}, bf16[64,1024]{1,0:T(8,128)(2,1)S(1)}, u32[]{:S(2)}, u32[]{:S(2)}) %collective-permute-start.30) | collective-permute-done | bytes 131104 | tf_op jit(solution)/shard_map/ppermute | solution.py:52
  165.9 6.1 %collective-permute-done.34.a = bf16[128,1024]{1,0:T(8,128)(2,1)S(1)} collective-permute-done((bf16[128,1024]{1,0:T(8,128)(2,1)S(1)}, bf16[128,1024]{1,0:T(8,128)(2,1)S(1)}, u32[]{:S(2)}, u32[]{:S(2)}) %collective-permute-start.34) | collective-permute-done | bytes 262176 | tf_op jit(solution)/shard_map/ppermute | solution.py:52
  172.0 1.4 collective-permute-start.36
  173.4 1.6 place.5
  175.0 2.6 %collective-permute-done.32.a = bf16[128,1024]{1,0:T(8,128)(2,1)S(1)} collective-permute-done((bf16[128,1024]{1,0:T(8,128)(2,1)S(1)}, bf16[128,1024]{1,0:T(8,128)(2,1)S(1)}, u32[]{:S(2)}, u32[]{:S(2)}) %collective-permute-start.32) | collective-permute-done | bytes 262176 | tf_op jit(solution)/shard_map/ppermute | solution.py:52
  177.7 1.4 collective-permute-start.35
  179.0 2.3 %collective-permute-done.36.far = bf16[256,1024]{1,0:T(8,128)(2,1)S(1)} collective-permute-done((bf16[256,1024]{1,0:T(8,128)(2,1)S(1)}, bf16[256,1024]{1,0:T(8,128)(2,1)S(1)}, u32[]{:S(2)}, u32[]{:S(2)}) %collective-permute-start.36) | collective-permute-done | bytes 524320 | tf_op jit(solution)/shard_map/ppermute | solution.py:52
  181.3 1.6 place.6
  182.9 4.0 %collective-permute-done.35.far = bf16[256,1024]{1,0:T(8,128)(2,1)S(1)} collective-permute-done((bf16[256,1024]{1,0:T(8,128)(2,1)S(1)}, bf16[256,1024]{1,0:T(8,128)(2,1)S(1)}, u32[]{:S(2)}, u32[]{:S(2)}) %collective-permute-start.35) | collective-permute-done | bytes 524320 | tf_op jit(solution)/shard_map/ppermute | solution.py:52
  186.9 1.6 place.7
  (72 shorter events, 11.3 us)
Async XLA Ops:
  0.0 9.4 %collective-permute-start.1 = (bf16[4,256,256]{2,1,0:T(8,128)(2,1)}, bf16[4,256,256]{2,1,0:T(8,128)(2,1)S(1)}, u32[]{:S(2)}, u32[]{:S(2)}) collective-permute-start(bf16[4,256,256]{2,1,0:T(8,128)(2,1)} %bitcast.7.a), channel_id=1, source_target_pairs={{0,2},{1,7},{2,0},{3,5},{4,6},{5,3},{6,4},{7,1},{8,10},{9,15},{10,... | collective-permute-start | bytes 1572872 | tf_op jit(solution)/shard_map/ppermute | solution.py:52
  11.5 2.9 %collective-permute-start.3 = (bf16[2,4,256,256]{3,2,1,0:T(8,128)(2,1)}, bf16[2,4,256,256]{3,2,1,0:T(8,128)(2,1)S(1)}, u32[]{:S(2)}, u32[]{:S(2)}) collective-permute-start(bf16[2,4,256,256]{3,2,1,0:T(8,128)(2,1)} %get-tuple-element.82.mine), channel_id=1, source_target_pairs={{0,1},{1,0},{2,3},{3,2},{4,5},{5,4},{6,7},{7,6},{8,9},{9,8},{10,11... | collective-permute-start | bytes 3145736 | tf_op jit(solution)/shard_map/ppermute | solution.py:56
  11.5 16.3 %collective-permute-start.2 = (bf16[2,4,256,256]{3,2,1,0:T(8,128)(2,1)}, bf16[2,4,256,256]{3,2,1,0:T(8,128)(2,1)}, u32[]{:S(2)}, u32[]{:S(2)}) collective-permute-start(bf16[2,4,256,256]{3,2,1,0:T(8,128)(2,1)} %get-tuple-element.82.mine), channel_id=1, source_target_pairs={{0,6},{1,3},{2,4},{3,1},{4,2},{5,7},{6,0},{7,5},{8,14},{9,11},{10,... | collective-permute-start | bytes 3145736 | tf_op jit(solution)/shard_map/ppermute | solution.py:52
  12.0 15.9 %collective-permute-start = (bf16[4,256,256]{2,1,0:T(8,128)(2,1)}, bf16[4,256,256]{2,1,0:T(8,128)(2,1)}, u32[]{:S(2)}, u32[]{:S(2)}) collective-permute-start(bf16[4,256,256]{2,1,0:T(8,128)(2,1)} %bitcast.7.a), channel_id=1, source_target_pairs={{0,8},{8,0},{1,9},{9,1},{2,10},{10,2},{3,11},{11,3},{4,12},{12,4},... | collective-permute-start | bytes 1572872 | tf_op jit(solution)/shard_map/ppermute | solution.py:56
  18.2 21.6 %collective-permute-start.7 = (bf16[2,256,1024]{2,1,0:T(8,128)(2,1)S(1)}, bf16[2,256,1024]{2,1,0:T(8,128)(2,1)S(1)}, u32[]{:S(2)}, u32[]{:S(2)}) collective-permute-start(bf16[2,256,1024]{2,1,0:T(8,128)(2,1)S(1)} %get-tuple-element.90), channel_id=1, source_target_pairs={{0,64},{1,193},{64,0},{65,129},{128,192},{129,65},{192,128},{193,1... | collective-permute-start | bytes 3145736 | tf_op jit(solution)/shard_map/ppermute | solution.py:52
  27.8 9.4 %collective-permute-start.4 = (bf16[4,256,256]{2,1,0:T(8,128)(2,1)}, bf16[4,256,256]{2,1,0:T(8,128)(2,1)S(1)}, u32[]{:S(2)}, u32[]{:S(2)}) collective-permute-start(bf16[4,256,256]{2,1,0:T(8,128)(2,1)} %get-tuple-element.86.a), channel_id=1, source_target_pairs={{0,2},{1,7},{2,0},{3,5},{4,6},{5,3},{6,4},{7,1},{8,10},{9,15},{10,... | collective-permute-start | bytes 1572872 | tf_op jit(solution)/shard_map/ppermute | solution.py:52
  27.9 13.4 %collective-permute-start.9 = (bf16[2,4,256,256]{3,2,1,0:T(8,128)(2,1)}, bf16[2,4,256,256]{3,2,1,0:T(8,128)(2,1)}, u32[]{:S(2)}, u32[]{:S(2)}) collective-permute-start(bf16[2,4,256,256]{3,2,1,0:T(8,128)(2,1)} %get-tuple-element.93.mine), channel_id=1, source_target_pairs={{0,1},{1,0},{2,3},{3,2},{4,5},{5,4},{6,7},{7,6},{8,9},{9,8},{10,11... | collective-permute-start | bytes 3145736 | tf_op jit(solution)/shard_map/ppermute | solution.py:56
  39.3 16.3 %collective-permute-start.6 = (bf16[2,4,256,256]{3,2,1,0:T(8,128)(2,1)}, bf16[2,4,256,256]{3,2,1,0:T(8,128)(2,1)}, u32[]{:S(2)}, u32[]{:S(2)}) collective-permute-start(bf16[2,4,256,256]{3,2,1,0:T(8,128)(2,1)} %get-tuple-element.88.mine), channel_id=1, source_target_pairs={{0,6},{1,3},{2,4},{3,1},{4,2},{5,7},{6,0},{7,5},{8,14},{9,11},{10,... | collective-permute-start | bytes 3145736 | tf_op jit(solution)/shard_map/ppermute | solution.py:52
  40.7 9.5 %collective-permute-start.8 = (bf16[2,128,1024]{2,1,0:T(8,128)(2,1)}, bf16[2,128,1024]{2,1,0:T(8,128)(2,1)}, u32[]{:S(2)}, u32[]{:S(2)}) collective-permute-start(bf16[2,128,1024]{2,1,0:T(8,128)(2,1)} %get-tuple-element.92), channel_id=1, source_target_pairs={{0,192},{1,65},{64,128},{65,1},{128,64},{129,193},{192,0},{193,129... | collective-permute-start | bytes 1572872 | tf_op jit(solution)/shard_map/ppermute | solution.py:52
  41.2 17.8 %collective-permute-start.5 = (bf16[2,4,256,256]{3,2,1,0:T(8,128)(2,1)}, bf16[2,4,256,256]{3,2,1,0:T(8,128)(2,1)}, u32[]{:S(2)}, u32[]{:S(2)}) collective-permute-start(bf16[2,4,256,256]{3,2,1,0:T(8,128)(2,1)} %get-tuple-element.88.mine), channel_id=1, source_target_pairs={{0,1},{1,0},{2,3},{3,2},{4,5},{5,4},{6,7},{7,6},{8,9},{9,8},{10,11... | collective-permute-start | bytes 3145736 | tf_op jit(solution)/shard_map/ppermute | solution.py:56
  46.4 1.0 copy-start
  47.4 17.3 %collective-permute-start.13 = (bf16[2,256,1024]{2,1,0:T(8,128)(2,1)}, bf16[2,256,1024]{2,1,0:T(8,128)(2,1)}, u32[]{:S(2)}, u32[]{:S(2)}) collective-permute-start(bf16[2,256,1024]{2,1,0:T(8,128)(2,1)} %get-tuple-element.103), channel_id=1, source_target_pairs={{0,64},{1,193},{64,0},{65,129},{128,192},{129,65},{192,128},{193,1... | collective-permute-start | bytes 3145736 | tf_op jit(solution)/shard_map/ppermute | solution.py:52
  55.6 11.8 %collective-permute-start.11 = (bf16[2,4,256,256]{3,2,1,0:T(8,128)(2,1)}, bf16[2,4,256,256]{3,2,1,0:T(8,128)(2,1)}, u32[]{:S(2)}, u32[]{:S(2)}) collective-permute-start(bf16[2,4,256,256]{3,2,1,0:T(8,128)(2,1)} %get-tuple-element.100.mine), channel_id=1, source_target_pairs={{0,1},{1,0},{2,3},{3,2},{4,5},{5,4},{6,7},{7,6},{8,9},{9,8},{10,11... | collective-permute-start | bytes 3145736 | tf_op jit(solution)/shard_map/ppermute | solution.py:56
  55.6 10.6 %collective-permute-start.12 = (bf16[2,64,1024]{2,1,0:T(8,128)(2,1)}, bf16[2,64,1024]{2,1,0:T(8,128)(2,1)S(1)}, u32[]{:S(2)}, u32[]{:S(2)}) collective-permute-start(bf16[2,64,1024]{2,1,0:T(8,128)(2,1)} %get-tuple-element.101), channel_id=1, source_target_pairs={{0,16},{1,49},{16,0},{17,33},{32,48},{33,17},{48,32},{49,1},{2,18}... | collective-permute-start | bytes 786440 | tf_op jit(solution)/shard_map/ppermute | solution.py:52
  59.0 5.6 %copy-start.1 = (bf16[2,256,1024]{2,1,0:T(8,128)(2,1)S(1)}, bf16[2,256,1024]{2,1,0:T(8,128)(2,1)}, u32[]{:S(2)}) copy-start(bf16[2,256,1024]{2,1,0:T(8,128)(2,1)} %copy-done) | copy-start | bytes 3145732
  63.3 15.6 %collective-permute-start.10 = (bf16[2,256,1024]{2,1,0:T(8,128)(2,1)S(1)}, bf16[2,256,1024]{2,1,0:T(8,128)(2,1)S(1)}, u32[]{:S(2)}, u32[]{:S(2)}) collective-permute-start(bf16[2,256,1024]{2,1,0:T(8,128)(2,1)S(1)} %get-tuple-element.99), channel_id=1, source_target_pairs={{0,64},{1,193},{64,0},{65,129},{128,192},{129,65},{192,128},{193,1... | collective-permute-start | bytes 3145736 | tf_op jit(solution)/shard_map/ppermute | solution.py:52
  71.5 23.5 %collective-permute-start.16 = (bf16[2,256,1024]{2,1,0:T(8,128)(2,1)S(1)}, bf16[2,256,1024]{2,1,0:T(8,128)(2,1)S(1)}, u32[]{:S(2)}, u32[]{:S(2)}) collective-permute-start(bf16[2,256,1024]{2,1,0:T(8,128)(2,1)S(1)} %get-tuple-element.111), channel_id=1, source_target_pairs={{0,64},{1,193},{64,0},{65,129},{128,192},{129,65},{192,128},{193,1... | collective-permute-start | bytes 3145736 | tf_op jit(solution)/shard_map/ppermute | solution.py:52
  72.9 14.9 %collective-permute-start.17 = (bf16[2,128,1024]{2,1,0:T(8,128)(2,1)S(1)}, bf16[2,128,1024]{2,1,0:T(8,128)(2,1)S(1)}, u32[]{:S(2)}, u32[]{:S(2)}) collective-permute-start(bf16[2,128,1024]{2,1,0:T(8,128)(2,1)S(1)} %get-tuple-element.112), channel_id=1, source_target_pairs={{0,192},{1,65},{64,128},{65,1},{128,64},{129,193},{192,0},{193,129... | collective-permute-start | bytes 1572872 | tf_op jit(solution)/shard_map/ppermute | solution.py:52
  72.9 22.8 %collective-permute-start.15 = (bf16[2,64,1024]{2,1,0:T(8,128)(2,1)S(1)}, bf16[2,64,1024]{2,1,0:T(8,128)(2,1)S(1)}, u32[]{:S(2)}, u32[]{:S(2)}) collective-permute-start(bf16[2,64,1024]{2,1,0:T(8,128)(2,1)S(1)} %get-tuple-element.109.refs_0_), channel_id=1, source_target_pairs={{0,48},{1,17},{16,32},{17,1},{32,16},{33,49},{48,0},{49,33},{2,50}... | collective-permute-start | bytes 786440 | tf_op jit(solution)/shard_map/ppermute | solution.py:52
  88.8 10.3 %collective-permute-start.19 = (bf16[2,64,1024]{2,1,0:T(8,128)(2,1)S(1)}, bf16[2,64,1024]{2,1,0:T(8,128)(2,1)S(1)}, u32[]{:S(2)}, u32[]{:S(2)}) collective-permute-start(bf16[2,64,1024]{2,1,0:T(8,128)(2,1)S(1)} %get-tuple-element.117), channel_id=1, source_target_pairs={{0,16},{1,49},{16,0},{17,33},{32,48},{33,17},{48,32},{49,1},{2,18}... | collective-permute-start | bytes 786440 | tf_op jit(solution)/shard_map/ppermute | solution.py:52
  95.2 10.7 %collective-permute-start.22 = (bf16[2,128,1024]{2,1,0:T(8,128)(2,1)S(1)}, bf16[2,128,1024]{2,1,0:T(8,128)(2,1)S(1)}, u32[]{:S(2)}, u32[]{:S(2)}) collective-permute-start(bf16[2,128,1024]{2,1,0:T(8,128)(2,1)S(1)} %get-tuple-element.122), channel_id=1, source_target_pairs={{0,192},{1,65},{64,128},{65,1},{128,64},{129,193},{192,0},{193,129... | collective-permute-start | bytes 1572872 | tf_op jit(solution)/shard_map/ppermute | solution.py:52
  95.8 9.6 %collective-permute-start.18 = (bf16[64,1024]{1,0:T(8,128)(2,1)S(1)}, bf16[64,1024]{1,0:T(8,128)(2,1)S(1)}, u32[]{:S(2)}, u32[]{:S(2)}) collective-permute-start(bf16[64,1024]{1,0:T(8,128)(2,1)S(1)} %get-tuple-element.116.b), channel_id=1, source_target_pairs={{0,16},{1,49},{16,0},{17,33},{32,48},{33,17},{48,32},{49,1},{2,18}... | collective-permute-start | bytes 393224 | tf_op jit(solution)/shard_map/ppermute | solution.py:52
  95.9 26.0 %collective-permute-start.14 = (bf16[2,128,1024]{2,1,0:T(8,128)(2,1)S(1)}, bf16[2,128,1024]{2,1,0:T(8,128)(2,1)S(1)}, u32[]{:S(2)}, u32[]{:S(2)}) collective-permute-start(bf16[2,128,1024]{2,1,0:T(8,128)(2,1)S(1)} %get-tuple-element.108), channel_id=1, source_target_pairs={{0,192},{1,65},{64,128},{65,1},{128,64},{129,193},{192,0},{193,129... | collective-permute-start | bytes 1572872 | tf_op jit(solution)/shard_map/ppermute | solution.py:52
  100.2 16.6 %collective-permute-start.21 = (bf16[2,64,1024]{2,1,0:T(8,128)(2,1)S(1)}, bf16[2,64,1024]{2,1,0:T(8,128)(2,1)S(1)}, u32[]{:S(2)}, u32[]{:S(2)}) collective-permute-start(bf16[2,64,1024]{2,1,0:T(8,128)(2,1)S(1)} %get-tuple-element.121.refs_0_), channel_id=1, source_target_pairs={{0,48},{1,17},{16,32},{17,1},{32,16},{33,49},{48,0},{49,33},{2,50}... | collective-permute-start | bytes 786440 | tf_op jit(solution)/shard_map/ppermute | solution.py:52
  105.4 11.4 %collective-permute-start.20 = (bf16[128,1024]{1,0:T(8,128)(2,1)S(1)}, bf16[128,1024]{1,0:T(8,128)(2,1)S(1)}, u32[]{:S(2)}, u32[]{:S(2)}) collective-permute-start(bf16[128,1024]{1,0:T(8,128)(2,1)S(1)} %get-tuple-element.120.b), channel_id=1, source_target_pairs={{0,192},{1,65},{64,128},{65,1},{128,64},{129,193},{192,0},{193,129... | collective-permute-start | bytes 786440 | tf_op jit(solution)/shard_map/ppermute | solution.py:52
  105.9 23.1 %collective-permute-start.24 = (bf16[2,64,1024]{2,1,0:T(8,128)(2,1)S(1)}, bf16[2,64,1024]{2,1,0:T(8,128)(2,1)S(1)}, u32[]{:S(2)}, u32[]{:S(2)}) collective-permute-start(bf16[2,64,1024]{2,1,0:T(8,128)(2,1)S(1)} %get-tuple-element.128), channel_id=1, source_target_pairs={{0,16},{1,49},{16,0},{17,33},{32,48},{33,17},{48,32},{49,1},{2,18}... | collective-permute-start | bytes 786440 | tf_op jit(solution)/shard_map/ppermute | solution.py:52
  116.9 28.7 %collective-permute-start.29 = (bf16[256,1024]{1,0:T(8,128)(2,1)S(1)}, bf16[256,1024]{1,0:T(8,128)(2,1)S(1)}, u32[]{:S(2)}, u32[]{:S(2)}) collective-permute-start(bf16[256,1024]{1,0:T(8,128)(2,1)S(1)} %get-tuple-element.136.near), channel_id=1, source_target_pairs={{0,64},{1,193},{64,0},{65,129},{128,192},{129,65},{192,128},{193,1... | collective-permute-start | bytes 1572872 | tf_op jit(solution)/shard_map/ppermute | solution.py:52
  121.9 7.1 %collective-permute-start.25 = (bf16[64,1024]{1,0:T(8,128)(2,1)S(1)}, bf16[64,1024]{1,0:T(8,128)(2,1)S(1)}, u32[]{:S(2)}, u32[]{:S(2)}) collective-permute-start(bf16[64,1024]{1,0:T(8,128)(2,1)S(1)} %get-tuple-element.129.b), channel_id=1, source_target_pairs={{0,16},{1,49},{16,0},{17,33},{32,48},{33,17},{48,32},{49,1},{2,18}... | collective-permute-start | bytes 393224 | tf_op jit(solution)/shard_map/ppermute | solution.py:52
  122.0 19.8 %collective-permute-start.23 = (bf16[2,64,1024]{2,1,0:T(8,128)(2,1)S(1)}, bf16[2,64,1024]{2,1,0:T(8,128)(2,1)S(1)}, u32[]{:S(2)}, u32[]{:S(2)}) collective-permute-start(bf16[2,64,1024]{2,1,0:T(8,128)(2,1)S(1)} %get-tuple-element.127), channel_id=1, source_target_pairs={{0,16},{1,49},{16,0},{17,33},{32,48},{33,17},{48,32},{49,1},{2,18}... | collective-permute-start | bytes 786440 | tf_op jit(solution)/shard_map/ppermute | solution.py:52
  129.2 24.1 %collective-permute-start.28 = (bf16[2,64,1024]{2,1,0:T(8,128)(2,1)S(1)}, bf16[2,64,1024]{2,1,0:T(8,128)(2,1)S(1)}, u32[]{:S(2)}, u32[]{:S(2)}) collective-permute-start(bf16[2,64,1024]{2,1,0:T(8,128)(2,1)S(1)} %get-tuple-element.135.refs_0_), channel_id=1, source_target_pairs={{0,48},{1,17},{16,32},{17,1},{32,16},{33,49},{48,0},{49,33},{2,50}... | collective-permute-start | bytes 786440 | tf_op jit(solution)/shard_map/ppermute | solution.py:52
  139.8 13.6 %collective-permute-start.27 = (bf16[128,1024]{1,0:T(8,128)(2,1)S(1)}, bf16[128,1024]{1,0:T(8,128)(2,1)S(1)}, u32[]{:S(2)}, u32[]{:S(2)}) collective-permute-start(bf16[128,1024]{1,0:T(8,128)(2,1)S(1)} %get-tuple-element.134.b), channel_id=1, source_target_pairs={{0,192},{1,65},{64,128},{65,1},{128,64},{129,193},{192,0},{193,129... | collective-permute-start | bytes 786440 | tf_op jit(solution)/shard_map/ppermute | solution.py:52
  142.0 16.0 %collective-permute-start.26 = (bf16[2,64,1024]{2,1,0:T(8,128)(2,1)S(1)}, bf16[2,64,1024]{2,1,0:T(8,128)(2,1)S(1)}, u32[]{:S(2)}, u32[]{:S(2)}) collective-permute-start(bf16[2,64,1024]{2,1,0:T(8,128)(2,1)S(1)} %get-tuple-element.133.refs_0_), channel_id=1, source_target_pairs={{0,48},{1,17},{16,32},{17,1},{32,16},{33,49},{48,0},{49,33},{2,50}... | collective-permute-start | bytes 786440 | tf_op jit(solution)/shard_map/ppermute | solution.py:52
  153.5 19.9 %collective-permute-start.33 = (bf16[256,1024]{1,0:T(8,128)(2,1)S(1)}, bf16[256,1024]{1,0:T(8,128)(2,1)S(1)}, u32[]{:S(2)}, u32[]{:S(2)}) collective-permute-start(bf16[256,1024]{1,0:T(8,128)(2,1)S(1)} %get-tuple-element.146.near), channel_id=1, source_target_pairs={{0,64},{1,193},{64,0},{65,129},{128,192},{129,65},{192,128},{193,1... | collective-permute-start | bytes 1572872 | tf_op jit(solution)/shard_map/ppermute | solution.py:52
  153.6 9.2 %collective-permute-start.31 = (bf16[64,1024]{1,0:T(8,128)(2,1)S(1)}, bf16[64,1024]{1,0:T(8,128)(2,1)S(1)}, u32[]{:S(2)}, u32[]{:S(2)}) collective-permute-start(bf16[64,1024]{1,0:T(8,128)(2,1)S(1)} %get-tuple-element.142.b), channel_id=1, source_target_pairs={{0,16},{1,49},{16,0},{17,33},{32,48},{33,17},{48,32},{49,1},{2,18}... | collective-permute-start | bytes 393224 | tf_op jit(solution)/shard_map/ppermute | solution.py:52
  158.1 7.7 %collective-permute-start.30 = (bf16[64,1024]{1,0:T(8,128)(2,1)S(1)}, bf16[64,1024]{1,0:T(8,128)(2,1)S(1)}, u32[]{:S(2)}, u32[]{:S(2)}) collective-permute-start(bf16[64,1024]{1,0:T(8,128)(2,1)S(1)} %get-tuple-element.141.b), channel_id=1, source_target_pairs={{0,16},{1,49},{16,0},{17,33},{32,48},{33,17},{48,32},{49,1},{2,18}... | collective-permute-start | bytes 393224 | tf_op jit(solution)/shard_map/ppermute | solution.py:52
  162.8 9.2 %collective-permute-start.34 = (bf16[128,1024]{1,0:T(8,128)(2,1)S(1)}, bf16[128,1024]{1,0:T(8,128)(2,1)S(1)}, u32[]{:S(2)}, u32[]{:S(2)}) collective-permute-start(bf16[128,1024]{1,0:T(8,128)(2,1)S(1)} %get-tuple-element.147.b), channel_id=1, source_target_pairs={{0,192},{1,65},{64,128},{65,1},{128,64},{129,193},{192,0},{193,129... | collective-permute-start | bytes 786440 | tf_op jit(solution)/shard_map/ppermute | solution.py:52
  165.8 11.9 %collective-permute-start.32 = (bf16[128,1024]{1,0:T(8,128)(2,1)S(1)}, bf16[128,1024]{1,0:T(8,128)(2,1)S(1)}, u32[]{:S(2)}, u32[]{:S(2)}) collective-permute-start(bf16[128,1024]{1,0:T(8,128)(2,1)S(1)} %get-tuple-element.145.b), channel_id=1, source_target_pairs={{0,192},{1,65},{64,128},{65,1},{128,64},{129,193},{192,0},{193,129... | collective-permute-start | bytes 786440 | tf_op jit(solution)/shard_map/ppermute | solution.py:52
  172.0 9.3 %collective-permute-start.36 = (bf16[256,1024]{1,0:T(8,128)(2,1)S(1)}, bf16[256,1024]{1,0:T(8,128)(2,1)S(1)}, u32[]{:S(2)}, u32[]{:S(2)}) collective-permute-start(bf16[256,1024]{1,0:T(8,128)(2,1)S(1)} %get-tuple-element.153.near), channel_id=1, source_target_pairs={{0,64},{1,193},{64,0},{65,129},{128,192},{129,65},{192,128},{193,1... | collective-permute-start | bytes 1572872 | tf_op jit(solution)/shard_map/ppermute | solution.py:52
  177.7 9.3 %collective-permute-start.35 = (bf16[256,1024]{1,0:T(8,128)(2,1)S(1)}, bf16[256,1024]{1,0:T(8,128)(2,1)S(1)}, u32[]{:S(2)}, u32[]{:S(2)}) collective-permute-start(bf16[256,1024]{1,0:T(8,128)(2,1)S(1)} %get-tuple-element.152.near), channel_id=1, source_target_pairs={{0,64},{1,193},{64,0},{65,129},{128,192},{129,65},{192,128},{193,1... | collective-permute-start | bytes 1572872 | tf_op jit(solution)/shard_map/ppermute | solution.py:52

commit v6 on v5

--- a/solution.py
+++ b/solution.py
@@ -118,12 +118,11 @@
         fetch(tile).start()
     for tile in range(2 * chips):
         cots = (mine, peer)[tile % 2]
+        squares = None
         for number in range(4):
             grad = jnp.dot(acts[number], cots[tile // 2, number], preferred_element_type=F32)
-            if number == 0:
-                total[...] = grad * grad
-            else:
-                total[...] += grad * grad
+            squares = grad * grad if squares is None else squares + grad * grad
+        total[...] = squares
         fetch(tile).wait()
         cols = slice(tile * TILE, (tile + 1) * TILE)
         for k in range(16):

time: 189 us -> 186 us (0.984)
  waiting for transfers between devices: 87.9 us -> 85.3 us
    ppermute x32, waiting for transfers between devices: 87.5 us -> 84.9 us  [exchange(): return lax.ppermute(value, (axis, 'c'), pairs)]
  transfers between devices with their start and end apart: 37 -> 37, of which waited for: 19 -> 18; matrix products, arithmetic and copies ran while one was open for 1% -> 1% of each run, Pallas kernels for 17% -> 18%
where the time goes in v6:
time: 186 us; the launch traced here: 184 us
  waiting for transfers between devices  85.3 us (46%)
  starting transfers between devices  59.7 us (32%)
  Pallas kernels  36.3 us (20%)
  local copies, waits for them, and re-layouts  2.77 us (1%)
    ppermute x32, waiting for transfers between devices, exchange(): return lax.ppermute(value, (axis, 'c'), pairs)  84.9 us
    ppermute x32, starting transfers between devices, exchange(): return lax.ppermute(value, (axis, 'c'), pairs)  57.7 us
    pallas_call x4, Pallas kernels, fisher_parts(): pl.pallas_call(fisher_kernel, out_shape=[jax.ShapeDtypeStruct((2, ROWS //...  17.4 us
    pallas_call x16, Pallas kernels, add_up(): pl.pallas_call(merge_kernel if divide else add_kernel, out_shape=[jax.Sha...  8.23 us
    pallas_call x4, Pallas kernels, place(): pl.pallas_call(place_kernel, out_shape=[jax.ShapeDtypeStruct(weights.shap...  6.28 us
    pallas_call x2, Pallas kernels, stack(): pl.pallas_call(stack_kernel, out_shape=[jax.ShapeDtypeStruct((2, *a.shape...  4.16 us
  transfers between devices with their start and end apart: 37, of which 18 were waited for; matrix products, arithmetic and copies ran while one was open for 1% of the time, Pallas kernels for 18%

profile of v6, /device:TPU:22, one launch (start us, length us, event | category | flops | bytes accessed | tf_op | source)
XLA Modules:
  0.0 184.5 jit_solution(8511839254718189829)
XLA Ops:
  0.8 1.5 copy.10
  2.3 7.1 %collective-permute-done.1.b = bf16[4,256,256]{2,1,0:T(8,128)(2,1)S(1)} collective-permute-done((bf16[4,256,256]{2,1,0:T(8,128)(2,1)}, bf16[4,256,256]{2,1,0:T(8,128)(2,1)S(1)}, u32[]{:S(2)}, u32[]{:S(2)}) %collective-permute-start.1) | collective-permute-done | bytes 524320 | tf_op jit(solution)/shard_map/ppermute | solution.py:52
  9.4 2.1 %stack.89 = (bf16[2,4,256,256]{3,2,1,0:T(8,128)(2,1)}, f32[8,128]{1,0:T(8,128)S(1)}) custom-call(bf16[4,256,256]{2,1,0:T(8,128)(2,1)} %bitcast.7.a, bf16[4,256,256]{2,1,0:T(8,128)(2,1)S(1)} %collective-permute-done.1.b, bf16[4,512,256]{2,1,0:T(8,128)(2,1)S(1)} %bitcast.22), custom_call_target="tpu_custom_call" | custom-call | flops 1 | bytes 1 | tf_op jit(solution)/shard_map/stack/pallas_call | solution.py:97
  12.0 1.9 %collective-permute-start = (bf16[4,256,256]{2,1,0:T(8,128)(2,1)}, bf16[4,256,256]{2,1,0:T(8,128)(2,1)}, u32[]{:S(2)}, u32[]{:S(2)}) collective-permute-start(bf16[4,256,256]{2,1,0:T(8,128)(2,1)} %bitcast.7.a), channel_id=1, source_target_pairs={{0,8},{8,0},{1,9},{9,1},{2,10},{10,2},{3,11},{11,3},{4,12},{12,4},... | collective-permute-start | bytes 1572872 | tf_op jit(solution)/shard_map/ppermute | solution.py:56
  14.3 3.8 %fisher_parts.4 = (bf16[2,256,1024]{2,1,0:T(8,128)(2,1)S(1)}, bf16[2,256,1024]{2,1,0:T(8,128)(2,1)S(1)}, f32[8,128]{1,0:T(8,128)S(1)}) custom-call(s32[5]{0:T(128)S(1)} %stack.78.where, bf16[4,512,256]{2,1,0:T(8,128)(2,1)S(1)} %bitcast.23, bf16[2,4,256,256]{3,2,1,0:T(8,128)(2,1)} %get-tuple-element.82.mine, ...), custom_call_target="tpu_custom_call" | custom-call | flops 1 | bytes 1 | tf_op jit(solution)/shard_map/fisher_parts/pallas_call | solution.py:141
  18.2 1.4 collective-permute-start.7
  19.6 8.2 %collective-permute-done.2.value = bf16[2,4,256,256]{3,2,1,0:T(8,128)(2,1)} collective-permute-done((bf16[2,4,256,256]{3,2,1,0:T(8,128)(2,1)}, bf16[2,4,256,256]{3,2,1,0:T(8,128)(2,1)}, u32[]{:S(2)}, u32[]{:S(2)}) %collective-permute-start.2) | collective-permute-done | bytes 1048608 | tf_op jit(solution)/shard_map/ppermute | solution.py:52
  27.9 9.3 %collective-permute-done.4.b = bf16[4,256,256]{2,1,0:T(8,128)(2,1)S(1)} collective-permute-done((bf16[4,256,256]{2,1,0:T(8,128)(2,1)}, bf16[4,256,256]{2,1,0:T(8,128)(2,1)S(1)}, u32[]{:S(2)}, u32[]{:S(2)}) %collective-permute-start.4) | collective-permute-done | bytes 524320 | tf_op jit(solution)/shard_map/ppermute | solution.py:52
  37.2 2.1 %stack.90 = (bf16[2,4,256,256]{3,2,1,0:T(8,128)(2,1)}, f32[8,128]{1,0:T(8,128)S(1)}) custom-call(bf16[4,256,256]{2,1,0:T(8,128)(2,1)} %get-tuple-element.86.a, bf16[4,256,256]{2,1,0:T(8,128)(2,1)S(1)} %collective-permute-done.4.b, f32[8,128]{1,0:T(8,128)S(1)} %get-tuple-element.87.after), custom_call_target="tpu_custom_call" | custom-call | flops 1 | bytes 1 | tf_op jit(solution)/shard_map/stack/pallas_call | solution.py:97
  41.3 5.1 %fisher_parts.5 = (bf16[2,256,1024]{2,1,0:T(8,128)(2,1)}, bf16[2,256,1024]{2,1,0:T(8,128)(2,1)S(1)}, f32[8,128]{1,0:T(8,128)S(1)}) custom-call(s32[5]{0:T(128)S(1)} %stack.83.where, bf16[4,512,256]{2,1,0:T(8,128)(2,1)S(1)} %bitcast.24, bf16[2,4,256,256]{3,2,1,0:T(8,128)(2,1)} %get-tuple-element.93.mine, ...), custom_call_target="tpu_custom_call" | custom-call | flops 1 | bytes 1 | tf_op jit(solution)/shard_map/fisher_parts/pallas_call | solution.py:141
  47.4 2.8 %collective-permute-start.13 = (bf16[2,256,1024]{2,1,0:T(8,128)(2,1)}, bf16[2,256,1024]{2,1,0:T(8,128)(2,1)}, u32[]{:S(2)}, u32[]{:S(2)}) collective-permute-start(bf16[2,256,1024]{2,1,0:T(8,128)(2,1)} %get-tuple-element.103), channel_id=1, source_target_pairs={{0,64},{1,193},{64,0},{65,129},{128,192},{129,65},{192,128},{193,1... | collective-permute-start | bytes 3145736 | tf_op jit(solution)/shard_map/ppermute | solution.py:52
  50.2 1.8 add_up.13
  52.0 3.6 %collective-permute-done.6.value = bf16[2,4,256,256]{3,2,1,0:T(8,128)(2,1)} collective-permute-done((bf16[2,4,256,256]{3,2,1,0:T(8,128)(2,1)}, bf16[2,4,256,256]{3,2,1,0:T(8,128)(2,1)}, u32[]{:S(2)}, u32[]{:S(2)}) %collective-permute-start.6) | collective-permute-done | bytes 1048608 | tf_op jit(solution)/shard_map/ppermute | solution.py:52
  55.6 3.3 %collective-permute-start.12 = (bf16[2,64,1024]{2,1,0:T(8,128)(2,1)}, bf16[2,64,1024]{2,1,0:T(8,128)(2,1)S(1)}, u32[]{:S(2)}, u32[]{:S(2)}) collective-permute-start(bf16[2,64,1024]{2,1,0:T(8,128)(2,1)} %get-tuple-element.101), channel_id=1, source_target_pairs={{0,16},{1,49},{16,0},{17,33},{32,48},{33,17},{48,32},{49,1},{2,18}... | collective-permute-start | bytes 786440 | tf_op jit(solution)/shard_map/ppermute | solution.py:52
  59.1 4.2 %fisher_parts.6 = (bf16[2,256,1024]{2,1,0:T(8,128)(2,1)S(1)}, bf16[2,256,1024]{2,1,0:T(8,128)(2,1)S(1)}, f32[8,128]{1,0:T(8,128)S(1)}) custom-call(s32[5]{0:T(128)S(1)} %stack.73.where, bf16[4,512,256]{2,1,0:T(8,128)(2,1)S(1)} %bitcast.25, bf16[2,4,256,256]{3,2,1,0:T(8,128)(2,1)} %get-tuple-element.88.mine, ...), custom_call_target="tpu_custom_call" | custom-call | flops 1 | bytes 1 | tf_op jit(solution)/shard_map/fisher_parts/pallas_call | solution.py:141
  63.3 1.4 collective-permute-start.10
  64.7 1.2 add_up.14
  66.3 1.1 add_up.15
  67.4 4.2 %fisher_parts.7 = (bf16[2,256,1024]{2,1,0:T(8,128)(2,1)S(1)}, bf16[2,256,1024]{2,1,0:T(8,128)(2,1)S(1)}, f32[8,128]{1,0:T(8,128)S(1)}) custom-call(s32[5]{0:T(128)S(1)} %stack.88.where, bf16[4,512,256]{2,1,0:T(8,128)(2,1)S(1)} %bitcast.26, bf16[2,4,256,256]{3,2,1,0:T(8,128)(2,1)} %get-tuple-element.100.mine, ...), custom_call_target="tpu_custom_call" | custom-call | flops 1 | bytes 1 | tf_op jit(solution)/shard_map/fisher_parts/pallas_call | solution.py:141
  71.6 1.4 collective-permute-start.16
  72.9 6.0 %collective-permute-start.15 = (bf16[2,64,1024]{2,1,0:T(8,128)(2,1)S(1)}, bf16[2,64,1024]{2,1,0:T(8,128)(2,1)S(1)}, u32[]{:S(2)}, u32[]{:S(2)}) collective-permute-start(bf16[2,64,1024]{2,1,0:T(8,128)(2,1)S(1)} %get-tuple-element.109.refs_0_), channel_id=1, source_target_pairs={{0,48},{1,17},{16,32},{17,1},{32,16},{33,49},{48,0},{49,33},{2,50}... | collective-permute-start | bytes 786440 | tf_op jit(solution)/shard_map/ppermute | solution.py:52
  79.0 8.7 %collective-permute-done.17.refs_2_ = bf16[2,128,1024]{2,1,0:T(8,128)(2,1)S(1)} collective-permute-done((bf16[2,128,1024]{2,1,0:T(8,128)(2,1)S(1)}, bf16[2,128,1024]{2,1,0:T(8,128)(2,1)S(1)}, u32[]{:S(2)}, u32[]{:S(2)}) %collective-permute-start.17) | collective-permute-done | bytes 524320 | tf_op jit(solution)/shard_map/ppermute | solution.py:52
  89.8 5.2 %collective-permute-done.16.refs_1_ = bf16[2,256,1024]{2,1,0:T(8,128)(2,1)S(1)} collective-permute-done((bf16[2,256,1024]{2,1,0:T(8,128)(2,1)S(1)}, bf16[2,256,1024]{2,1,0:T(8,128)(2,1)S(1)}, u32[]{:S(2)}, u32[]{:S(2)}) %collective-permute-start.16) | collective-permute-done | bytes 1048608 | tf_op jit(solution)/shard_map/ppermute | solution.py:52
  95.9 1.6 collective-permute-start.14
  97.6 1.6 collective-permute-done.19.refs_3_
  99.1 1.1 add_up.19
  100.2 5.2 %collective-permute-start.21 = (bf16[2,64,1024]{2,1,0:T(8,128)(2,1)S(1)}, bf16[2,64,1024]{2,1,0:T(8,128)(2,1)S(1)}, u32[]{:S(2)}, u32[]{:S(2)}) collective-permute-start(bf16[2,64,1024]{2,1,0:T(8,128)(2,1)S(1)} %get-tuple-element.121.refs_0_), channel_id=1, source_target_pairs={{0,48},{1,17},{16,32},{17,1},{32,16},{33,49},{48,0},{49,33},{2,50}... | collective-permute-start | bytes 786440 | tf_op jit(solution)/shard_map/ppermute | solution.py:52
  105.9 2.0 %collective-permute-start.24 = (bf16[2,64,1024]{2,1,0:T(8,128)(2,1)S(1)}, bf16[2,64,1024]{2,1,0:T(8,128)(2,1)S(1)}, u32[]{:S(2)}, u32[]{:S(2)}) collective-permute-start(bf16[2,64,1024]{2,1,0:T(8,128)(2,1)S(1)} %get-tuple-element.128), channel_id=1, source_target_pairs={{0,16},{1,49},{16,0},{17,33},{32,48},{33,17},{48,32},{49,1},{2,18}... | collective-permute-start | bytes 786440 | tf_op jit(solution)/shard_map/ppermute | solution.py:52
  107.9 8.9 %collective-permute-done.21.refs_1_ = bf16[2,64,1024]{2,1,0:T(8,128)(2,1)S(1)} collective-permute-done((bf16[2,64,1024]{2,1,0:T(8,128)(2,1)S(1)}, bf16[2,64,1024]{2,1,0:T(8,128)(2,1)S(1)}, u32[]{:S(2)}, u32[]{:S(2)}) %collective-permute-start.21) | collective-permute-done | bytes 262176 | tf_op jit(solution)/shard_map/ppermute | solution.py:52
  116.9 5.0 %collective-permute-start.29 = (bf16[256,1024]{1,0:T(8,128)(2,1)S(1)}, bf16[256,1024]{1,0:T(8,128)(2,1)S(1)}, u32[]{:S(2)}, u32[]{:S(2)}) collective-permute-start(bf16[256,1024]{1,0:T(8,128)(2,1)S(1)} %get-tuple-element.136.near), channel_id=1, source_target_pairs={{0,64},{1,193},{64,0},{65,129},{128,192},{129,65},{192,128},{193,1... | collective-permute-start | bytes 1572872 | tf_op jit(solution)/shard_map/ppermute | solution.py:52
  122.0 3.2 %collective-permute-start.23 = (bf16[2,64,1024]{2,1,0:T(8,128)(2,1)S(1)}, bf16[2,64,1024]{2,1,0:T(8,128)(2,1)S(1)}, u32[]{:S(2)}, u32[]{:S(2)}) collective-permute-start(bf16[2,64,1024]{2,1,0:T(8,128)(2,1)S(1)} %get-tuple-element.127), channel_id=1, source_target_pairs={{0,16},{1,49},{16,0},{17,33},{32,48},{33,17},{48,32},{49,1},{2,18}... | collective-permute-start | bytes 786440 | tf_op jit(solution)/shard_map/ppermute | solution.py:52
  125.2 3.9 %collective-permute-done.25.a = bf16[64,1024]{1,0:T(8,128)(2,1)S(1)} collective-permute-done((bf16[64,1024]{1,0:T(8,128)(2,1)S(1)}, bf16[64,1024]{1,0:T(8,128)(2,1)S(1)}, u32[]{:S(2)}, u32[]{:S(2)}) %collective-permute-start.25) | collective-permute-done | bytes 131104 | tf_op jit(solution)/shard_map/ppermute | solution.py:52
  129.3 4.5 %collective-permute-start.28 = (bf16[2,64,1024]{2,1,0:T(8,128)(2,1)S(1)}, bf16[2,64,1024]{2,1,0:T(8,128)(2,1)S(1)}, u32[]{:S(2)}, u32[]{:S(2)}) collective-permute-start(bf16[2,64,1024]{2,1,0:T(8,128)(2,1)S(1)} %get-tuple-element.135.refs_0_), channel_id=1, source_target_pairs={{0,48},{1,17},{16,32},{17,1},{32,16},{33,49},{48,0},{49,33},{2,50}... | collective-permute-start | bytes 786440 | tf_op jit(solution)/shard_map/ppermute | solution.py:52
  133.8 6.4 %collective-permute-done.23.refs_3_ = bf16[2,64,1024]{2,1,0:T(8,128)(2,1)S(1)} collective-permute-done((bf16[2,64,1024]{2,1,0:T(8,128)(2,1)S(1)}, bf16[2,64,1024]{2,1,0:T(8,128)(2,1)S(1)}, u32[]{:S(2)}, u32[]{:S(2)}) %collective-permute-start.23) | collective-permute-done | bytes 262176 | tf_op jit(solution)/shard_map/ppermute | solution.py:52
  140.3 4.0 %collective-permute-start.26 = (bf16[2,64,1024]{2,1,0:T(8,128)(2,1)S(1)}, bf16[2,64,1024]{2,1,0:T(8,128)(2,1)S(1)}, u32[]{:S(2)}, u32[]{:S(2)}) collective-permute-start(bf16[2,64,1024]{2,1,0:T(8,128)(2,1)S(1)} %get-tuple-element.133.refs_0_), channel_id=1, source_target_pairs={{0,48},{1,17},{16,32},{17,1},{32,16},{33,49},{48,0},{49,33},{2,50}... | collective-permute-start | bytes 786440 | tf_op jit(solution)/shard_map/ppermute | solution.py:52
  144.3 1.6 place.4
  146.2 5.3 %collective-permute-start.31 = (bf16[64,1024]{1,0:T(8,128)(2,1)S(1)}, bf16[64,1024]{1,0:T(8,128)(2,1)S(1)}, u32[]{:S(2)}, u32[]{:S(2)}) collective-permute-start(bf16[64,1024]{1,0:T(8,128)(2,1)S(1)} %get-tuple-element.142.b), channel_id=1, source_target_pairs={{0,16},{1,49},{16,0},{17,33},{32,48},{33,17},{48,32},{49,1},{2,18}... | collective-permute-start | bytes 393224 | tf_op jit(solution)/shard_map/ppermute | solution.py:52
  151.5 2.4 %collective-permute-done.26.refs_1_ = bf16[2,64,1024]{2,1,0:T(8,128)(2,1)S(1)} collective-permute-done((bf16[2,64,1024]{2,1,0:T(8,128)(2,1)S(1)}, bf16[2,64,1024]{2,1,0:T(8,128)(2,1)S(1)}, u32[]{:S(2)}, u32[]{:S(2)}) %collective-permute-start.26) | collective-permute-done | bytes 262176 | tf_op jit(solution)/shard_map/ppermute | solution.py:52
  154.1 4.4 %collective-permute-start.30 = (bf16[64,1024]{1,0:T(8,128)(2,1)S(1)}, bf16[64,1024]{1,0:T(8,128)(2,1)S(1)}, u32[]{:S(2)}, u32[]{:S(2)}) collective-permute-start(bf16[64,1024]{1,0:T(8,128)(2,1)S(1)} %get-tuple-element.141.b), channel_id=1, source_target_pairs={{0,16},{1,49},{16,0},{17,33},{32,48},{33,17},{48,32},{49,1},{2,18}... | collective-permute-start | bytes 393224 | tf_op jit(solution)/shard_map/ppermute | solution.py:52
  158.7 2.8 %collective-permute-done.30.a = bf16[64,1024]{1,0:T(8,128)(2,1)S(1)} collective-permute-done((bf16[64,1024]{1,0:T(8,128)(2,1)S(1)}, bf16[64,1024]{1,0:T(8,128)(2,1)S(1)}, u32[]{:S(2)}, u32[]{:S(2)}) %collective-permute-start.30) | collective-permute-done | bytes 131104 | tf_op jit(solution)/shard_map/ppermute | solution.py:52
  161.4 1.6 collective-permute-start.32
  163.0 4.8 %collective-permute-done.34.a = bf16[128,1024]{1,0:T(8,128)(2,1)S(1)} collective-permute-done((bf16[128,1024]{1,0:T(8,128)(2,1)S(1)}, bf16[128,1024]{1,0:T(8,128)(2,1)S(1)}, u32[]{:S(2)}, u32[]{:S(2)}) %collective-permute-start.34) | collective-permute-done | bytes 262176 | tf_op jit(solution)/shard_map/ppermute | solution.py:52
  168.0 1.6 place.5
  169.5 3.9 %collective-permute-done.32.a = bf16[128,1024]{1,0:T(8,128)(2,1)S(1)} collective-permute-done((bf16[128,1024]{1,0:T(8,128)(2,1)S(1)}, bf16[128,1024]{1,0:T(8,128)(2,1)S(1)}, u32[]{:S(2)}, u32[]{:S(2)}) %collective-permute-start.32) | collective-permute-done | bytes 262176 | tf_op jit(solution)/shard_map/ppermute | solution.py:52
  173.6 3.5 %collective-permute-done.36.far = bf16[256,1024]{1,0:T(8,128)(2,1)S(1)} collective-permute-done((bf16[256,1024]{1,0:T(8,128)(2,1)S(1)}, bf16[256,1024]{1,0:T(8,128)(2,1)S(1)}, u32[]{:S(2)}, u32[]{:S(2)}) %collective-permute-start.36) | collective-permute-done | bytes 524320 | tf_op jit(solution)/shard_map/ppermute | solution.py:52
  177.1 1.6 place.6
  178.7 4.0 %collective-permute-done.35.far = bf16[256,1024]{1,0:T(8,128)(2,1)S(1)} collective-permute-done((bf16[256,1024]{1,0:T(8,128)(2,1)S(1)}, bf16[256,1024]{1,0:T(8,128)(2,1)S(1)}, u32[]{:S(2)}, u32[]{:S(2)}) %collective-permute-start.35) | collective-permute-done | bytes 524320 | tf_op jit(solution)/shard_map/ppermute | solution.py:52
  182.7 1.6 place.7
  (72 shorter events, 10.3 us)
Async XLA Ops:
  0.0 9.4 %collective-permute-start.1 = (bf16[4,256,256]{2,1,0:T(8,128)(2,1)}, bf16[4,256,256]{2,1,0:T(8,128)(2,1)S(1)}, u32[]{:S(2)}, u32[]{:S(2)}) collective-permute-start(bf16[4,256,256]{2,1,0:T(8,128)(2,1)} %bitcast.7.a), channel_id=1, source_target_pairs={{0,2},{1,7},{2,0},{3,5},{4,6},{5,3},{6,4},{7,1},{8,10},{9,15},{10,... | collective-permute-start | bytes 1572872 | tf_op jit(solution)/shard_map/ppermute | solution.py:52
  11.5 2.9 %collective-permute-start.3 = (bf16[2,4,256,256]{3,2,1,0:T(8,128)(2,1)}, bf16[2,4,256,256]{3,2,1,0:T(8,128)(2,1)S(1)}, u32[]{:S(2)}, u32[]{:S(2)}) collective-permute-start(bf16[2,4,256,256]{3,2,1,0:T(8,128)(2,1)} %get-tuple-element.82.mine), channel_id=1, source_target_pairs={{0,1},{1,0},{2,3},{3,2},{4,5},{5,4},{6,7},{7,6},{8,9},{9,8},{10,11... | collective-permute-start | bytes 3145736 | tf_op jit(solution)/shard_map/ppermute | solution.py:56
  11.5 16.3 %collective-permute-start.2 = (bf16[2,4,256,256]{3,2,1,0:T(8,128)(2,1)}, bf16[2,4,256,256]{3,2,1,0:T(8,128)(2,1)}, u32[]{:S(2)}, u32[]{:S(2)}) collective-permute-start(bf16[2,4,256,256]{3,2,1,0:T(8,128)(2,1)} %get-tuple-element.82.mine), channel_id=1, source_target_pairs={{0,6},{1,3},{2,4},{3,1},{4,2},{5,7},{6,0},{7,5},{8,14},{9,11},{10,... | collective-permute-start | bytes 3145736 | tf_op jit(solution)/shard_map/ppermute | solution.py:52
  12.0 15.9 %collective-permute-start = (bf16[4,256,256]{2,1,0:T(8,128)(2,1)}, bf16[4,256,256]{2,1,0:T(8,128)(2,1)}, u32[]{:S(2)}, u32[]{:S(2)}) collective-permute-start(bf16[4,256,256]{2,1,0:T(8,128)(2,1)} %bitcast.7.a), channel_id=1, source_target_pairs={{0,8},{8,0},{1,9},{9,1},{2,10},{10,2},{3,11},{11,3},{4,12},{12,4},... | collective-permute-start | bytes 1572872 | tf_op jit(solution)/shard_map/ppermute | solution.py:56
  18.2 21.6 %collective-permute-start.7 = (bf16[2,256,1024]{2,1,0:T(8,128)(2,1)S(1)}, bf16[2,256,1024]{2,1,0:T(8,128)(2,1)S(1)}, u32[]{:S(2)}, u32[]{:S(2)}) collective-permute-start(bf16[2,256,1024]{2,1,0:T(8,128)(2,1)S(1)} %get-tuple-element.90), channel_id=1, source_target_pairs={{0,64},{1,193},{64,0},{65,129},{128,192},{129,65},{192,128},{193,1... | collective-permute-start | bytes 3145736 | tf_op jit(solution)/shard_map/ppermute | solution.py:52
  27.8 9.4 %collective-permute-start.4 = (bf16[4,256,256]{2,1,0:T(8,128)(2,1)}, bf16[4,256,256]{2,1,0:T(8,128)(2,1)S(1)}, u32[]{:S(2)}, u32[]{:S(2)}) collective-permute-start(bf16[4,256,256]{2,1,0:T(8,128)(2,1)} %get-tuple-element.86.a), channel_id=1, source_target_pairs={{0,2},{1,7},{2,0},{3,5},{4,6},{5,3},{6,4},{7,1},{8,10},{9,15},{10,... | collective-permute-start | bytes 1572872 | tf_op jit(solution)/shard_map/ppermute | solution.py:52
  27.9 13.4 %collective-permute-start.9 = (bf16[2,4,256,256]{3,2,1,0:T(8,128)(2,1)}, bf16[2,4,256,256]{3,2,1,0:T(8,128)(2,1)}, u32[]{:S(2)}, u32[]{:S(2)}) collective-permute-start(bf16[2,4,256,256]{3,2,1,0:T(8,128)(2,1)} %get-tuple-element.93.mine), channel_id=1, source_target_pairs={{0,1},{1,0},{2,3},{3,2},{4,5},{5,4},{6,7},{7,6},{8,9},{9,8},{10,11... | collective-permute-start | bytes 3145736 | tf_op jit(solution)/shard_map/ppermute | solution.py:56
  39.3 16.3 %collective-permute-start.6 = (bf16[2,4,256,256]{3,2,1,0:T(8,128)(2,1)}, bf16[2,4,256,256]{3,2,1,0:T(8,128)(2,1)}, u32[]{:S(2)}, u32[]{:S(2)}) collective-permute-start(bf16[2,4,256,256]{3,2,1,0:T(8,128)(2,1)} %get-tuple-element.88.mine), channel_id=1, source_target_pairs={{0,6},{1,3},{2,4},{3,1},{4,2},{5,7},{6,0},{7,5},{8,14},{9,11},{10,... | collective-permute-start | bytes 3145736 | tf_op jit(solution)/shard_map/ppermute | solution.py:52
  40.7 9.5 %collective-permute-start.8 = (bf16[2,128,1024]{2,1,0:T(8,128)(2,1)}, bf16[2,128,1024]{2,1,0:T(8,128)(2,1)}, u32[]{:S(2)}, u32[]{:S(2)}) collective-permute-start(bf16[2,128,1024]{2,1,0:T(8,128)(2,1)} %get-tuple-element.92), channel_id=1, source_target_pairs={{0,192},{1,65},{64,128},{65,1},{128,64},{129,193},{192,0},{193,129... | collective-permute-start | bytes 1572872 | tf_op jit(solution)/shard_map/ppermute | solution.py:52
  41.2 17.8 %collective-permute-start.5 = (bf16[2,4,256,256]{3,2,1,0:T(8,128)(2,1)}, bf16[2,4,256,256]{3,2,1,0:T(8,128)(2,1)}, u32[]{:S(2)}, u32[]{:S(2)}) collective-permute-start(bf16[2,4,256,256]{3,2,1,0:T(8,128)(2,1)} %get-tuple-element.88.mine), channel_id=1, source_target_pairs={{0,1},{1,0},{2,3},{3,2},{4,5},{5,4},{6,7},{7,6},{8,9},{9,8},{10,11... | collective-permute-start | bytes 3145736 | tf_op jit(solution)/shard_map/ppermute | solution.py:56
  46.4 1.0 copy-start
  47.4 17.3 %collective-permute-start.13 = (bf16[2,256,1024]{2,1,0:T(8,128)(2,1)}, bf16[2,256,1024]{2,1,0:T(8,128)(2,1)}, u32[]{:S(2)}, u32[]{:S(2)}) collective-permute-start(bf16[2,256,1024]{2,1,0:T(8,128)(2,1)} %get-tuple-element.103), channel_id=1, source_target_pairs={{0,64},{1,193},{64,0},{65,129},{128,192},{129,65},{192,128},{193,1... | collective-permute-start | bytes 3145736 | tf_op jit(solution)/shard_map/ppermute | solution.py:52
  55.6 11.8 %collective-permute-start.11 = (bf16[2,4,256,256]{3,2,1,0:T(8,128)(2,1)}, bf16[2,4,256,256]{3,2,1,0:T(8,128)(2,1)}, u32[]{:S(2)}, u32[]{:S(2)}) collective-permute-start(bf16[2,4,256,256]{3,2,1,0:T(8,128)(2,1)} %get-tuple-element.100.mine), channel_id=1, source_target_pairs={{0,1},{1,0},{2,3},{3,2},{4,5},{5,4},{6,7},{7,6},{8,9},{9,8},{10,11... | collective-permute-start | bytes 3145736 | tf_op jit(solution)/shard_map/ppermute | solution.py:56
  55.6 10.6 %collective-permute-start.12 = (bf16[2,64,1024]{2,1,0:T(8,128)(2,1)}, bf16[2,64,1024]{2,1,0:T(8,128)(2,1)S(1)}, u32[]{:S(2)}, u32[]{:S(2)}) collective-permute-start(bf16[2,64,1024]{2,1,0:T(8,128)(2,1)} %get-tuple-element.101), channel_id=1, source_target_pairs={{0,16},{1,49},{16,0},{17,33},{32,48},{33,17},{48,32},{49,1},{2,18}... | collective-permute-start | bytes 786440 | tf_op jit(solution)/shard_map/ppermute | solution.py:52
  59.0 5.6 %copy-start.1 = (bf16[2,256,1024]{2,1,0:T(8,128)(2,1)S(1)}, bf16[2,256,1024]{2,1,0:T(8,128)(2,1)}, u32[]{:S(2)}) copy-start(bf16[2,256,1024]{2,1,0:T(8,128)(2,1)} %copy-done) | copy-start | bytes 3145732
  63.3 15.6 %collective-permute-start.10 = (bf16[2,256,1024]{2,1,0:T(8,128)(2,1)S(1)}, bf16[2,256,1024]{2,1,0:T(8,128)(2,1)S(1)}, u32[]{:S(2)}, u32[]{:S(2)}) collective-permute-start(bf16[2,256,1024]{2,1,0:T(8,128)(2,1)S(1)} %get-tuple-element.99), channel_id=1, source_target_pairs={{0,64},{1,193},{64,0},{65,129},{128,192},{129,65},{192,128},{193,1... | collective-permute-start | bytes 3145736 | tf_op jit(solution)/shard_map/ppermute | solution.py:52
  71.6 23.5 %collective-permute-start.16 = (bf16[2,256,1024]{2,1,0:T(8,128)(2,1)S(1)}, bf16[2,256,1024]{2,1,0:T(8,128)(2,1)S(1)}, u32[]{:S(2)}, u32[]{:S(2)}) collective-permute-start(bf16[2,256,1024]{2,1,0:T(8,128)(2,1)S(1)} %get-tuple-element.111), channel_id=1, source_target_pairs={{0,64},{1,193},{64,0},{65,129},{128,192},{129,65},{192,128},{193,1... | collective-permute-start | bytes 3145736 | tf_op jit(solution)/shard_map/ppermute | solution.py:52
  72.9 14.9 %collective-permute-start.17 = (bf16[2,128,1024]{2,1,0:T(8,128)(2,1)S(1)}, bf16[2,128,1024]{2,1,0:T(8,128)(2,1)S(1)}, u32[]{:S(2)}, u32[]{:S(2)}) collective-permute-start(bf16[2,128,1024]{2,1,0:T(8,128)(2,1)S(1)} %get-tuple-element.112), channel_id=1, source_target_pairs={{0,192},{1,65},{64,128},{65,1},{128,64},{129,193},{192,0},{193,129... | collective-permute-start | bytes 1572872 | tf_op jit(solution)/shard_map/ppermute | solution.py:52
  72.9 22.8 %collective-permute-start.15 = (bf16[2,64,1024]{2,1,0:T(8,128)(2,1)S(1)}, bf16[2,64,1024]{2,1,0:T(8,128)(2,1)S(1)}, u32[]{:S(2)}, u32[]{:S(2)}) collective-permute-start(bf16[2,64,1024]{2,1,0:T(8,128)(2,1)S(1)} %get-tuple-element.109.refs_0_), channel_id=1, source_target_pairs={{0,48},{1,17},{16,32},{17,1},{32,16},{33,49},{48,0},{49,33},{2,50}... | collective-permute-start | bytes 786440 | tf_op jit(solution)/shard_map/ppermute | solution.py:52
  88.9 10.3 %collective-permute-start.19 = (bf16[2,64,1024]{2,1,0:T(8,128)(2,1)S(1)}, bf16[2,64,1024]{2,1,0:T(8,128)(2,1)S(1)}, u32[]{:S(2)}, u32[]{:S(2)}) collective-permute-start(bf16[2,64,1024]{2,1,0:T(8,128)(2,1)S(1)} %get-tuple-element.117), channel_id=1, source_target_pairs={{0,16},{1,49},{16,0},{17,33},{32,48},{33,17},{48,32},{49,1},{2,18}... | collective-permute-start | bytes 786440 | tf_op jit(solution)/shard_map/ppermute | solution.py:52
  95.2 10.7 %collective-permute-start.22 = (bf16[2,128,1024]{2,1,0:T(8,128)(2,1)S(1)}, bf16[2,128,1024]{2,1,0:T(8,128)(2,1)S(1)}, u32[]{:S(2)}, u32[]{:S(2)}) collective-permute-start(bf16[2,128,1024]{2,1,0:T(8,128)(2,1)S(1)} %get-tuple-element.122), channel_id=1, source_target_pairs={{0,192},{1,65},{64,128},{65,1},{128,64},{129,193},{192,0},{193,129... | collective-permute-start | bytes 1572872 | tf_op jit(solution)/shard_map/ppermute | solution.py:52
  95.8 9.6 %collective-permute-start.18 = (bf16[64,1024]{1,0:T(8,128)(2,1)S(1)}, bf16[64,1024]{1,0:T(8,128)(2,1)S(1)}, u32[]{:S(2)}, u32[]{:S(2)}) collective-permute-start(bf16[64,1024]{1,0:T(8,128)(2,1)S(1)} %get-tuple-element.116.b), channel_id=1, source_target_pairs={{0,16},{1,49},{16,0},{17,33},{32,48},{33,17},{48,32},{49,1},{2,18}... | collective-permute-start | bytes 393224 | tf_op jit(solution)/shard_map/ppermute | solution.py:52
  95.9 26.0 %collective-permute-start.14 = (bf16[2,128,1024]{2,1,0:T(8,128)(2,1)S(1)}, bf16[2,128,1024]{2,1,0:T(8,128)(2,1)S(1)}, u32[]{:S(2)}, u32[]{:S(2)}) collective-permute-start(bf16[2,128,1024]{2,1,0:T(8,128)(2,1)S(1)} %get-tuple-element.108), channel_id=1, source_target_pairs={{0,192},{1,65},{64,128},{65,1},{128,64},{129,193},{192,0},{193,129... | collective-permute-start | bytes 1572872 | tf_op jit(solution)/shard_map/ppermute | solution.py:52
  100.2 16.6 %collective-permute-start.21 = (bf16[2,64,1024]{2,1,0:T(8,128)(2,1)S(1)}, bf16[2,64,1024]{2,1,0:T(8,128)(2,1)S(1)}, u32[]{:S(2)}, u32[]{:S(2)}) collective-permute-start(bf16[2,64,1024]{2,1,0:T(8,128)(2,1)S(1)} %get-tuple-element.121.refs_0_), channel_id=1, source_target_pairs={{0,48},{1,17},{16,32},{17,1},{32,16},{33,49},{48,0},{49,33},{2,50}... | collective-permute-start | bytes 786440 | tf_op jit(solution)/shard_map/ppermute | solution.py:52
  105.4 11.4 %collective-permute-start.20 = (bf16[128,1024]{1,0:T(8,128)(2,1)S(1)}, bf16[128,1024]{1,0:T(8,128)(2,1)S(1)}, u32[]{:S(2)}, u32[]{:S(2)}) collective-permute-start(bf16[128,1024]{1,0:T(8,128)(2,1)S(1)} %get-tuple-element.120.b), channel_id=1, source_target_pairs={{0,192},{1,65},{64,128},{65,1},{128,64},{129,193},{192,0},{193,129... | collective-permute-start | bytes 786440 | tf_op jit(solution)/shard_map/ppermute | solution.py:52
  105.9 23.2 %collective-permute-start.24 = (bf16[2,64,1024]{2,1,0:T(8,128)(2,1)S(1)}, bf16[2,64,1024]{2,1,0:T(8,128)(2,1)S(1)}, u32[]{:S(2)}, u32[]{:S(2)}) collective-permute-start(bf16[2,64,1024]{2,1,0:T(8,128)(2,1)S(1)} %get-tuple-element.128), channel_id=1, source_target_pairs={{0,16},{1,49},{16,0},{17,33},{32,48},{33,17},{48,32},{49,1},{2,18}... | collective-permute-start | bytes 786440 | tf_op jit(solution)/shard_map/ppermute | solution.py:52
  116.9 27.4 %collective-permute-start.29 = (bf16[256,1024]{1,0:T(8,128)(2,1)S(1)}, bf16[256,1024]{1,0:T(8,128)(2,1)S(1)}, u32[]{:S(2)}, u32[]{:S(2)}) collective-permute-start(bf16[256,1024]{1,0:T(8,128)(2,1)S(1)} %get-tuple-element.136.near), channel_id=1, source_target_pairs={{0,64},{1,193},{64,0},{65,129},{128,192},{129,65},{192,128},{193,1... | collective-permute-start | bytes 1572872 | tf_op jit(solution)/shard_map/ppermute | solution.py:52
  121.9 7.3 %collective-permute-start.25 = (bf16[64,1024]{1,0:T(8,128)(2,1)S(1)}, bf16[64,1024]{1,0:T(8,128)(2,1)S(1)}, u32[]{:S(2)}, u32[]{:S(2)}) collective-permute-start(bf16[64,1024]{1,0:T(8,128)(2,1)S(1)} %get-tuple-element.129.b), channel_id=1, source_target_pairs={{0,16},{1,49},{16,0},{17,33},{32,48},{33,17},{48,32},{49,1},{2,18}... | collective-permute-start | bytes 393224 | tf_op jit(solution)/shard_map/ppermute | solution.py:52
  122.0 18.2 %collective-permute-start.23 = (bf16[2,64,1024]{2,1,0:T(8,128)(2,1)S(1)}, bf16[2,64,1024]{2,1,0:T(8,128)(2,1)S(1)}, u32[]{:S(2)}, u32[]{:S(2)}) collective-permute-start(bf16[2,64,1024]{2,1,0:T(8,128)(2,1)S(1)} %get-tuple-element.127), channel_id=1, source_target_pairs={{0,16},{1,49},{16,0},{17,33},{32,48},{33,17},{48,32},{49,1},{2,18}... | collective-permute-start | bytes 786440 | tf_op jit(solution)/shard_map/ppermute | solution.py:52
  129.3 16.6 %collective-permute-start.28 = (bf16[2,64,1024]{2,1,0:T(8,128)(2,1)S(1)}, bf16[2,64,1024]{2,1,0:T(8,128)(2,1)S(1)}, u32[]{:S(2)}, u32[]{:S(2)}) collective-permute-start(bf16[2,64,1024]{2,1,0:T(8,128)(2,1)S(1)} %get-tuple-element.135.refs_0_), channel_id=1, source_target_pairs={{0,48},{1,17},{16,32},{17,1},{32,16},{33,49},{48,0},{49,33},{2,50}... | collective-permute-start | bytes 786440 | tf_op jit(solution)/shard_map/ppermute | solution.py:52
  133.8 12.2 %collective-permute-start.27 = (bf16[128,1024]{1,0:T(8,128)(2,1)S(1)}, bf16[128,1024]{1,0:T(8,128)(2,1)S(1)}, u32[]{:S(2)}, u32[]{:S(2)}) collective-permute-start(bf16[128,1024]{1,0:T(8,128)(2,1)S(1)} %get-tuple-element.134.b), channel_id=1, source_target_pairs={{0,192},{1,65},{64,128},{65,1},{128,64},{129,193},{192,0},{193,129... | collective-permute-start | bytes 786440 | tf_op jit(solution)/shard_map/ppermute | solution.py:52
  140.3 13.7 %collective-permute-start.26 = (bf16[2,64,1024]{2,1,0:T(8,128)(2,1)S(1)}, bf16[2,64,1024]{2,1,0:T(8,128)(2,1)S(1)}, u32[]{:S(2)}, u32[]{:S(2)}) collective-permute-start(bf16[2,64,1024]{2,1,0:T(8,128)(2,1)S(1)} %get-tuple-element.133.refs_0_), channel_id=1, source_target_pairs={{0,48},{1,17},{16,32},{17,1},{32,16},{33,49},{48,0},{49,33},{2,50}... | collective-permute-start | bytes 786440 | tf_op jit(solution)/shard_map/ppermute | solution.py:52
  146.1 21.9 %collective-permute-start.33 = (bf16[256,1024]{1,0:T(8,128)(2,1)S(1)}, bf16[256,1024]{1,0:T(8,128)(2,1)S(1)}, u32[]{:S(2)}, u32[]{:S(2)}) collective-permute-start(bf16[256,1024]{1,0:T(8,128)(2,1)S(1)} %get-tuple-element.146.near), channel_id=1, source_target_pairs={{0,64},{1,193},{64,0},{65,129},{128,192},{129,65},{192,128},{193,1... | collective-permute-start | bytes 1572872 | tf_op jit(solution)/shard_map/ppermute | solution.py:52
  146.2 12.3 %collective-permute-start.31 = (bf16[64,1024]{1,0:T(8,128)(2,1)S(1)}, bf16[64,1024]{1,0:T(8,128)(2,1)S(1)}, u32[]{:S(2)}, u32[]{:S(2)}) collective-permute-start(bf16[64,1024]{1,0:T(8,128)(2,1)S(1)} %get-tuple-element.142.b), channel_id=1, source_target_pairs={{0,16},{1,49},{16,0},{17,33},{32,48},{33,17},{48,32},{49,1},{2,18}... | collective-permute-start | bytes 393224 | tf_op jit(solution)/shard_map/ppermute | solution.py:52
  154.1 7.4 %collective-permute-start.30 = (bf16[64,1024]{1,0:T(8,128)(2,1)S(1)}, bf16[64,1024]{1,0:T(8,128)(2,1)S(1)}, u32[]{:S(2)}, u32[]{:S(2)}) collective-permute-start(bf16[64,1024]{1,0:T(8,128)(2,1)S(1)} %get-tuple-element.141.b), channel_id=1, source_target_pairs={{0,16},{1,49},{16,0},{17,33},{32,48},{33,17},{48,32},{49,1},{2,18}... | collective-permute-start | bytes 393224 | tf_op jit(solution)/shard_map/ppermute | solution.py:52
  158.5 9.3 %collective-permute-start.34 = (bf16[128,1024]{1,0:T(8,128)(2,1)S(1)}, bf16[128,1024]{1,0:T(8,128)(2,1)S(1)}, u32[]{:S(2)}, u32[]{:S(2)}) collective-permute-start(bf16[128,1024]{1,0:T(8,128)(2,1)S(1)} %get-tuple-element.147.b), channel_id=1, source_target_pairs={{0,192},{1,65},{64,128},{65,1},{128,64},{129,193},{192,0},{193,129... | collective-permute-start | bytes 786440 | tf_op jit(solution)/shard_map/ppermute | solution.py:52
  161.4 12.0 %collective-permute-start.32 = (bf16[128,1024]{1,0:T(8,128)(2,1)S(1)}, bf16[128,1024]{1,0:T(8,128)(2,1)S(1)}, u32[]{:S(2)}, u32[]{:S(2)}) collective-permute-start(bf16[128,1024]{1,0:T(8,128)(2,1)S(1)} %get-tuple-element.145.b), channel_id=1, source_target_pairs={{0,192},{1,65},{64,128},{65,1},{128,64},{129,193},{192,0},{193,129... | collective-permute-start | bytes 786440 | tf_op jit(solution)/shard_map/ppermute | solution.py:52
  167.8 9.3 %collective-permute-start.36 = (bf16[256,1024]{1,0:T(8,128)(2,1)S(1)}, bf16[256,1024]{1,0:T(8,128)(2,1)S(1)}, u32[]{:S(2)}, u32[]{:S(2)}) collective-permute-start(bf16[256,1024]{1,0:T(8,128)(2,1)S(1)} %get-tuple-element.153.near), channel_id=1, source_target_pairs={{0,64},{1,193},{64,0},{65,129},{128,192},{129,65},{192,128},{193,1... | collective-permute-start | bytes 1572872 | tf_op jit(solution)/shard_map/ppermute | solution.py:52
  173.5 9.3 %collective-permute-start.35 = (bf16[256,1024]{1,0:T(8,128)(2,1)S(1)}, bf16[256,1024]{1,0:T(8,128)(2,1)S(1)}, u32[]{:S(2)}, u32[]{:S(2)}) collective-permute-start(bf16[256,1024]{1,0:T(8,128)(2,1)S(1)} %get-tuple-element.152.near), channel_id=1, source_target_pairs={{0,64},{1,193},{64,0},{65,129},{128,192},{129,65},{192,128},{193,1... | collective-permute-start | bytes 1572872 | tf_op jit(solution)/shard_map/ppermute | solution.py:52
